TPU v7x, 256 devices: a whole 4x4x8 slice. The times are simulated.
256 devices in a mesh: grp: 4 (over y), dom: 64 (over z, x, core).
Axes of the slice: x: 4, y: 4, z: 8, core: 2. Of those that a mesh axis runs over, the one named last changes fastest.
Arguments:
- u_int: bfloat16 [131072, 192], P(('grp', 'dom')), may hold values from -1.59375 to 1.59375
- u_if: bfloat16 [5632, 192], P('dom'), may hold values from -1.59375 to 1.59375
- load_int: float32 [131072, 192], P(('grp', 'dom')), may hold values from -6 to 6
- load_if: float32 [5632, 192], P('dom'), may hold values from -6 to 6
- conn: int32 [524288, 8], P(('grp', 'dom')), may hold values from 0 to 727
- send_map: int32 [1024, 32], P(('grp', 'dom')), may hold values from 0 to 599
- counts: int32 [256], P(('grp', 'dom')), may hold values from 256 to 2048, as said below
- elem_size: float32 [524288], P(('grp', 'dom')), may hold values from 0.7 to 1.4
- stiffness: float32 [524288], P(('grp', 'dom')), may hold values from 0.5 to 2
- yield_stress: float32 [524288], P(('grp', 'dom')), may hold values from 0.5 to 2
- relax_rate: float32 [524288], P(('grp', 'dom')), may hold values from 0.02 to 0.5
- stress_init: float32 [48, 524288], P(None, ('grp', 'dom')), may hold values from -6 to 6
- kinv_int: bfloat16 [393216, 1536], P(('grp', 'dom')), may hold values from -0.15625 to 0.15625
- sinv: bfloat16 [16896, 16896], P('grp', 'dom'), may hold values from -0.125 to 0.125
Outputs:
- du_int: float32 [131072, 192], P(('grp', 'dom'))
- du_if: float32 [5632, 192], P(('grp', 'dom'))
- stress_end: float32 [48, 524288], P(None, ('grp', 'dom'))
Inputs may be any that keep to these rules, and one draw needn't show every extreme that they name: `counts`: every partition has at least 256 live elements and some partition has exactly 2048.
All inputs are finite; a program needn't handle non-finite values.
Results may differ from a plain program's by a relative error of at most 0.0046.
Values may be sent and summed in bfloat16 or wider, within the bound.
A program may use at most 128 MiB of HBM per device.

v0:
```python
import math

import jax
import jax.numpy as jnp
import numpy as np
from jax import lax
from jax.sharding import PartitionSpec as P

TIMES = 32


POISSON = 0.3
HIGHEST = lax.Precision.HIGHEST


def passed_along(shard, axis, by):
    peers = lax.axis_size(axis)
    return lax.ppermute(shard, axis, [(i, (i + by) % peers) for i in range(peers)])


def copy_for_each(shard, axis):
    copies = jnp.broadcast_to(shard, (lax.axis_size(axis), *shard.shape))
    return lax.all_to_all(copies, axis, split_axis=0, concat_axis=0, tiled=True)


def taken_together(shard, axis):
    return copy_for_each(shard, axis).sum(axis=0)


def cut_along(shard, dim, peers):
    lengths = shard.shape
    pieces = shard.reshape(*lengths[:dim], peers, lengths[dim] // peers, *lengths[dim + 1 :])
    return jnp.moveaxis(pieces, dim, 0)


def summed_on_arrival(shard, axis, dim):
    peers = lax.axis_size(axis)
    pieces = lax.all_to_all(cut_along(shard, dim, peers), axis, 0, 0, tiled=True)
    return jnp.sum(pieces, axis=0)


def strain_table():
    gauss = 1.0 / math.sqrt(3.0)
    table = np.zeros((6, 8, 8, 3))
    for point in range(8):
        coords = [((point >> bit & 1) * 2 - 1) * gauss for bit in range(3)]
        for corner in range(8):
            signs = [(corner >> bit & 1) * 2 - 1 for bit in range(3)]
            deriv = []
            for axis in range(3):
                value = signs[axis] / 8.0
                for other in range(3):
                    if other != axis:
                        value = value * (1.0 + signs[other] * coords[other])
                deriv.append(value)
            table[0, point, corner, 0] = deriv[0]
            table[1, point, corner, 1] = deriv[1]
            table[2, point, corner, 2] = deriv[2]
            table[3, point, corner, 0] = deriv[1]
            table[3, point, corner, 1] = deriv[0]
            table[4, point, corner, 1] = deriv[2]
            table[4, point, corner, 2] = deriv[1]
            table[5, point, corner, 2] = deriv[0]
            table[5, point, corner, 0] = deriv[2]
    return jnp.asarray(table.reshape(48, 24), jnp.float32).astype(jnp.bfloat16)


def time_tables(times, fourier):
    theta = 2.0 * math.pi * (np.arange(times) + 0.3) / times
    synthesis = np.zeros((fourier, times))
    for column in range(fourier):
        harmonic = column // 2
        if column % 2 == 0:
            synthesis[column] = np.cos(harmonic * theta)
        else:
            synthesis[column] = np.sin((harmonic + 1) * theta)
    analysis = synthesis.T * (2.0 / times)
    analysis[:, 0] = 1.0 / times
    return (jnp.asarray(synthesis, jnp.float32), jnp.asarray(analysis, jnp.float32))


def element_update(rows, conn_dev, count, size_e, stiff_e, yield_e, rate_e, stress_zero):
    table = strain_table().reshape(48, 8, 3)
    width = rows.shape[1]
    fourier = width // 3
    buffer_rows = rows.shape[0]
    synthesis, analysis = time_tables(TIMES, fourier)
    elems = conn_dev.shape[0]
    columns = jnp.transpose(rows)
    corner_index = jnp.transpose(conn_dev).reshape(-1)
    gathered = jnp.take(columns, corner_index, axis=1).reshape(3, fourier, 8, elems)
    strain_hat = jnp.einsum("qai,ifae->qfe", table, gathered, preferred_element_type=jnp.float32)
    strain = jnp.einsum("fm,qfe->mqe", synthesis, strain_hat, precision=HIGHEST) * (2.0 / size_e)
    delta = strain - jnp.roll(strain, 1, axis=0)
    delta = delta.reshape(delta.shape[0], 6, 8, elems)
    lame_first = POISSON / ((1.0 + POISSON) * (1.0 - 2.0 * POISSON))
    shear_mod = 1.0 / (2.0 * (1.0 + POISSON))
    coef = jnp.asarray(
        np.array([2.0 * shear_mod] * 3 + [shear_mod] * 3).reshape(6, 1, 1), jnp.float32
    )
    normal_mask = jnp.asarray(
        np.array([1.0, 1.0, 1.0, 0.0, 0.0, 0.0]).reshape(6, 1, 1), jnp.float32
    )
    stress_start = stress_zero.reshape(6, 8, elems)

    def advance(stress, step_delta):
        trace = step_delta[0] + step_delta[1] + step_delta[2]
        increment = coef * step_delta + lame_first * normal_mask * trace[None]
        stress = stress + stiff_e * increment - rate_e * yield_e * jnp.tanh(stress / yield_e)
        return (stress, stress)

    final, history = lax.scan(advance, stress_start, delta, unroll=8)
    live = (jnp.arange(elems) < count).astype(jnp.float32)
    history = history.reshape(history.shape[0], 48, elems)
    stress_hat = jnp.einsum("mf,mqe->fqe", analysis, history, precision=HIGHEST)
    forces = jnp.einsum("qai,fqe->ifae", table.astype(jnp.float32), stress_hat, precision=HIGHEST)
    forces = forces * (size_e * size_e * 0.25 * live)
    forces = forces.reshape(width, 8 * elems)
    assembled = jnp.zeros((width, buffer_rows), jnp.float32).at[:, corner_index].add(forces)
    return (final.reshape(48, elems) * live, jnp.transpose(assembled))


def per_device(
    u_int,
    u_if,
    load_int,
    load_if,
    conn,
    send_map,
    counts,
    elem_size,
    stiffness,
    yield_stress,
    relax_rate,
    stress_init,
    kinv_int,
    sinv,
):
    width = u_int.shape[1]
    fourier = width // 3
    int_nodes = u_int.shape[0]
    neighbours = send_map.shape[0]
    slots = send_map.shape[1]
    reach = neighbours // 2
    offsets = list(range(-reach, 0)) + list(range(1, reach + 1))
    local = jnp.concatenate([u_int, u_if], axis=0)
    local_rows = local.shape[0]
    blocks = jnp.take(local, send_map.reshape(-1), axis=0).reshape(neighbours, slots, width)
    halo = jnp.stack(
        [
            passed_along(blocks[slot_index], "dom", offsets[slot_index])
            for slot_index in range(neighbours)
        ],
        axis=0,
    )
    buffer = jnp.concatenate([local, halo.reshape(neighbours * slots, width)], axis=0)
    stress_end, assembled = element_update(
        buffer, conn, counts[0], elem_size, stiffness, yield_stress, relax_rate, stress_init
    )
    owned = assembled[:local_rows]
    back = assembled[local_rows:].reshape(neighbours, slots, width)
    returned = jnp.stack(
        [
            passed_along(back[slot_index], "dom", -offsets[slot_index])
            for slot_index in range(neighbours)
        ],
        axis=0,
    )
    owned = owned + jax.ops.segment_sum(
        returned.reshape(neighbours * slots, width), send_map.reshape(-1), num_segments=local_rows
    )
    r_int = load_int - owned[:int_nodes]
    group_force = taken_together(owned[int_nodes:], "grp")
    r_if = load_if - group_force
    rhs_int = r_int.astype(jnp.bfloat16).reshape(3 * int_nodes, fourier)
    rhs_if = r_if.astype(jnp.bfloat16).reshape(3 * r_if.shape[0], fourier)
    dom_count = lax.axis_size("dom")
    out_rows = sinv.shape[0] // 3 // dom_count
    du_if = summed_on_arrival(
        jnp.dot(sinv, rhs_if, preferred_element_type=jnp.float32).reshape(
            out_rows * lax.axis_size("dom"), width
        ),
        "dom",
        0,
    )
    du_int = jnp.dot(kinv_int, rhs_int, preferred_element_type=jnp.float32).reshape(
        int_nodes, width
    )
    return (du_int, du_if, stress_end)


def solution(mesh):
    return jax.shard_map(
        per_device,
        mesh=mesh,
        in_specs=(
            P(("grp", "dom"), None),
            P("dom", None),
            P(("grp", "dom"), None),
            P("dom", None),
            P(("grp", "dom"), None),
            P(("grp", "dom"), None),
            P(("grp", "dom")),
            P(("grp", "dom")),
            P(("grp", "dom")),
            P(("grp", "dom")),
            P(("grp", "dom")),
            P(None, ("grp", "dom")),
            P(("grp", "dom"), None),
            P("grp", "dom"),
        ),
        out_specs=(P(("grp", "dom"), None), P(("grp", "dom"), None), P(None, ("grp", "dom"))),
        check_vma=False,
    )
```

profile of v0, /device:TPU:4, one launch (start us, length us, event | category | flops | bytes accessed | tf_op | source)
XLA Modules:
  0.0 578.2 jit_solution(10705444367839839668)
XLA Ops:
  17.9 65.2 %gather_fusion.1 = bf16[16384,192]{1,0:T(8,128)(2,1)} fusion(bf16[192,728]{0,1:T(8,128)(2,1)S(1)} %maximum_bitcast_fusion, s32[16384]{0:T(1024)S(1)} %broadcast_clamp_fusion), kind=kCustom, calls=%fused_computation.1 | custom fusion | bytes 12648448 | tf_op jit(solution)/shard_map/jit(_take)/gather | solution.py:91
  83.1 10.2 %copy.38 = bf16[192,16384]{1,0:T(8,128)(2,1)} copy(bf16[192,16384]{0,1:T(8,128)(2,1)} %bitcast.273) | data formatting | bytes 12582912 | tf_op jit(solution)/shard_map/jit(_take)/gather | solution.py:91
  93.3 7.8 %copy.88 = bf16[24,8,8,2048]{3,2,1,0:T(8,128)(2,1)S(1)} copy(bf16[24,8,8,2048]{3,1,2,0:T(8,128)(2,1)} %bitcast.274) | data formatting | bytes 12582912
  101.1 10.2 %convolution_bitcast_fusion = f32[48,64,2048]{2,0,1:T(8,128)} fusion(pred[8,2048]{1,0:T(8,128)(4,1)S(1)} %compare_and_fusion, bf16[48,8,3,1]{0,1,2,3:T(8,128)(2,1)S(1)} %copy-done.16, bf16[3,64,8,2048]{3,2,1,0:T(8,128)(2,1)S(1)} %bitcast.266), kind=kOutput, calls=%fused_computation.127 | convolution fusion | flops 305135616 | bytes 31475968 | tf_op jit(solution)/shard_map/qai,ifae->qfe/dot_general | solution.py:92
  111.4 38.0 %multiply_bitcast_fusion.1 = f32[32,48,2048]{2,0,1:T(8,128)S(1)} fusion(f32[2048]{0:T(1024)S(1)} %get-tuple-element.235, f32[64,32,1]{0,1,2:T(8,128)S(1)} %copy-done.19, f32[48,64,2048]{2,0,1:T(8,128)} %convolution_bitcast_fusion), kind=kOutput, calls=%fused_computation.125 | convolution fusion | flops 2419064832 | bytes 37765120 | tf_op jit(solution)/shard_map/fm,qfe->mqe/dot_general | solution.py:93
  149.8 6.0 %maximum_subtract_fusion = f32[32,48,2048]{2,0,1:T(8,128)} fusion(f32[32,48,2048]{2,0,1:T(8,128)S(1)} %multiply_bitcast_fusion.1, f32[31,48,2048]{2,0,1:T(8,128)S(1)} %bitcast.267, f32[1,48,2048]{2,0,1:T(1,128)S(1)} %slice.355), kind=kLoop, calls=%fused_computation.121 | loop fusion | flops 6291456 | bytes 37748736 | tf_op jit(solution)/shard_map/sub | solution.py:94
  155.8 133.6 %while.15 = (s32[]{:T(128)}, f32[6,8,2048]{2,1,0:T(8,128)}, f32[4,8,6,8,2048]{4,3,2,1,0:T(8,128)}, f32[2048]{0:T(1024)S(1)}, f32[4,8,6,8,2048]{4,1,0,3,2:T(8,128...) while((s32[]{:T(128)}, f32[6,8,2048]{2,1,0:T(8,128)}, ...), condition=%wide.region_1.2_spmd.clone, body=%wide.region_0.1_spmd.sunk.clone.sunk | while | flops 9699336 | bytes 36118600 | solution.py:112
  156.1 8.5 %constant_dynamic-slice_fusion.34 = (f32[1,1,1,8,2048]{4,1,0,3,2:T(1,128)}, f32[1,1,1,8,2048]{4,1,0,3,2:T(1,128)}, f32[1,1,1,8,2048]{4,1,0,3,2:T(1,128)}, f32[1,...) fusion(f32[4,8,6,8,2048]{4,1,0,3,2:T(8,128)} %get-tuple-element, ...), kind=kLoop, calls=%fused_computation.104.clone.1 | loop fusion | bytes 3145760 | tf_op jit(solution)/shard_map/while/body/eval_jaxpr/slice | solution.py:107
  165.3 13.0 %constant_dynamic-slice_fusion.35 = (f32[1,1,6,8,2048]{4,1,0,3,2:T(1,128)}, f32[1,1,6,8,2048]{4,1,0,3,2:T(1,128)S(1)}, f32[1,1,6,8,2048]{4,1,0,3,2:T(1,128)}, f3...) fusion(f32[4,8,6,8,2048]{4,1,0,3,2:T(8,128)} %get-tuple-element, ...), kind=kLoop, calls=%fused_computation.100.clone.1 | loop fusion | bytes 6291488 | tf_op jit(solution)/shard_map/while/body/slice | solution.py:112
  189.7 7.8 %constant_dynamic-slice_fusion.34 = (f32[1,1,1,8,2048]{4,1,0,3,2:T(1,128)}, f32[1,1,1,8,2048]{4,1,0,3,2:T(1,128)}, f32[1,1,1,8,2048]{4,1,0,3,2:T(1,128)}, f32[1,...) fusion(f32[4,8,6,8,2048]{4,1,0,3,2:T(8,128)} %get-tuple-element, ...), kind=kLoop, calls=%fused_computation.104.clone.1 | loop fusion | bytes 3145760 | tf_op jit(solution)/shard_map/while/body/eval_jaxpr/slice | solution.py:107
  198.3 12.7 %constant_dynamic-slice_fusion.35 = (f32[1,1,6,8,2048]{4,1,0,3,2:T(1,128)}, f32[1,1,6,8,2048]{4,1,0,3,2:T(1,128)S(1)}, f32[1,1,6,8,2048]{4,1,0,3,2:T(1,128)}, f3...) fusion(f32[4,8,6,8,2048]{4,1,0,3,2:T(8,128)} %get-tuple-element, ...), kind=kLoop, calls=%fused_computation.100.clone.1 | loop fusion | bytes 6291488 | tf_op jit(solution)/shard_map/while/body/slice | solution.py:112
  222.5 8.6 %constant_dynamic-slice_fusion.34 = (f32[1,1,1,8,2048]{4,1,0,3,2:T(1,128)}, f32[1,1,1,8,2048]{4,1,0,3,2:T(1,128)}, f32[1,1,1,8,2048]{4,1,0,3,2:T(1,128)}, f32[1,...) fusion(f32[4,8,6,8,2048]{4,1,0,3,2:T(8,128)} %get-tuple-element, ...), kind=kLoop, calls=%fused_computation.104.clone.1 | loop fusion | bytes 3145760 | tf_op jit(solution)/shard_map/while/body/eval_jaxpr/slice | solution.py:107
  231.8 12.7 %constant_dynamic-slice_fusion.35 = (f32[1,1,6,8,2048]{4,1,0,3,2:T(1,128)}, f32[1,1,6,8,2048]{4,1,0,3,2:T(1,128)S(1)}, f32[1,1,6,8,2048]{4,1,0,3,2:T(1,128)}, f3...) fusion(f32[4,8,6,8,2048]{4,1,0,3,2:T(8,128)} %get-tuple-element, ...), kind=kLoop, calls=%fused_computation.100.clone.1 | loop fusion | bytes 6291488 | tf_op jit(solution)/shard_map/while/body/slice | solution.py:112
  256.0 8.5 %constant_dynamic-slice_fusion.34 = (f32[1,1,1,8,2048]{4,1,0,3,2:T(1,128)}, f32[1,1,1,8,2048]{4,1,0,3,2:T(1,128)}, f32[1,1,1,8,2048]{4,1,0,3,2:T(1,128)}, f32[1,...) fusion(f32[4,8,6,8,2048]{4,1,0,3,2:T(8,128)} %get-tuple-element, ...), kind=kLoop, calls=%fused_computation.104.clone.1 | loop fusion | bytes 3145760 | tf_op jit(solution)/shard_map/while/body/eval_jaxpr/slice | solution.py:107
  265.2 12.7 %constant_dynamic-slice_fusion.35 = (f32[1,1,6,8,2048]{4,1,0,3,2:T(1,128)}, f32[1,1,6,8,2048]{4,1,0,3,2:T(1,128)S(1)}, f32[1,1,6,8,2048]{4,1,0,3,2:T(1,128)}, f3...) fusion(f32[4,8,6,8,2048]{4,1,0,3,2:T(8,128)} %get-tuple-element, ...), kind=kLoop, calls=%fused_computation.100.clone.1 | loop fusion | bytes 6291488 | tf_op jit(solution)/shard_map/while/body/slice | solution.py:112
  289.5 34.3 %fusion.54 = f32[64,48,2048,1]{2,0,1,3:T(8,128)} fusion(f32[32,64,1]{1,0,2:T(8,128)S(1)} %copy-done.18, f32[32,48,2048]{2,1,0:T(8,128)} %bitcast.272), kind=kOutput, calls=%fused_computation.126 | convolution fusion | flops 2415919104 | bytes 37756928 | tf_op jit(solution)/shard_map/mf,mqe->fqe/dot_general | solution.py:115
  323.8 31.5 %multiply_bitcast_fusion = f32[3,64,8,2048]{3,2,0,1:T(8,128)} fusion(f32[2048]{0:T(1024)S(1)} %get-tuple-element.236, bf16[48,8,3,1]{0,1,2,3:T(8,128)(2,1)S(1)} %copy-done.16, f32[64,48,2048,1]{2,0,1,3:T(8,128)} %fusion.54), kind=kOutput, calls=%fused_computation.124 | convolution fusion | flops 1815085056 | bytes 37759232 | tf_op jit(solution)/shard_map/qai,fqe->ifae/dot_general | solution.py:116
  355.3 11.3 %copy.44 = f32[3,64,8,2048]{3,2,1,0:T(8,128)} copy(f32[3,64,8,2048]{3,2,0,1:T(8,128)} %multiply_bitcast_fusion) | data formatting | bytes 25165824 | tf_op jit(solution)/shard_map/mul | solution.py:117
  366.6 21.3 %copy.89 = f32[24,8,8,2048]{3,1,2,0:T(8,128)} copy(f32[24,8,8,2048]{3,2,1,0:T(8,128)} %bitcast.271) | data formatting | bytes 25165824
  387.9 14.7 %copy.45 = f32[16384,192]{1,0:T(8,128)} copy(f32[16384,192]{0,1:T(8,128)} %bitcast.270) | data formatting | bytes 25165824 | tf_op jit(solution)/shard_map/reshape | solution.py:118
  402.6 88.3 %scatter_custom_fusion = f32[192,728]{0,1:T(8,128)S(1)} fusion(s32[16384]{0:T(1024)} %bitcast.290, f32[16384,192]{1,0:T(8,128)} %copy.45, f32[]{:T(128)} %constant.64.clone.1), kind=kCustom, calls=%fused_computation.138 | custom fusion | flops 3145728 | bytes 559616 | tf_op jit(solution)/shard_map/scatter-add | solution.py:119
  500.4 11.7 %all_to_all.10 = f32[4,88,192]{2,1,0:T(8,128)} all-to-all(f32[4,88,192]{2,1,0:T(8,128)S(1)} %broadcast_in_dim.118), channel_id=1, replica_groups=mesh['grp'=4,'dom'=64] {'grp'}, dimensions={0} | all-to-all | bytes 540672 | tf_op jit(solution)/shard_map/all_to_all | solution.py:23
  520.8 14.8 %all-to-all-start.1 = ((f32[64,22,192]{2,1,0:T(8,128)}), f32[64,22,192]{2,1,0:T(8,128)}, u32[]{:S(2)}, u32[]{:S(2)}) async-start(f32[64,22,192]{2,1,0:T(8,128)} %reshape_reshape.11), calls=%async_computation.1 | async-start | bytes 3145728 | tf_op jit(solution)/shard_map/all_to_all | solution.py:38
  545.2 30.4 %all-to-all-done.1 = f32[64,22,192]{2,1,0:T(8,128)} async-done(((f32[64,22,192]{2,1,0:T(8,128)}), f32[64,22,192]{2,1,0:T(8,128)}, u32[]{:S(2)}, u32[]{:S(2)}) %all-to-all-start.1) | async-done | bytes 1081376 | tf_op jit(solution)/shard_map/all_to_all | solution.py:38
  (203 shorter events, 95.0 us)
Async XLA Ops:
  0.6 512.6 %copy-start = (bf16[4224,264]{0,1:T(8,128)(2,1)S(1)}, bf16[4224,264]{0,1:T(8,128)(2,1)}, u32[]{:S(2)}) copy-start(bf16[4224,264]{0,1:T(8,128)(2,1)} %param.34) | copy-start | bytes 6690820
  7.0 7.2 %collective-permute-start = (bf16[32,192]{1,0:T(8,128)(2,1)S(1)}, bf16[32,192]{1,0:T(8,128)(2,1)S(1)}, u32[]{:S(2)}, u32[]{:S(2)}) collective-permute-start(bf16[32,192]{1,0:T(8,128)(2,1)S(1)} %get-tuple-element.231), channel_id=1, source_target_pairs={{0,62},{1,63},{2,0},{3,1},{4,2},{5,3},{6,4},{7,5},{8,6},{9,7},{10,... | collective-permute-start | bytes 36872 | tf_op jit(solution)/shard_map/ppermute | solution.py:18
  7.6 6.6 %collective-permute-start.1 = (bf16[32,192]{1,0:T(8,128)(2,1)S(1)}, bf16[32,192]{1,0:T(8,128)(2,1)S(1)}, u32[]{:S(2)}, u32[]{:S(2)}) collective-permute-start(bf16[32,192]{1,0:T(8,128)(2,1)S(1)} %get-tuple-element.234), channel_id=1, source_target_pairs={{0,63},{1,0},{2,1},{3,2},{4,3},{5,4},{6,5},{7,6},{8,7},{9,8},{10,9... | collective-permute-start | bytes 36872 | tf_op jit(solution)/shard_map/ppermute | solution.py:18
  7.6 6.6 %collective-permute-start.2 = (bf16[32,192]{1,0:T(8,128)(2,1)S(1)}, bf16[32,192]{1,0:T(8,128)(2,1)S(1)}, u32[]{:S(2)}, u32[]{:S(2)}) collective-permute-start(bf16[32,192]{1,0:T(8,128)(2,1)S(1)} %get-tuple-element.233), channel_id=1, source_target_pairs={{0,1},{1,2},{2,3},{3,4},{4,5},{5,6},{6,7},{7,8},{8,9},{9,10},{10,1... | collective-permute-start | bytes 36872 | tf_op jit(solution)/shard_map/ppermute | solution.py:18
  8.1 9.0 %collective-permute-start.3 = (bf16[32,192]{1,0:T(8,128)(2,1)S(1)}, bf16[32,192]{1,0:T(8,128)(2,1)S(1)}, u32[]{:S(2)}, u32[]{:S(2)}) collective-permute-start(bf16[32,192]{1,0:T(8,128)(2,1)S(1)} %get-tuple-element.232), channel_id=1, source_target_pairs={{0,2},{1,3},{2,4},{3,5},{4,6},{5,7},{6,8},{7,9},{8,10},{9,11},{10,... | collective-permute-start | bytes 36872 | tf_op jit(solution)/shard_map/ppermute | solution.py:18
  101.1 10.2 %copy-start.19 = (f32[64,32,1]{0,1,2:T(8,128)S(1)}, f32[64,32,1]{0,1,2:T(8,128)}, u32[]{:S(2)}) copy-start(f32[64,32,1]{0,1,2:T(8,128)} %constant.90) | copy-start | bytes 24580
  155.8 133.7 %copy-start.18 = (f32[32,64,1]{1,0,2:T(8,128)S(1)}, f32[32,64,1]{1,0,2:T(8,128)}, u32[]{:S(2)}) copy-start(f32[32,64,1]{1,0,2:T(8,128)} %constant.88) | copy-start | bytes 24580
  178.3 8.0 %copy-start.7 = (f32[1,1,1,8,2048]{4,1,0,3,2:T(1,128)S(1)}, f32[1,1,1,8,2048]{4,1,0,3,2:T(1,128)}, u32[]{:S(2)}) copy-start(f32[1,1,1,8,2048]{4,1,0,3,2:T(1,128)} %get-tuple-element.365) | copy-start | bytes 196612 | tf_op jit(solution)/shard_map/while
  178.3 8.0 %copy-start.8 = (f32[1,1,1,8,2048]{4,1,0,3,2:T(1,128)S(1)}, f32[1,1,1,8,2048]{4,1,0,3,2:T(1,128)}, u32[]{:S(2)}) copy-start(f32[1,1,1,8,2048]{4,1,0,3,2:T(1,128)} %get-tuple-element.367) | copy-start | bytes 196612 | tf_op jit(solution)/shard_map/while
  178.3 8.0 %copy-start.9 = (f32[1,1,1,8,2048]{4,1,0,3,2:T(1,128)S(1)}, f32[1,1,1,8,2048]{4,1,0,3,2:T(1,128)}, u32[]{:S(2)}) copy-start(f32[1,1,1,8,2048]{4,1,0,3,2:T(1,128)} %get-tuple-element.368) | copy-start | bytes 196612 | tf_op jit(solution)/shard_map/while
  178.3 8.0 %copy-start.10 = (f32[1,1,1,8,2048]{4,1,0,3,2:T(1,128)S(1)}, f32[1,1,1,8,2048]{4,1,0,3,2:T(1,128)}, u32[]{:S(2)}) copy-start(f32[1,1,1,8,2048]{4,1,0,3,2:T(1,128)} %get-tuple-element.369) | copy-start | bytes 196612 | tf_op jit(solution)/shard_map/while
  178.3 8.0 %copy-start.11 = (f32[1,1,1,8,2048]{4,1,0,3,2:T(1,128)S(1)}, f32[1,1,1,8,2048]{4,1,0,3,2:T(1,128)}, u32[]{:S(2)}) copy-start(f32[1,1,1,8,2048]{4,1,0,3,2:T(1,128)} %get-tuple-element.364) | copy-start | bytes 196612 | tf_op jit(solution)/shard_map/while
  178.3 8.3 %copy-start.2 = (f32[1,1,6,8,2048]{4,1,0,3,2:T(1,128)S(1)}, f32[1,1,6,8,2048]{4,1,0,3,2:T(1,128)}, u32[]{:S(2)}) copy-start(f32[1,1,6,8,2048]{4,1,0,3,2:T(1,128)} %get-tuple-element.373) | copy-start | bytes 1179652 | tf_op jit(solution)/shard_map/while
  211.0 8.3 %copy-start.2 = (f32[1,1,6,8,2048]{4,1,0,3,2:T(1,128)S(1)}, f32[1,1,6,8,2048]{4,1,0,3,2:T(1,128)}, u32[]{:S(2)}) copy-start(f32[1,1,6,8,2048]{4,1,0,3,2:T(1,128)} %get-tuple-element.373) | copy-start | bytes 1179652 | tf_op jit(solution)/shard_map/while
  244.6 8.3 %copy-start.2 = (f32[1,1,6,8,2048]{4,1,0,3,2:T(1,128)S(1)}, f32[1,1,6,8,2048]{4,1,0,3,2:T(1,128)}, u32[]{:S(2)}) copy-start(f32[1,1,6,8,2048]{4,1,0,3,2:T(1,128)} %get-tuple-element.373) | copy-start | bytes 1179652 | tf_op jit(solution)/shard_map/while
  278.0 8.3 %copy-start.2 = (f32[1,1,6,8,2048]{4,1,0,3,2:T(1,128)S(1)}, f32[1,1,6,8,2048]{4,1,0,3,2:T(1,128)}, u32[]{:S(2)}) copy-start(f32[1,1,6,8,2048]{4,1,0,3,2:T(1,128)} %get-tuple-element.373) | copy-start | bytes 1179652 | tf_op jit(solution)/shard_map/while
  387.9 110.9 %copy-start.21 = (s32[128]{0:T(128)S(1)}, s32[128]{0:T(128)}, u32[]{:S(2)}) copy-start(s32[128]{0:T(128)} %copy-done.20) | copy-start | bytes 1540
  387.9 125.2 %copy-start.17 = (f32[88,192]{1,0:T(8,128)S(1)}, f32[88,192]{1,0:T(8,128)}, u32[]{:S(2)}) copy-start(f32[88,192]{1,0:T(8,128)} %param.24) | copy-start | bytes 202756
  491.0 7.3 %collective-permute-start.4 = (f32[32,192]{1,0:T(8,128)S(1)}, f32[32,192]{1,0:T(8,128)S(1)}, u32[]{:S(2)}, u32[]{:S(2)}) collective-permute-start(f32[32,192]{1,0:T(8,128)S(1)} %get-tuple-element.227), channel_id=1, source_target_pairs={{0,2},{1,3},{2,4},{3,5},{4,6},{5,7},{6,8},{7,9},{8,10},{9,11},{10,... | collective-permute-start | bytes 73736 | tf_op jit(solution)/shard_map/ppermute | solution.py:18
  491.5 6.8 %collective-permute-start.5 = (f32[32,192]{1,0:T(8,128)S(1)}, f32[32,192]{1,0:T(8,128)S(1)}, u32[]{:S(2)}, u32[]{:S(2)}) collective-permute-start(f32[32,192]{1,0:T(8,128)S(1)} %get-tuple-element.230), channel_id=1, source_target_pairs={{0,1},{1,2},{2,3},{3,4},{4,5},{5,6},{6,7},{7,8},{8,9},{9,10},{10,1... | collective-permute-start | bytes 73736 | tf_op jit(solution)/shard_map/ppermute | solution.py:18
  491.7 6.6 %collective-permute-start.6 = (f32[32,192]{1,0:T(8,128)S(1)}, f32[32,192]{1,0:T(8,128)S(1)}, u32[]{:S(2)}, u32[]{:S(2)}) collective-permute-start(f32[32,192]{1,0:T(8,128)S(1)} %get-tuple-element.229), channel_id=1, source_target_pairs={{0,63},{1,0},{2,1},{3,2},{4,3},{5,4},{6,5},{7,6},{8,7},{9,8},{10,9... | collective-permute-start | bytes 73736 | tf_op jit(solution)/shard_map/ppermute | solution.py:18
  493.3 5.5 collective-permute-start.7
  500.3 37.3 %copy-start.1 = (f32[6,8,2048]{2,1,0:T(8,128)S(1)}, f32[6,8,2048]{2,1,0:T(8,128)}, u32[]{:S(2)}) copy-start(f32[6,8,2048]{2,1,0:T(8,128)} %get-tuple-element.111) | copy-start | bytes 1179652
  520.8 54.8 %all-to-all-start.1 = ((f32[64,22,192]{2,1,0:T(8,128)}), f32[64,22,192]{2,1,0:T(8,128)}, u32[]{:S(2)}, u32[]{:S(2)}) async-start(f32[64,22,192]{2,1,0:T(8,128)} %reshape_reshape.11), calls=%async_computation.1 | async-start | bytes 3145728 | tf_op jit(solution)/shard_map/all_to_all | solution.py:38
  (31 other events, 217.4 us)
where the time goes:
time: 588 us; the launch traced here: 578 us
  local copies, waits for them, and re-layouts  241 us (41%)
  other arithmetic  146 us (25%)
  matrix products  120 us (20%)
  waiting for transfers between devices  33.8 us (6%)
  starting transfers between devices  23.6 us (4%)
  blocking collectives  11.7 us (2%)
    scatter-add x1, other arithmetic, element_update(): jnp.zeros((width, buffer_rows), jnp.float32).at[:, corner_index].add(forces)  88.3 us
    gather x2, local copies, waits for them, and re-layouts, element_update(): jnp.take(columns, corner_index, axis=1).reshape(3, fourier, 8, elems)  75.4 us
    slice x4, local copies, waits for them, and re-layouts, element_update(): final, history = lax.scan(advance, stress_start, delta, unroll=8)  51 us
    dot_general x1, matrix products, element_update(): jnp.einsum('fm,qfe->mqe', synthesis, strain_hat, precision=HIGHEST)  38 us
    unnamed x35, local copies, waits for them, and re-layouts  36.6 us
    dot_general x1, matrix products, element_update(): stress_hat = jnp.einsum('mf,mqe->fqe', analysis, history, precision=HIGHEST)  34.3 us
    slice x4, local copies, waits for them, and re-layouts, advance(): trace = step_delta[0] + step_delta[1] + step_delta[2]  33.5 us
    dot_general x1, matrix products, element_update(): jnp.einsum('qai,fqe->ifae', table.astype(jnp.float32), stress_hat, precis...  31.5 us
  transfers between devices with their start and end apart: 9, of which 3 were waited for; matrix products, arithmetic and copies ran while one was open for 2% of the time, Pallas kernels for 0%

commit v1 on v0

v1 whole, which is shorter than its diff:
```python
import functools
import math

import jax
import jax.numpy as jnp
import numpy as np
from jax import lax
from jax.experimental import pallas as pl
from jax.experimental.pallas import tpu as pltpu
from jax.sharding import PartitionSpec as P

TIMES = 32
GROUP = 8
POISSON = 0.3
BF16 = jnp.bfloat16
F32 = jnp.float32


def strain_table():
    gauss = 1.0 / math.sqrt(3.0)
    table = np.zeros((6, 8, 8, 3))
    for point in range(8):
        coords = [((point >> bit & 1) * 2 - 1) * gauss for bit in range(3)]
        for corner in range(8):
            signs = [(corner >> bit & 1) * 2 - 1 for bit in range(3)]
            deriv = []
            for axis in range(3):
                value = signs[axis] / 8.0
                for other in range(3):
                    if other != axis:
                        value = value * (1.0 + signs[other] * coords[other])
                deriv.append(value)
            table[0, point, corner, 0] = deriv[0]
            table[1, point, corner, 1] = deriv[1]
            table[2, point, corner, 2] = deriv[2]
            table[3, point, corner, 0] = deriv[1]
            table[3, point, corner, 1] = deriv[0]
            table[4, point, corner, 1] = deriv[2]
            table[4, point, corner, 2] = deriv[1]
            table[5, point, corner, 2] = deriv[0]
            table[5, point, corner, 0] = deriv[2]
    return np.asarray(np.asarray(table.reshape(48, 24), np.float32), BF16).astype(np.float64)


def time_tables(times, fourier):
    theta = 2.0 * math.pi * (np.arange(times) + 0.3) / times
    synthesis = np.zeros((fourier, times))
    for column in range(fourier):
        harmonic = column // 2
        if column % 2 == 0:
            synthesis[column] = np.cos(harmonic * theta)
        else:
            synthesis[column] = np.sin((harmonic + 1) * theta)
    analysis = synthesis.T * (2.0 / times)
    analysis[:, 0] = 1.0 / times
    return synthesis.astype(np.float32).astype(np.float64), analysis.astype(np.float32).astype(np.float64)


def two_parts(x):
    high = np.asarray(x, np.float32).astype(BF16)
    low = (np.asarray(x, np.float64) - high.astype(np.float64)).astype(BF16)
    return jnp.asarray(high), jnp.asarray(low)


@functools.lru_cache(None)
def host_tables(fourier):
    table = strain_table()
    synthesis, analysis = time_tables(TIMES, fourier)
    groups = TIMES // GROUP
    steps = synthesis - np.roll(synthesis, 1, axis=1)
    synth = np.zeros((groups, 3, GROUP, 3, fourier))
    analyse = np.zeros((groups, 3, 2, GROUP, 3, fourier))
    for g in range(groups):
        for i in range(3):
            for m in range(GROUP):
                synth[g, i, m, i] = steps[:, g * GROUP + m]
                analyse[g, i, :, m, i] = analysis[g * GROUP + m]
    strain = np.zeros((GROUP, 48, 8, 3, 2, GROUP))
    force = np.zeros((8, 3, GROUP, GROUP, 48))
    shaped = table.reshape(48, 8, 3)
    for m in range(GROUP):
        for part in range(2):
            strain[m, :, :, :, part, m] = shaped
        force[:, :, m, m, :] = np.transpose(shaped, (1, 2, 0))
    width = 3 * fourier
    return (
        synth.reshape(TIMES * 3, width),
        analyse.reshape(TIMES * 6, width),
        strain.reshape(GROUP * 48, GROUP * 48),
        force.reshape(GROUP * 24, GROUP * 48),
    )


def split_rows(x):
    rows, n = x.shape
    high = x.astype(BF16).astype(F32)
    low = x - high
    parts = jnp.concatenate(
        [high.reshape(rows // 8, 1, 8, n), low.reshape(rows // 8, 1, 8, n)], axis=1
    )
    return parts.reshape(rows * 2, n).astype(BF16)


def dot(a, b):
    return lax.dot_general(a, b, (((1,), (0,)), ((), ())), preferred_element_type=F32)


def dot_t(a, b):
    return lax.dot_general(a, b, (((1,), (1,)), ((), ())), preferred_element_type=F32)


LAME = POISSON / ((1.0 + POISSON) * (1.0 - 2.0 * POISSON))
SHEAR = 1.0 / (2.0 * (1.0 + POISSON))


def element_kernel(
    counts_ref, rows_ref, conn_ref, params_ref, stress_ref,
    synth_hi_ref, synth_lo_ref, an_hi_ref, an_lo_ref, strain_ref, force_ref,
    stress_out, force_out,
    nodal, onehot, gathered, stresses, forces, total,
):
    step = pl.program_id(0)
    block = conn_ref.shape[1]
    nodes = nodal.shape[1]
    groups = TIMES // GROUP

    @pl.when(step == 0)
    def _():
        rows = rows_ref[...]
        values = dot_t(synth_hi_ref[...], rows) + dot_t(synth_lo_ref[...], rows)
        nodal[...] = split_rows(values)
        total[...] = jnp.zeros_like(total)

    iota = lax.broadcasted_iota(jnp.int16, (nodes, block), 0)
    for a in range(8):
        index = conn_ref[a : a + 1, :].astype(jnp.int16)
        hit = iota == jnp.broadcast_to(index, (nodes, block))
        onehot[:, a * block : (a + 1) * block] = jnp.where(
            hit, jnp.ones((), BF16), jnp.zeros((), BF16)
        )
    table = nodal[...]
    for a in range(8):
        picked = dot(table, onehot[:, a * block : (a + 1) * block]).astype(BF16)
        for g in range(groups):
            gathered[g, a * 48 : (a + 1) * 48, :] = picked[g * 48 : (g + 1) * 48, :]

    size = params_ref[0:1, :]
    stiff = params_ref[1:2, :]
    yields = params_ref[2:3, :]
    rate8 = jnp.broadcast_to(params_ref[3:4, :], (8, block))
    inverse = 1.0 / yields
    weight = stiff * (2.0 / size) * inverse
    shear8 = jnp.broadcast_to(weight * SHEAR, (8, block))
    shear28 = shear8 * 2.0
    lame8 = jnp.broadcast_to(weight * LAME, (8, block))
    slot = lax.broadcasted_iota(jnp.int32, (1, block), 1) + step * block
    live = (slot < counts_ref[0]).astype(F32)
    scale = size * size * 0.25 * live * yields
    state = [stress_ref[c * 8 : (c + 1) * 8, :] * inverse for c in range(6)]
    for g in range(groups):
        delta = dot(strain_ref[...], gathered[g])
        for m in range(GROUP):
            d = [delta[m * 48 + c * 8 : m * 48 + c * 8 + 8, :] for c in range(6)]
            volume = (d[0] + d[1] + d[2]) * lame8
            for c in range(6):
                rise = d[c] * shear28 + volume if c < 3 else d[c] * shear8
                state[c] = state[c] + rise - rate8 * jnp.tanh(state[c])
            stresses[m * 48 : (m + 1) * 48, :] = jnp.concatenate(state, axis=0).astype(BF16)
        pushed = dot(force_ref[...], stresses[...]) * scale
        for a in range(8):
            forces[g * 48 : (g + 1) * 48, a * block : (a + 1) * block] = split_rows(
                pushed[a * 24 : (a + 1) * 24, :]
            )
    stress_out[...] = jnp.concatenate(state, axis=0) * (yields * live)
    total[...] += dot_t(onehot[...], forces[...])

    @pl.when(step == pl.num_programs(0) - 1)
    def _():
        summed = total[...]
        high = summed.astype(BF16)
        low = (summed - high.astype(F32)).astype(BF16)
        force_out[...] = (
            dot(high, an_hi_ref[...]) + dot(high, an_lo_ref[...]) + dot(low, an_hi_ref[...])
        )


def element_update(rows, conn_dev, count, params, stress_zero, block=256):
    elems = conn_dev.shape[0]
    nodes, width = rows.shape
    padded = -(-nodes // 256) * 256
    rows = jnp.pad(rows, ((0, padded - nodes), (0, 0)))
    synth, analyse, strain, force = host_tables(width // 3)
    synth_hi, synth_lo = two_parts(synth)
    an_hi, an_lo = two_parts(analyse)
    strain = jnp.asarray(strain, BF16)
    force = jnp.asarray(force, BF16)
    conn_t = jnp.transpose(conn_dev)
    whole = lambda x: pl.BlockSpec(x.shape, lambda s: (0,) * x.ndim)
    by_block = lambda r: pl.BlockSpec((r, block), lambda s: (0, s))
    return pl.pallas_call(
        element_kernel,
        grid=(elems // block,),
        out_shape=(
            jax.ShapeDtypeStruct(stress_zero.shape, F32),
            jax.ShapeDtypeStruct((padded, width), F32),
        ),
        in_specs=[
            pl.BlockSpec(memory_space=pltpu.SMEM),
            whole(rows), by_block(8), by_block(4), by_block(48),
            whole(synth_hi), whole(synth_lo), whole(an_hi), whole(an_lo),
            whole(strain), whole(force),
        ],
        out_specs=(by_block(48), pl.BlockSpec((padded, width), lambda s: (0, 0))),
        scratch_shapes=[
            pltpu.VMEM((6 * TIMES, padded), BF16),
            pltpu.VMEM((padded, 8 * block), BF16),
            pltpu.VMEM((TIMES // GROUP, GROUP * 48, block), BF16),
            pltpu.VMEM((GROUP * 48, block), BF16),
            pltpu.VMEM((6 * TIMES, 8 * block), BF16),
            pltpu.VMEM((padded, 6 * TIMES), F32),
        ],
        compiler_params=pltpu.CompilerParams(
            vmem_limit_bytes=40 * 1024 * 1024, dimension_semantics=("arbitrary",)
        ),
        name="elements",
    )(count, rows, conn_t, params, stress_zero, synth_hi, synth_lo, an_hi, an_lo, strain, force)


def passed_along(shard, axis, by):
    peers = lax.axis_size(axis)
    return lax.ppermute(shard, axis, [(i, (i + by) % peers) for i in range(peers)])


def per_device(
    u_int, u_if, load_int, load_if, conn, send_map, counts, elem_size, stiffness,
    yield_stress, relax_rate, stress_init, kinv_int, sinv,
):
    width = u_int.shape[1]
    fourier = width // 3
    int_nodes = u_int.shape[0]
    neighbours, slots = send_map.shape
    reach = neighbours // 2
    offsets = list(range(-reach, 0)) + list(range(1, reach + 1))
    local = jnp.concatenate([u_int, u_if], axis=0)
    local_rows = local.shape[0]
    blocks = jnp.take(local, send_map.reshape(-1), axis=0).reshape(neighbours, slots, width)
    halo = [passed_along(blocks[j], "dom", offsets[j]) for j in range(neighbours)]
    buffer = jnp.concatenate([local] + halo, axis=0)
    params = jnp.stack([elem_size, stiffness, yield_stress, relax_rate], axis=0)
    stress_end, assembled = element_update(buffer, conn, counts, params, stress_init)
    owned = assembled[:local_rows]
    back = assembled[local_rows : local_rows + neighbours * slots].reshape(neighbours, slots, width)
    returned = jnp.stack([passed_along(back[j], "dom", -offsets[j]) for j in range(neighbours)], axis=0)
    owned = owned + jax.ops.segment_sum(
        returned.reshape(neighbours * slots, width), send_map.reshape(-1), num_segments=local_rows
    )
    r_int = load_int - owned[:int_nodes]
    shared = owned[int_nodes:]
    group_force = lax.psum(shared, "grp")
    r_if = load_if - group_force
    rhs_int = r_int.astype(BF16).reshape(3 * int_nodes, fourier)
    rhs_if = r_if.astype(BF16).reshape(3 * r_if.shape[0], fourier)
    partial = jnp.dot(sinv, rhs_if, preferred_element_type=F32)
    du_if = lax.psum_scatter(partial, "dom", scatter_dimension=0, tiled=True)
    du_if = du_if.reshape(-1, width)
    du_int = jnp.dot(kinv_int, rhs_int, preferred_element_type=F32).reshape(int_nodes, width)
    return (du_int, du_if, stress_end)


def solution(mesh):
    both = ("grp", "dom")
    return jax.shard_map(
        per_device,
        mesh=mesh,
        in_specs=(
            P(both, None), P("dom", None), P(both, None), P("dom", None), P(both, None),
            P(both, None), P(both), P(both), P(both), P(both), P(both), P(None, both),
            P(both, None), P("grp", "dom"),
        ),
        out_specs=(P(both, None), P(both, None), P(None, both)),
        check_vma=False,
    )
```

time: 588 us -> 316 us (0.54); the launches traced: 578 us -> 315 us
  local copies, waits for them, and re-layouts: 241 us -> 13.5 us
  waiting for transfers between devices: 33.8 us -> 235 us
  other arithmetic: 146 us -> 7.78 us
  matrix products: 120 us -> 5.55 us
  Pallas kernels: 0 us -> 28.4 us
  starting transfers between devices: 23.6 us -> 9.04 us
  between operations: 2.1 us -> 15.7 us
  blocking collectives: 11.7 us -> 0 us
    unnamed x0 -> x3, waiting for transfers between devices: none -> 179 us
    dot_general x6 -> x2, matrix products: 120 us -> 5.55 us  [the longest x1 3.91 us: per_device(): jnp.dot(kinv_int, rhs_int, preferred_element_type=F32)]
    scatter-add x1 -> x0, other arithmetic: 88.3 us -> none  [element_update(): jnp.zeros((width, buffer_rows), jnp.float32).at[:, corner_index].add(forces)]
    slice x12 -> x3, local copies, waits for them, and re-layouts: 84.9 us -> 0.66 us  [the longest x1 0.64 us: per_device(): shared = owned[int_nodes:]]
    gather x2 -> x0, local copies, waits for them, and re-layouts: 75.4 us -> none  [element_update(): jnp.take(columns, corner_index, axis=1).reshape(3, fourier, 8, elems)]
    psum x0 -> x1, waiting for transfers between devices: none -> 49.1 us  [per_device(): group_force = lax.psum(shared, 'grp')]
    all_to_all x1 -> x0, waiting for transfers between devices: 30.4 us -> none  [summed_on_arrival(): lax.all_to_all(cut_along(shard, dim, peers), axis, 0, 0, tiled=True)]
    unnamed x35 -> x38, local copies, waits for them, and re-layouts: 36.6 us -> 6.46 us
  transfers between devices with their start and end apart: 9 -> 10, of which waited for: 3 -> 4; matrix products, arithmetic and copies ran while one was open for 2% -> 3% of each run, Pallas kernels for 0% -> 0%
where the time goes in v1:
time: 316 us; the launch traced here: 315 us
  waiting for transfers between devices  235 us (74%)
  Pallas kernels  28.4 us (9%)
  between operations  15.7 us (5%)
  local copies, waits for them, and re-layouts  13.5 us (4%)
  starting transfers between devices  9.04 us (3%)
  other arithmetic  7.78 us (2%)
  matrix products  5.55 us (2%)
    unnamed x3, waiting for transfers between devices  179 us
    psum x1, waiting for transfers between devices, per_device(): group_force = lax.psum(shared, 'grp')  49.1 us
    pallas_call x1, Pallas kernels, element_update(): pl.pallas_call(element_kernel, grid=(elems // block,), out_shape=(jax.Sha...  28.4 us
    ppermute x8, starting transfers between devices, passed_along(): lax.ppermute(shard, axis, [(i, (i + by) % peers) for i in range(peers)])  8.78 us
    ppermute x8, waiting for transfers between devices, passed_along(): lax.ppermute(shard, axis, [(i, (i + by) % peers) for i in range(peers)])  6.52 us
    unnamed x38, local copies, waits for them, and re-layouts  6.46 us
  transfers between devices with their start and end apart: 10, of which 4 were waited for; matrix products, arithmetic and copies ran while one was open for 3% of the time, Pallas kernels for 0%

profile of v1, /device:TPU:4, one launch (start us, length us, event | category | flops | bytes accessed | tf_op | source)
XLA Modules:
  0.0 314.8 jit_solution(17117428720695407230)
XLA Ops:
  7.4 0.9 reshape.79
  8.3 0.8 reshape.78
  9.1 1.8 copy.33
  12.0 1.7 pad_maximum_fusion
  13.8 1.9 gather_fusion
  17.5 1.5 collective-permute-start.3
  19.0 1.0 constant_dynamic-update-slice_fusion.5
  20.0 0.8 pad_maximum_fusion.2.params_ref
  21.5 5.0 %collective-permute-done.3 = bf16[32,192]{1,0:T(8,128)(2,1)S(1)} collective-permute-done((bf16[32,192]{1,0:T(8,128)(2,1)S(1)}, bf16[32,192]{1,0:T(8,128)(2,1)S(1)}, u32[]{:S(2)}, u32[]{:S(2)}) %collective-permute-start.3) | collective-permute-done | bytes 12320 | tf_op jit(solution)/shard_map/ppermute | solution.py:231
  26.6 28.4 %elements.1 = (f32[48,2048]{1,0:T(8,128)}, f32[768,192]{1,0:T(8,128)S(1)}) custom-call(s32[1]{0:T(128)S(6)} %copy.48.counts_ref, bf16[768,192]{1,0:T(8,128)(2,1)S(1)} %pad.4.rows_ref, s32[8,2048]{1,0:T(8,128)S(1)} %bitcast.23, f32[4,2048]{1,0:T(4,128)S(1)} %pad_maximum_fusion.2.params_ref, f32[48,2048]{1,0:T(8,128)S(1)} %copy-done.1, ...), custom_call_target="tpu_custom_call" | custom-call | tf_op jit(solution)/shard_map/elements/pallas_call | solution.py:200
  55.2 1.7 collective-permute-start.6
  56.9 4.3 %collective-permute-start.7 = (f32[32,192]{1,0:T(8,128)S(1)}, f32[32,192]{1,0:T(8,128)S(1)}, u32[]{:S(2)}, u32[]{:S(2)}) collective-permute-start(f32[32,192]{1,0:T(8,128)S(1)} %get-tuple-element.14), channel_id=1, source_target_pairs={{0,62},{1,63},{2,0},{3,1},{4,2},{5,3},{6,4},{7,5},{8,6},{9,7},{10,... | collective-permute-start | bytes 73736 | tf_op jit(solution)/shard_map/ppermute | solution.py:231
  61.3 1.5 collective-permute-done.7
  62.8 1.6 scatter_fusion
  65.4 1.2 copy.34
  67.8 49.1 %all-reduce.5.cloned.1.call-done = f32[88,192]{1,0:T(8,128)} async-done(((f32[88,192]{1,0:T(8,128)}), f32[88,192]{1,0:T(8,128)}) %all-reduce.5.cloned.1.call-update) | async-done | bytes 67600 | tf_op jit(solution)/shard_map/psum | solution.py:259
  117.0 0.9 subtract_convert_fusion
  118.0 1.6 convolution_bitcast_fusion
  119.7 0.8 fusion
  120.5 1.2 reshape.81
  121.7 3.9 %convolution_bitcast_fusion.1 = f32[1536,64]{0,1:T(8,128)S(1)} fusion(bf16[1536,64]{1,0:T(8,128)(2,1)S(1)} %reshape.81, bf16[1536,1536]{1,0:T(8,128)(2,1)} %param.32), kind=kOutput, calls=%fused_computation.3 | convolution fusion | flops 301989888 | bytes 5308416 | tf_op jit(solution)/shard_map/dot_general | solution.py:266
  126.2 0.9 copy.37
  127.1 179.2 %all-reduce.7.cloned.1.call-done = f32[4224,64]{0,1:T(8,128)} async-done(((f32[4224,64]{0,1:T(8,128)}), f32[4224,64]{0,1:T(8,128)}) %all-reduce.7.cloned.1.call-update) | async-done | bytes 1081360
  306.3 0.9 constant_dynamic-slice_fusion
  (64 shorter events, 6.5 us)
Async XLA Ops:
  7.2 110.9 %copy-start = (bf16[4224,264]{0,1:T(8,128)(2,1)S(1)}, bf16[4224,264]{0,1:T(8,128)(2,1)}, u32[]{:S(2)}) copy-start(bf16[4224,264]{0,1:T(8,128)(2,1)} %param.33) | copy-start | bytes 6690820
  7.2 19.4 %copy-start.7 = (bf16[96,192]{1,0:T(8,128)(2,1)S(1)}, bf16[96,192]{1,0:T(8,128)(2,1)}, u32[]{:S(2)}) copy-start(bf16[96,192]{1,0:T(8,128)(2,1)} %constant.32.clone.synth_hi_ref) | copy-start | bytes 110596
  7.2 19.4 %copy-start.8 = (bf16[96,192]{1,0:T(8,128)(2,1)S(1)}, bf16[96,192]{1,0:T(8,128)(2,1)}, u32[]{:S(2)}) copy-start(bf16[96,192]{1,0:T(8,128)(2,1)} %constant.33.clone.synth_lo_ref) | copy-start | bytes 110596
  7.2 19.4 %copy-start.4 = (bf16[192,192]{1,0:T(8,128)(2,1)S(1)}, bf16[192,192]{1,0:T(8,128)(2,1)}, u32[]{:S(2)}) copy-start(bf16[192,192]{1,0:T(8,128)(2,1)} %constant.34.clone.an_hi_ref) | copy-start | bytes 221188
  7.2 19.4 %copy-start.5 = (bf16[192,192]{1,0:T(8,128)(2,1)S(1)}, bf16[192,192]{1,0:T(8,128)(2,1)}, u32[]{:S(2)}) copy-start(bf16[192,192]{1,0:T(8,128)(2,1)} %constant.35.clone.an_lo_ref) | copy-start | bytes 221188
  7.2 19.4 %copy-start.2 = (bf16[384,384]{1,0:T(8,128)(2,1)S(1)}, bf16[384,384]{1,0:T(8,128)(2,1)}, u32[]{:S(2)}) copy-start(bf16[384,384]{1,0:T(8,128)(2,1)} %constant.36.clone.strain_ref) | copy-start | bytes 884740
  7.2 19.4 %copy-start.3 = (bf16[192,384]{1,0:T(8,128)(2,1)S(1)}, bf16[192,384]{1,0:T(8,128)(2,1)}, u32[]{:S(2)}) copy-start(bf16[192,384]{1,0:T(8,128)(2,1)} %constant.37.clone.force_ref) | copy-start | bytes 442372
  7.3 13.5 %copy-start.9 = (bf16[88,192]{1,0:T(8,128)(2,1)S(1)}, bf16[88,192]{1,0:T(8,128)(2,1)}, u32[]{:S(2)}) copy-start(bf16[88,192]{1,0:T(8,128)(2,1)} %param.21) | copy-start | bytes 101380
  7.3 12.7 %copy-start.11 = (f32[2048]{0:T(1024)S(1)}, f32[2048]{0:T(1024)}, u32[]{:S(2)}) copy-start(f32[2048]{0:T(1024)} %param.29) | copy-start | bytes 24580
  7.3 12.7 %copy-start.10 = (f32[2048]{0:T(1024)S(1)}, f32[2048]{0:T(1024)}, u32[]{:S(2)}) copy-start(f32[2048]{0:T(1024)} %param.30) | copy-start | bytes 24580
  7.3 19.3 %copy-start.6 = (s32[2048,8]{0,1:T(8,128)S(1)}, s32[2048,8]{0,1:T(8,128)}, u32[]{:S(2)}) copy-start(s32[2048,8]{0,1:T(8,128)} %param.24) | copy-start | bytes 196612
  7.3 19.3 %copy-start.1 = (f32[48,2048]{1,0:T(8,128)S(1)}, f32[48,2048]{1,0:T(8,128)}, u32[]{:S(2)}) copy-start(f32[48,2048]{1,0:T(8,128)} %stress_ref.1) | copy-start | bytes 1179652
  7.3 109.7 %all-reduce.5.cloned.1.call-start = ((), (), s32[]{:S(2)}) async-start(), calls=%async_computation | async-start | bytes 180224 | tf_op jit(solution)/shard_map/psum | solution.py:259
  9.1 3.0 copy-start.12
  16.4 5.0 %collective-permute-start = (bf16[32,192]{1,0:T(8,128)(2,1)S(1)}, bf16[32,192]{1,0:T(8,128)(2,1)S(1)}, u32[]{:S(2)}, u32[]{:S(2)}) collective-permute-start(bf16[32,192]{1,0:T(8,128)(2,1)S(1)} %get-tuple-element.20), channel_id=1, source_target_pairs={{0,62},{1,63},{2,0},{3,1},{4,2},{5,3},{6,4},{7,5},{8,6},{9,7},{10,... | collective-permute-start | bytes 36872 | tf_op jit(solution)/shard_map/ppermute | solution.py:231
  17.0 4.4 %collective-permute-start.1 = (bf16[32,192]{1,0:T(8,128)(2,1)S(1)}, bf16[32,192]{1,0:T(8,128)(2,1)S(1)}, u32[]{:S(2)}, u32[]{:S(2)}) collective-permute-start(bf16[32,192]{1,0:T(8,128)(2,1)S(1)} %get-tuple-element.19), channel_id=1, source_target_pairs={{0,63},{1,0},{2,1},{3,2},{4,3},{5,4},{6,5},{7,6},{8,7},{9,8},{10,9... | collective-permute-start | bytes 36872 | tf_op jit(solution)/shard_map/ppermute | solution.py:231
  17.0 4.5 %collective-permute-start.2 = (bf16[32,192]{1,0:T(8,128)(2,1)S(1)}, bf16[32,192]{1,0:T(8,128)(2,1)S(1)}, u32[]{:S(2)}, u32[]{:S(2)}) collective-permute-start(bf16[32,192]{1,0:T(8,128)(2,1)S(1)} %get-tuple-element.18), channel_id=1, source_target_pairs={{0,1},{1,2},{2,3},{3,4},{4,5},{5,6},{6,7},{7,8},{8,9},{9,10},{10,1... | collective-permute-start | bytes 36872 | tf_op jit(solution)/shard_map/ppermute | solution.py:231
  17.5 9.0 %collective-permute-start.3 = (bf16[32,192]{1,0:T(8,128)(2,1)S(1)}, bf16[32,192]{1,0:T(8,128)(2,1)S(1)}, u32[]{:S(2)}, u32[]{:S(2)}) collective-permute-start(bf16[32,192]{1,0:T(8,128)(2,1)S(1)} %get-tuple-element.17), channel_id=1, source_target_pairs={{0,2},{1,3},{2,4},{3,5},{4,6},{5,7},{6,8},{7,9},{8,10},{9,11},{10,... | collective-permute-start | bytes 36872 | tf_op jit(solution)/shard_map/ppermute | solution.py:231
  55.0 6.2 %collective-permute-start.4 = (f32[32,192]{1,0:T(8,128)S(1)}, f32[32,192]{1,0:T(8,128)S(1)}, u32[]{:S(2)}, u32[]{:S(2)}) collective-permute-start(f32[32,192]{1,0:T(8,128)S(1)} %get-tuple-element.13), channel_id=1, source_target_pairs={{0,2},{1,3},{2,4},{3,5},{4,6},{5,7},{6,8},{7,9},{8,10},{9,11},{10,... | collective-permute-start | bytes 73736 | tf_op jit(solution)/shard_map/ppermute | solution.py:231
  55.1 6.2 %collective-permute-start.5 = (f32[32,192]{1,0:T(8,128)S(1)}, f32[32,192]{1,0:T(8,128)S(1)}, u32[]{:S(2)}, u32[]{:S(2)}) collective-permute-start(f32[32,192]{1,0:T(8,128)S(1)} %get-tuple-element.16), channel_id=1, source_target_pairs={{0,1},{1,2},{2,3},{3,4},{4,5},{5,6},{6,7},{7,8},{8,9},{9,10},{10,1... | collective-permute-start | bytes 73736 | tf_op jit(solution)/shard_map/ppermute | solution.py:231
  55.2 6.1 %collective-permute-start.6 = (f32[32,192]{1,0:T(8,128)S(1)}, f32[32,192]{1,0:T(8,128)S(1)}, u32[]{:S(2)}, u32[]{:S(2)}) collective-permute-start(f32[32,192]{1,0:T(8,128)S(1)} %get-tuple-element.15), channel_id=1, source_target_pairs={{0,63},{1,0},{2,1},{3,2},{4,3},{5,4},{6,5},{7,6},{8,7},{9,8},{10,9... | collective-permute-start | bytes 73736 | tf_op jit(solution)/shard_map/ppermute | solution.py:231
  56.9 9.6 %copy-start.13 = (u32[256]{0:T(256)S(1)}, u32[256]{0:T(256)}, u32[]{:S(2)}) copy-start(u32[256]{0:T(256)} %constant.47) | copy-start | bytes 3076
  56.9 5.9 %collective-permute-start.7 = (f32[32,192]{1,0:T(8,128)S(1)}, f32[32,192]{1,0:T(8,128)S(1)}, u32[]{:S(2)}, u32[]{:S(2)}) collective-permute-start(f32[32,192]{1,0:T(8,128)S(1)} %get-tuple-element.14), channel_id=1, source_target_pairs={{0,62},{1,63},{2,0},{3,1},{4,2},{5,3},{6,4},{7,5},{8,6},{9,7},{10,... | collective-permute-start | bytes 73736 | tf_op jit(solution)/shard_map/ppermute | solution.py:231
  65.1 241.2 %all-reduce.7.cloned.1.call-start = ((), (), s32[]{:S(2)}) async-start(), calls=%async_computation.1 | async-start | bytes 2162688
Sparse Core Ops, SparseCore 0:
  65.2 51.6 all-reduce.4
  120.8 185.4 all-reduce.6

commit v2 on v1

--- a/solution.py
+++ b/solution.py
@@ -114,7 +114,7 @@
 
 
 def element_kernel(
-    counts_ref, rows_ref, conn_ref, params_ref, stress_ref,
+    counts_ref, rows_ref, conn_ref, size_ref, stiff_ref, yield_ref, rate_ref, stress_ref,
     synth_hi_ref, synth_lo_ref, an_hi_ref, an_lo_ref, strain_ref, force_ref,
     stress_out, force_out,
     nodal, onehot, gathered, stresses, forces, total,
@@ -144,10 +144,10 @@
         for g in range(groups):
             gathered[g, a * 48 : (a + 1) * 48, :] = picked[g * 48 : (g + 1) * 48, :]
 
-    size = params_ref[0:1, :]
-    stiff = params_ref[1:2, :]
-    yields = params_ref[2:3, :]
-    rate8 = jnp.broadcast_to(params_ref[3:4, :], (8, block))
+    size = size_ref[...]
+    stiff = stiff_ref[...]
+    yields = yield_ref[...]
+    rate8 = jnp.broadcast_to(rate_ref[...], (8, block))
     inverse = 1.0 / yields
     weight = stiff * (2.0 / size) * inverse
     shear8 = jnp.broadcast_to(weight * SHEAR, (8, block))
@@ -184,17 +184,14 @@
         )
 
 
-def element_update(rows, conn_dev, count, params, stress_zero, block=256):
-    elems = conn_dev.shape[0]
-    nodes, width = rows.shape
-    padded = -(-nodes // 256) * 256
-    rows = jnp.pad(rows, ((0, padded - nodes), (0, 0)))
+def element_update(rows, conn_t, count, params, stress_zero, block=256):
+    elems = conn_t.shape[1]
+    padded, width = rows.shape
     synth, analyse, strain, force = host_tables(width // 3)
     synth_hi, synth_lo = two_parts(synth)
     an_hi, an_lo = two_parts(analyse)
     strain = jnp.asarray(strain, BF16)
     force = jnp.asarray(force, BF16)
-    conn_t = jnp.transpose(conn_dev)
     whole = lambda x: pl.BlockSpec(x.shape, lambda s: (0,) * x.ndim)
     by_block = lambda r: pl.BlockSpec((r, block), lambda s: (0, s))
     return pl.pallas_call(
@@ -206,7 +203,7 @@
         ),
         in_specs=[
             pl.BlockSpec(memory_space=pltpu.SMEM),
-            whole(rows), by_block(8), by_block(4), by_block(48),
+            whole(rows), by_block(8), by_block(1), by_block(1), by_block(1), by_block(1), by_block(48),
             whole(synth_hi), whole(synth_lo), whole(an_hi), whole(an_lo),
             whole(strain), whole(force),
         ],
@@ -223,47 +220,314 @@
             vmem_limit_bytes=40 * 1024 * 1024, dimension_semantics=("arbitrary",)
         ),
         name="elements",
-    )(count, rows, conn_t, params, stress_zero, synth_hi, synth_lo, an_hi, an_lo, strain, force)
-
-
-def passed_along(shard, axis, by):
-    peers = lax.axis_size(axis)
-    return lax.ppermute(shard, axis, [(i, (i + by) % peers) for i in range(peers)])
+    )(count, rows, conn_t, *params, stress_zero, synth_hi, synth_lo, an_hi, an_lo, strain, force)
+
+
+MESH = pl.DeviceIdType.MESH
+
+
+def pair_hits(map_ref, rows):
+    neighbours, slots = map_ref.shape
+    listed = jnp.concatenate([map_ref[j : j + 1, :] for j in range(neighbours)], axis=1)
+    iota = lax.broadcasted_iota(jnp.int32, (rows, neighbours * slots), 0)
+    return (iota == listed).astype(F32)
+
+
+def greet(peers):
+    barrier = pltpu.get_barrier_semaphore()
+    for peer in peers:
+        pl.semaphore_signal(barrier, inc=1, device_id=peer, device_id_type=MESH)
+    pl.semaphore_wait(barrier, len(peers))
+
+
+def send(src, dst, send_sem, recv_sem, peer):
+    copy = pltpu.make_async_remote_copy(
+        src_ref=src, dst_ref=dst, send_sem=send_sem, recv_sem=recv_sem,
+        device_id=peer, device_id_type=MESH,
+    )
+    copy.start()
+    return copy
+
+
+def halo_kernel(dom, offsets, int_ref, if_ref, map_ref, conn_ref, rows_out, conn_out, out_block, in_block, send_sem, recv_sem):
+    me = lax.axis_index("dom")
+    near = [{"dom": lax.rem(me + off + dom, dom)} for off in offsets]
+    int_nodes, width = int_ref.shape
+    if_nodes = if_ref.shape[0]
+    slots = map_ref.shape[1]
+    owned = int_nodes + if_nodes
+    local = jnp.concatenate([int_ref[...], if_ref[...]], axis=0)
+    hits = jnp.transpose(pair_hits(map_ref, owned)).astype(BF16)
+    picked = dot(hits, local).astype(BF16)
+    for j in range(len(offsets)):
+        out_block[j] = picked[j * slots : (j + 1) * slots]
+    greet(near)
+    copies = [
+        send(out_block.at[j], in_block.at[j], send_sem.at[j], recv_sem.at[j], near[j])
+        for j in range(len(offsets))
+    ]
+    conn_out[...] = jnp.transpose(conn_ref[...])
+    rows_out[...] = jnp.zeros_like(rows_out)
+    rows_out[0:owned] = local
+    for j, copy in enumerate(copies):
+        copy.wait()
+        rows_out[owned + j * slots : owned + (j + 1) * slots] = in_block[j]
+
+
+def halo(u_int, u_if, send_map, conn, offsets, dom):
+    neighbours, slots = send_map.shape
+    width = u_int.shape[1]
+    used = u_int.shape[0] + u_if.shape[0] + neighbours * slots
+    padded = -(-used // 256) * 256
+    vmem = pl.BlockSpec(memory_space=pltpu.VMEM)
+    return pl.pallas_call(
+        functools.partial(halo_kernel, dom, offsets),
+        out_shape=(
+            jax.ShapeDtypeStruct((padded, width), BF16),
+            jax.ShapeDtypeStruct((conn.shape[1], conn.shape[0]), jnp.int32),
+        ),
+        in_specs=[vmem] * 4,
+        out_specs=(vmem, vmem),
+        scratch_shapes=[
+            pltpu.VMEM((neighbours, slots, width), BF16),
+            pltpu.VMEM((neighbours, slots, width), BF16),
+            pltpu.SemaphoreType.DMA((neighbours,)),
+            pltpu.SemaphoreType.DMA((neighbours,)),
+        ],
+        compiler_params=pltpu.CompilerParams(
+            collective_id=0, has_side_effects=True, vmem_limit_bytes=24 * 1024 * 1024
+        ),
+        name="halo",
+    )(u_int, u_if, send_map, conn)
+
+
+def finish_kernel(
+    sizes, offsets,
+    force_ref, map_ref, load_int_ref, load_if_ref, kinv_hbm, sinv_hbm,
+    du_int_ref, du_if_ref,
+    kinv, sinv, out_ret, in_ret, spread, spread_if, rhs_int,
+    out_grp, in_grp, out_rhs, all_rhs, flat,
+    own1, out1, in1, out2, in2, own3, out3, in3, last,
+    local_sem, ret_sem, grp_sem, rhs_sem, sem1, sem2, sem3,
+):
+    zs, xs, cores, grps = sizes
+    dom = zs * xs * cores
+    me = lax.axis_index("dom")
+    my_grp = lax.axis_index("grp")
+    core = lax.rem(me, cores)
+    x = lax.rem(me // cores, xs)
+    z = me // (cores * xs)
+    fetch_kinv = pltpu.make_async_copy(kinv_hbm, kinv, local_sem.at[0])
+    fetch_sinv = pltpu.make_async_copy(sinv_hbm, sinv, local_sem.at[1])
+    fetch_kinv.start()
+    fetch_sinv.start()
+    at = lambda zz, xx, cc: {"dom": (zz * xs + xx) * cores + cc}
+    owners = [{"dom": lax.rem(me - off + dom, dom)} for off in offsets]
+    groups = [{"grp": lax.rem(my_grp + s, grps)} for s in range(1, grps)]
+    sibling = at(z, x, 1 - core)
+    along_x = [at(z, lax.rem(x + s, xs), core) for s in range(1, xs)]
+    along_z = [at(lax.rem(z + s, zs), x, core) for s in range(1, zs)]
+    neighbours, slots = map_ref.shape
+    int_nodes, width = load_int_ref.shape
+    if_nodes = load_if_ref.shape[0]
+    fourier = width // 3
+    owned = int_nodes + if_nodes
+    for j in range(neighbours):
+        out_ret[j] = force_ref[owned + j * slots : owned + (j + 1) * slots, :]
+    greet(owners + groups + [sibling] + along_x + along_z)
+    copies = [
+        send(out_ret.at[j], in_ret.at[j], ret_sem.at[0, j], ret_sem.at[1, j], owners[j])
+        for j in range(neighbours)
+    ]
+    hits = pair_hits(map_ref, owned).astype(BF16)
+    for copy in copies:
+        copy.wait()
+    back = jnp.concatenate([in_ret[j] for j in range(neighbours)], axis=0)
+    high = back.astype(BF16)
+    low = (back - high.astype(F32)).astype(BF16)
+    force = force_ref[0:owned, :] + dot(hits, high) + dot(hits, low)
+    share = out_grp.shape[1]
+    pieces = jnp.concatenate(
+        [force[int_nodes:], jnp.zeros((grps * share - if_nodes, width), F32)], axis=0
+    )
+    for q in range(grps):
+        out_grp[q] = pieces[q * share : (q + 1) * share]
+    copies = [
+        send(out_grp.at[peer["grp"]], in_grp.at[s], grp_sem.at[0, s], grp_sem.at[1, s], peer)
+        for s, peer in enumerate(groups)
+    ]
+    r_int = load_int_ref[...] - force[:int_nodes]
+    for i in range(3):
+        spread[pl.ds(i, int_nodes, stride=3), :] = r_int[:, i * fourier : (i + 1) * fourier]
+    rhs_int[...] = spread[...].astype(BF16)
+    fetch_kinv.wait()
+    chunk = 256
+    chunks = kinv.shape[0] // chunk
+
+    def solve(c, _):
+        rows = pl.ds(pl.multiple_of(c * chunk, chunk), chunk)
+        spread[rows, :] = dot(kinv[rows, :], rhs_int[...])
+        return 0
+
+    lax.fori_loop(0, chunks // 2, solve, 0)
+    loads = jnp.concatenate(
+        [load_if_ref[...], jnp.zeros((grps * share - if_nodes, width), F32)], axis=0
+    )
+    mine = loads[0:share]
+    for q in range(1, grps):
+        mine = jnp.where(my_grp == q, loads[q * share : (q + 1) * share], mine)
+    total = out_grp[my_grp]
+    for s, copy in enumerate(copies):
+        copy.wait()
+        total = total + in_grp[s]
+    out_rhs[...] = (mine - total).astype(BF16)
+    copies = [
+        send(out_rhs, all_rhs.at[my_grp], rhs_sem.at[0, s], rhs_sem.at[1, s], peer)
+        for s, peer in enumerate(groups)
+    ]
+    all_rhs[my_grp] = out_rhs[...]
+    lax.fori_loop(chunks // 2, chunks, solve, 0)
+    for copy in copies:
+        copy.wait()
+    gathered = jnp.concatenate([all_rhs[q].astype(F32) for q in range(grps)], axis=0)[:if_nodes]
+    for i in range(3):
+        spread_if[pl.ds(i, if_nodes, stride=3), :] = gathered[:, i * fourier : (i + 1) * fourier]
+    rhs_if = spread_if[...]
+    empty = jnp.zeros_like(rhs_if)
+    left = jnp.concatenate([rhs_if, empty], axis=1).astype(BF16)
+    right = jnp.concatenate([empty, rhs_if], axis=1).astype(BF16)
+    fetch_sinv.wait()
+    half = zs // 2
+    per_owner = sinv.shape[0] // dom
+    per_z = per_owner * xs * cores
+    for q in range(half):
+        flat[q * per_z : (q + 1) * per_z, :] = dot(
+            sinv[q * per_z : (q + 1) * per_z, :], left
+        ) + dot(sinv[(half + q) * per_z : (half + q + 1) * per_z, :], right)
+    fill = jnp.zeros((out1.shape[1] - half * per_owner, 2 * fourier), F32)
+    for k in range(xs):
+        by_core = []
+        for c in range(cores):
+            rows = [
+                flat[q * per_z + (k * cores + c) * per_owner : q * per_z + (k * cores + c + 1) * per_owner, :]
+                for q in range(half)
+            ]
+            by_core.append(jnp.concatenate(rows + [fill], axis=0))
+        own1[k] = jnp.where(core == 0, by_core[0], by_core[1])
+        out1[k] = jnp.where(core == 0, by_core[1], by_core[0]).astype(BF16)
+    copy = send(out1, in1, sem1.at[0], sem1.at[1], sibling)
+    for i in range(3):
+        du_int_ref[:, i * fourier : (i + 1) * fourier] = spread[pl.ds(i, int_nodes, stride=3), :]
+    copy.wait()
+    for k in range(xs):
+        summed = own1[k] + in1[k].astype(F32)
+        own1[k] = summed
+        out2[k] = summed.astype(BF16)
+    copies = [
+        send(out2.at[lax.rem(x + s + 1, xs)], in2.at[s], sem2.at[0, s], sem2.at[1, s], peer)
+        for s, peer in enumerate(along_x)
+    ]
+    summed = own1[x]
+    for s, copy in enumerate(copies):
+        copy.wait()
+        summed = summed + in2[s].astype(F32)
+    turned = pltpu.roll(summed, fourier, 1)
+    short = per_owner // 2
+    first = lax.broadcasted_iota(jnp.int32, (short, 2 * fourier), 1) < fourier
+    fill = jnp.zeros((out3.shape[1] - short, 2 * fourier), F32)
+    for q in range(half):
+        top = slice(q * per_owner, q * per_owner + short)
+        low_rows = slice(q * per_owner + short, (q + 1) * per_owner)
+        for h, (a, b) in enumerate(((summed, turned), (turned, summed))):
+            block = jnp.concatenate([jnp.where(first, a[top], b[low_rows]), fill], axis=0)
+            own3[h * half + q] = block
+            out3[h * half + q] = block.astype(BF16)
+    copies = [
+        send(out3.at[lax.rem(z + s + 1, zs)], in3.at[s], sem3.at[0, s], sem3.at[1, s], peer)
+        for s, peer in enumerate(along_z)
+    ]
+    summed = own3[z]
+    for s, copy in enumerate(copies):
+        copy.wait()
+        summed = summed + in3[s].astype(F32)
+    last[0] = summed
+    last[1] = pltpu.roll(summed, fourier, 1)
+    nodes = short // 3
+    for h in range(2):
+        for i in range(3):
+            du_if_ref[h * nodes : (h + 1) * nodes, i * fourier : (i + 1) * fourier] = last[
+                h, pl.ds(i, nodes, stride=3), :
+            ][:, :fourier]
+
+
+def finish(force, send_map, load_int, load_if, kinv_int, sinv, offsets, sizes):
+    zs, xs, cores, grps = sizes
+    neighbours, slots = send_map.shape
+    int_nodes, width = load_int.shape
+    if_nodes = load_if.shape[0]
+    fourier = width // 3
+    dom = zs * xs * cores
+    per_owner = sinv.shape[0] // dom
+    up = lambda n, k: -(-n // k) * k
+    share = up(-(-if_nodes // grps), 8)
+    rows1 = up(per_owner * (zs // 2), 16)
+    rows3 = up(per_owner // 2, 16)
+    vmem = pl.BlockSpec(memory_space=pltpu.VMEM)
+    far = pl.BlockSpec(memory_space=pl.ANY)
+    sems = pltpu.SemaphoreType.DMA
+    lanes = 2 * fourier
+    return pl.pallas_call(
+        functools.partial(finish_kernel, sizes, offsets),
+        out_shape=(
+            jax.ShapeDtypeStruct((int_nodes, width), F32),
+            jax.ShapeDtypeStruct((per_owner // 3, width), F32),
+        ),
+        in_specs=[vmem] * 4 + [far, far],
+        out_specs=(vmem, vmem),
+        scratch_shapes=[
+            pltpu.VMEM(kinv_int.shape, BF16),
+            pltpu.VMEM(sinv.shape, BF16),
+            pltpu.VMEM((neighbours, slots, width), F32),
+            pltpu.VMEM((neighbours, slots, width), F32),
+            pltpu.VMEM((3 * int_nodes, fourier), F32),
+            pltpu.VMEM((3 * if_nodes, fourier), F32),
+            pltpu.VMEM((3 * int_nodes, fourier), BF16),
+            pltpu.VMEM((grps, share, width), F32),
+            pltpu.VMEM((grps - 1, share, width), F32),
+            pltpu.VMEM((share, width), BF16),
+            pltpu.VMEM((grps, share, width), BF16),
+            pltpu.VMEM((sinv.shape[0] // 2, lanes), F32),
+            pltpu.VMEM((xs, rows1, lanes), F32),
+            pltpu.VMEM((xs, rows1, lanes), BF16),
+            pltpu.VMEM((xs, rows1, lanes), BF16),
+            pltpu.VMEM((xs, rows1, lanes), BF16),
+            pltpu.VMEM((xs - 1, rows1, lanes), BF16),
+            pltpu.VMEM((zs, rows3, lanes), F32),
+            pltpu.VMEM((zs, rows3, lanes), BF16),
+            pltpu.VMEM((zs - 1, rows3, lanes), BF16),
+            pltpu.VMEM((2, rows3, lanes), F32),
+            sems((2,)), sems((2, neighbours)), sems((2, grps - 1)), sems((2, grps - 1)),
+            sems((2,)), sems((2, xs - 1)), sems((2, zs - 1)),
+        ],
+        compiler_params=pltpu.CompilerParams(
+            collective_id=1, has_side_effects=True, vmem_limit_bytes=40 * 1024 * 1024
+        ),
+        name="finish",
+    )(force, send_map, load_int, load_if, kinv_int, sinv)
 
 
 def per_device(
     u_int, u_if, load_int, load_if, conn, send_map, counts, elem_size, stiffness,
     yield_stress, relax_rate, stress_init, kinv_int, sinv,
 ):
-    width = u_int.shape[1]
-    fourier = width // 3
-    int_nodes = u_int.shape[0]
-    neighbours, slots = send_map.shape
-    reach = neighbours // 2
+    reach = send_map.shape[0] // 2
     offsets = list(range(-reach, 0)) + list(range(1, reach + 1))
-    local = jnp.concatenate([u_int, u_if], axis=0)
-    local_rows = local.shape[0]
-    blocks = jnp.take(local, send_map.reshape(-1), axis=0).reshape(neighbours, slots, width)
-    halo = [passed_along(blocks[j], "dom", offsets[j]) for j in range(neighbours)]
-    buffer = jnp.concatenate([local] + halo, axis=0)
-    params = jnp.stack([elem_size, stiffness, yield_stress, relax_rate], axis=0)
-    stress_end, assembled = element_update(buffer, conn, counts, params, stress_init)
-    owned = assembled[:local_rows]
-    back = assembled[local_rows : local_rows + neighbours * slots].reshape(neighbours, slots, width)
-    returned = jnp.stack([passed_along(back[j], "dom", -offsets[j]) for j in range(neighbours)], axis=0)
-    owned = owned + jax.ops.segment_sum(
-        returned.reshape(neighbours * slots, width), send_map.reshape(-1), num_segments=local_rows
-    )
-    r_int = load_int - owned[:int_nodes]
-    shared = owned[int_nodes:]
-    group_force = lax.psum(shared, "grp")
-    r_if = load_if - group_force
-    rhs_int = r_int.astype(BF16).reshape(3 * int_nodes, fourier)
-    rhs_if = r_if.astype(BF16).reshape(3 * r_if.shape[0], fourier)
-    partial = jnp.dot(sinv, rhs_if, preferred_element_type=F32)
-    du_if = lax.psum_scatter(partial, "dom", scatter_dimension=0, tiled=True)
-    du_if = du_if.reshape(-1, width)
-    du_int = jnp.dot(kinv_int, rhs_int, preferred_element_type=F32).reshape(int_nodes, width)
+    dom, grps = lax.axis_size("dom"), lax.axis_size("grp")
+    sizes = (dom // 8, 4, 2, grps)
+    rows, conn_t = halo(u_int, u_if, send_map, conn, offsets, dom)
+    params = [v.reshape(1, -1) for v in (elem_size, stiffness, yield_stress, relax_rate)]
+    stress_end, force = element_update(rows, conn_t, counts, params, stress_init)
+    du_int, du_if = finish(force, send_map, load_int, load_if, kinv_int, sinv, offsets, sizes)
     return (du_int, du_if, stress_end)
 
 

time: 316 us -> 92.9 us (0.29)
  waiting for transfers between devices: 235 us -> 0 us
  Pallas kernels: 28.4 us -> 72.2 us
  between operations: 15.7 us -> 1.65 us
  starting transfers between devices: 9.04 us -> 0 us
  other arithmetic: 7.78 us -> 0 us
  matrix products: 5.55 us -> 0 us
  local copies, waits for them, and re-layouts: 13.5 us -> 18.6 us
    unnamed x3 -> x0, waiting for transfers between devices: 179 us -> none
    psum x1 -> x0, waiting for transfers between devices: 49.1 us -> none  [per_device(): group_force = lax.psum(shared, 'grp')]
    pallas_call x0 -> x2, Pallas kernels: none -> 43.9 us  [the longest x1 38.7 us: finish(): pl.pallas_call(functools.partial(finish_kernel, sizes, offsets), out_shap...]
    unnamed x38 -> x46, local copies, waits for them, and re-layouts: 6.46 us -> 18.6 us
    ppermute x8 -> x0, starting transfers between devices: 8.78 us -> none  [passed_along(): lax.ppermute(shard, axis, [(i, (i + by) % peers) for i in range(peers)])]
    ppermute x8 -> x0, waiting for transfers between devices: 6.52 us -> none  [passed_along(): lax.ppermute(shard, axis, [(i, (i + by) % peers) for i in range(peers)])]
    dot_general x2 -> x0, matrix products: 5.55 us -> none  [the longest x1 3.91 us: per_device(): jnp.dot(kinv_int, rhs_int, preferred_element_type=F32)]
    reshape x6 -> x0, local copies, waits for them, and re-layouts: 3.99 us -> none  [the longest x2 1.71 us: per_device(): send_map.reshape(-1)]
  transfers between devices with their start and end apart: 10 -> 0, of which waited for: 4 -> 0; matrix products, arithmetic and copies ran while one was open for 3% -> 0% of each run, Pallas kernels for 0% -> 0%
where the time goes in v2:
time: 92.9 us; the launch traced here: 92.4 us
  Pallas kernels  72.2 us (78%)
  local copies, waits for them, and re-layouts  18.6 us (20%)
  between operations  1.65 us (2%)
    pallas_call x1, Pallas kernels, finish(): pl.pallas_call(functools.partial(finish_kernel, sizes, offsets), out_shap...  38.7 us
    pallas_call x1, Pallas kernels, element_update(): pl.pallas_call(element_kernel, grid=(elems // block,), out_shape=(jax.Sha...  28.3 us
    unnamed x46, local copies, waits for them, and re-layouts  18.6 us
    pallas_call x1, Pallas kernels, halo(): pl.pallas_call(functools.partial(halo_kernel, dom, offsets), out_shape=(j...  5.17 us

profile of v2, /device:TPU:4, one launch (start us, length us, event | category | flops | bytes accessed | tf_op | source)
XLA Modules:
  0.0 92.4 jit_solution(4613278144693355462)
XLA Ops:
  0.6 0.0 copy-start.7
  0.6 0.0 copy-start.6
  0.7 0.0 copy-start.8
  0.7 0.0 copy-start.9
  0.7 0.0 copy-start.11
  0.7 0.0 copy-start.12
  1.5 1.1 %copy.23.int_ref = bf16[512,192]{1,0:T(8,128)(2,1)S(1)} copy(bf16[512,192]{0,1:T(8,128)(2,1)} %param.20) | data formatting | bytes 393216 | tf_op args[0]
  2.6 2.0 %copy.25.load_int_ref = f32[512,192]{1,0:T(8,128)} copy(f32[512,192]{0,1:T(8,128)} %param.22) | data formatting | bytes 786432 | tf_op args[2]
  4.6 1.2 %copy.24.conn_ref = s32[2048,8]{1,0:T(8,128)S(1)} copy(s32[2048,8]{0,1:T(8,128)} %param.24) | data formatting | bytes 131072 | tf_op args[4]
  5.8 0.8 copy-done.13
  6.5 0.7 copy-done.18
  7.2 5.2 %halo.1 = (bf16[768,192]{1,0:T(8,128)(2,1)S(1)}, s32[8,2048]{1,0:T(8,128)S(1)}) custom-call(bf16[512,192]{1,0:T(8,128)(2,1)S(1)} %copy.23.int_ref, bf16[88,192]{1,0:T(8,128)(2,1)S(1)} %copy-done.13, s32[4,32]{1,0:T(4,128)S(1)} %copy-done.18, s32[2048,8]{1,0:T(8,128)S(1)} %copy.24.conn_ref), custom_call_target="tpu_custom_call" | custom-call | tf_op jit(solution)/shard_map/halo/pallas_call | solution.py:283
  12.5 0.0 copy-start.10
  12.5 28.3 %elements.1 = (f32[48,2048]{1,0:T(8,128)}, f32[768,192]{1,0:T(8,128)S(1)}) custom-call(s32[1]{0:T(128)S(6)} %copy.29.counts_ref, bf16[768,192]{1,0:T(8,128)(2,1)S(1)} %get-tuple-element.9.rows_ref, s32[8,2048]{1,0:T(8,128)S(1)} %get-tuple-element.10.conn_ref, f32[1,2048]{1,0:T(1,128)S(1)} %bitcast.4, f32[1,2048]{1,0:T(1,128)S(1)} %bitcast.5, ...), custom_call_target="tpu_custom_call" | custom-call | tf_op jit(solution)/shard_map/elements/pallas_call | solution.py:197
  40.8 0.9 copy-done.2
  41.7 4.0 %copy.26.sinv_hbm = bf16[4224,264]{1,0:T(8,128)(2,1)S(1)} copy(bf16[4224,264]{0,1:T(8,128)(2,1)} %param.33) | data formatting | bytes 4460544 | tf_op args[13]
  45.8 0.0 copy-start
  45.8 2.3 %copy-done = bf16[1536,1536]{1,0:T(8,128)(2,1)S(1)} copy-done((bf16[1536,1536]{1,0:T(8,128)(2,1)S(1)}, bf16[1536,1536]{1,0:T(8,128)(2,1)}, u32[]{:S(2)}) %copy-start) | copy-done | bytes 4718616
  48.1 1.0 %copy-done.1 = f32[512,192]{1,0:T(8,128)S(1)} copy-done((f32[512,192]{1,0:T(8,128)S(1)}, f32[512,192]{1,0:T(8,128)}, u32[]{:S(2)}) %copy-start.1) | copy-done | bytes 393240
  49.1 1.1 %copy-done.3 = f32[768,192]{1,0:T(8,128)S(1)} copy-done((f32[768,192]{1,0:T(8,128)S(1)}, f32[768,192]{1,0:T(8,128)}, u32[]{:S(2)}) %copy-start.3) | copy-done | bytes 589848
  50.3 38.7 %finish.1 = (f32[512,192]{1,0:T(8,128)S(1)}, f32[22,192]{1,0:T(8,128)S(1)}) custom-call(f32[768,192]{1,0:T(8,128)S(1)} %copy-done.3, s32[4,32]{1,0:T(4,128)S(1)} %copy-done.19, f32[512,192]{1,0:T(8,128)S(1)} %copy-done.1, f32[88,192]{1,0:T(8,128)S(1)} %copy-done.10, bf16[1536,1536]{1,0:T(8,128)(2,1)S(1)} %copy-done, bf16[4224,264]{1,0:T(8,128)(2,1)S(1)} %copy.26.sinv_hbm), custom_call_target="tpu_custom_call" | custom-call | tf_op jit(solution)/shard_map/finish/pallas_call | solution.py:479
  89.0 0.8 copy-done.4
  89.8 2.0 %copy.27 = f32[512,192]{0,1:T(8,128)} copy(f32[512,192]{1,0:T(8,128)} %copy-done.4) | data formatting | bytes 786432
  91.8 0.6 copy.30
  (25 shorter events, 0.1 us)
Async XLA Ops:
  0.6 11.8 %copy-start.7 = (bf16[192,384]{1,0:T(8,128)(2,1)S(1)}, bf16[192,384]{1,0:T(8,128)(2,1)}, u32[]{:S(2)}) copy-start(bf16[192,384]{1,0:T(8,128)(2,1)} %constant.17.clone.force_ref) | copy-start | bytes 442372
  0.6 11.8 %copy-start.6 = (bf16[384,384]{1,0:T(8,128)(2,1)S(1)}, bf16[384,384]{1,0:T(8,128)(2,1)}, u32[]{:S(2)}) copy-start(bf16[384,384]{1,0:T(8,128)(2,1)} %constant.16.clone.strain_ref) | copy-start | bytes 884740
  0.7 11.8 %copy-start.8 = (bf16[192,192]{1,0:T(8,128)(2,1)S(1)}, bf16[192,192]{1,0:T(8,128)(2,1)}, u32[]{:S(2)}) copy-start(bf16[192,192]{1,0:T(8,128)(2,1)} %constant.15.clone.an_lo_ref) | copy-start | bytes 221188
  0.7 11.8 %copy-start.9 = (bf16[192,192]{1,0:T(8,128)(2,1)S(1)}, bf16[192,192]{1,0:T(8,128)(2,1)}, u32[]{:S(2)}) copy-start(bf16[192,192]{1,0:T(8,128)(2,1)} %constant.14.clone.an_hi_ref) | copy-start | bytes 221188
  0.7 11.8 %copy-start.11 = (bf16[96,192]{1,0:T(8,128)(2,1)S(1)}, bf16[96,192]{1,0:T(8,128)(2,1)}, u32[]{:S(2)}) copy-start(bf16[96,192]{1,0:T(8,128)(2,1)} %constant.13.clone.synth_lo_ref) | copy-start | bytes 110596
  0.7 11.8 %copy-start.12 = (bf16[96,192]{1,0:T(8,128)(2,1)S(1)}, bf16[96,192]{1,0:T(8,128)(2,1)}, u32[]{:S(2)}) copy-start(bf16[96,192]{1,0:T(8,128)(2,1)} %constant.12.clone.synth_hi_ref) | copy-start | bytes 110596
  0.7 11.8 %copy-start.5 = (f32[48,2048]{1,0:T(8,128)S(1)}, f32[48,2048]{1,0:T(8,128)}, u32[]{:S(2)}) copy-start(f32[48,2048]{1,0:T(8,128)} %stress_ref.1) | copy-start | bytes 1179652
  0.7 11.8 %copy-start.17 = (f32[2048]{0:T(1024)S(1)}, f32[2048]{0:T(1024)}, u32[]{:S(2)}) copy-start(f32[2048]{0:T(1024)} %param.30) | copy-start | bytes 24580
  0.7 11.8 %copy-start.16 = (f32[2048]{0:T(1024)S(1)}, f32[2048]{0:T(1024)}, u32[]{:S(2)}) copy-start(f32[2048]{0:T(1024)} %param.29) | copy-start | bytes 24580
  0.7 11.8 %copy-start.15 = (f32[2048]{0:T(1024)S(1)}, f32[2048]{0:T(1024)}, u32[]{:S(2)}) copy-start(f32[2048]{0:T(1024)} %param.28) | copy-start | bytes 24580
  0.7 11.8 %copy-start.14 = (f32[2048]{0:T(1024)S(1)}, f32[2048]{0:T(1024)}, u32[]{:S(2)}) copy-start(f32[2048]{0:T(1024)} %param.27) | copy-start | bytes 24580
  5.7 0.8 copy-start.13
  6.5 0.7 copy-start.18
  12.5 33.2 %copy-start.10 = (f32[88,192]{1,0:T(8,128)S(1)}, f32[88,192]{1,0:T(8,128)}, u32[]{:S(2)}) copy-start(f32[88,192]{1,0:T(8,128)} %load_if_ref.1) | copy-start | bytes 202756
  12.5 33.2 %copy-start.19 = (s32[4,32]{1,0:T(4,128)S(1)}, s32[4,32]{1,0:T(4,128)}, u32[]{:S(2)}) copy-start(s32[4,32]{1,0:T(4,128)} %map_ref.3) | copy-start | bytes 1540
  40.8 0.9 copy-start.2
  45.8 2.3 %copy-start = (bf16[1536,1536]{1,0:T(8,128)(2,1)S(1)}, bf16[1536,1536]{1,0:T(8,128)(2,1)}, u32[]{:S(2)}) copy-start(bf16[1536,1536]{1,0:T(8,128)(2,1)} %kinv_hbm.1) | copy-start | bytes 14155780
  48.1 1.0 %copy-start.1 = (f32[512,192]{1,0:T(8,128)S(1)}, f32[512,192]{1,0:T(8,128)}, u32[]{:S(2)}) copy-start(f32[512,192]{1,0:T(8,128)} %copy.25.load_int_ref) | copy-start | bytes 1179652
  49.1 1.1 %copy-start.3 = (f32[768,192]{1,0:T(8,128)S(1)}, f32[768,192]{1,0:T(8,128)}, u32[]{:S(2)}) copy-start(f32[768,192]{1,0:T(8,128)} %copy-done.2) | copy-start | bytes 1769476
  89.0 0.8 copy-start.4

commit v3 on v2

--- a/solution.py
+++ b/solution.py
@@ -114,7 +114,7 @@
 
 
 def element_kernel(
-    counts_ref, rows_ref, conn_ref, size_ref, stiff_ref, yield_ref, rate_ref, stress_ref,
+    counts_ref, int_ref, tail_ref, conn_ref, size_ref, stiff_ref, yield_ref, rate_ref, stress_ref,
     synth_hi_ref, synth_lo_ref, an_hi_ref, an_lo_ref, strain_ref, force_ref,
     stress_out, force_out,
     nodal, onehot, gathered, stresses, forces, total,
@@ -126,9 +126,11 @@
 
     @pl.when(step == 0)
     def _():
-        rows = rows_ref[...]
-        values = dot_t(synth_hi_ref[...], rows) + dot_t(synth_lo_ref[...], rows)
-        nodal[...] = split_rows(values)
+        inner, tail = int_ref[...], tail_ref[...]
+        first = inner.shape[1]
+        high, low = synth_hi_ref[...], synth_lo_ref[...]
+        nodal[:, :first] = split_rows(dot(high, inner) + dot(low, inner))
+        nodal[:, first:] = split_rows(dot_t(high, tail) + dot_t(low, tail))
         total[...] = jnp.zeros_like(total)
 
     iota = lax.broadcasted_iota(jnp.int16, (nodes, block), 0)
@@ -184,9 +186,10 @@
         )
 
 
-def element_update(rows, conn_t, count, params, stress_zero, block=256):
+def element_update(inner, tail, conn_t, count, params, stress_zero, block=256):
     elems = conn_t.shape[1]
-    padded, width = rows.shape
+    width = inner.shape[0]
+    padded = inner.shape[1] + tail.shape[0]
     synth, analyse, strain, force = host_tables(width // 3)
     synth_hi, synth_lo = two_parts(synth)
     an_hi, an_lo = two_parts(analyse)
@@ -203,7 +206,7 @@
         ),
         in_specs=[
             pl.BlockSpec(memory_space=pltpu.SMEM),
-            whole(rows), by_block(8), by_block(1), by_block(1), by_block(1), by_block(1), by_block(48),
+            whole(inner), whole(tail), by_block(8), by_block(1), by_block(1), by_block(1), by_block(1), by_block(48),
             whole(synth_hi), whole(synth_lo), whole(an_hi), whole(an_lo),
             whole(strain), whole(force),
         ],
@@ -217,10 +220,11 @@
             pltpu.VMEM((padded, 6 * TIMES), F32),
         ],
         compiler_params=pltpu.CompilerParams(
-            vmem_limit_bytes=40 * 1024 * 1024, dimension_semantics=("arbitrary",)
+            vmem_limit_bytes=24 * 1024 * 1024, dimension_semantics=("arbitrary",)
         ),
+        cost_estimate=pl.CostEstimate(flops=25000000000, bytes_accessed=4000000, transcendentals=0),
         name="elements",
-    )(count, rows, conn_t, *params, stress_zero, synth_hi, synth_lo, an_hi, an_lo, strain, force)
+    )(count, inner, tail, conn_t, *params, stress_zero, synth_hi, synth_lo, an_hi, an_lo, strain, force)
 
 
 MESH = pl.DeviceIdType.MESH
@@ -249,16 +253,16 @@
     return copy
 
 
-def halo_kernel(dom, offsets, int_ref, if_ref, map_ref, conn_ref, rows_out, conn_out, out_block, in_block, send_sem, recv_sem):
+def halo_kernel(dom, offsets, int_ref, if_ref, map_ref, tail_out, out_block, in_block, send_sem, recv_sem):
     me = lax.axis_index("dom")
     near = [{"dom": lax.rem(me + off + dom, dom)} for off in offsets]
-    int_nodes, width = int_ref.shape
+    width, int_nodes = int_ref.shape
     if_nodes = if_ref.shape[0]
     slots = map_ref.shape[1]
-    owned = int_nodes + if_nodes
-    local = jnp.concatenate([int_ref[...], if_ref[...]], axis=0)
-    hits = jnp.transpose(pair_hits(map_ref, owned)).astype(BF16)
-    picked = dot(hits, local).astype(BF16)
+    hits = jnp.transpose(pair_hits(map_ref, int_nodes + if_nodes)).astype(BF16)
+    picked = (
+        dot_t(hits[:, :int_nodes], int_ref[...]) + dot(hits[:, int_nodes:], if_ref[...])
+    ).astype(BF16)
     for j in range(len(offsets)):
         out_block[j] = picked[j * slots : (j + 1) * slots]
     greet(near)
@@ -266,28 +270,24 @@
         send(out_block.at[j], in_block.at[j], send_sem.at[j], recv_sem.at[j], near[j])
         for j in range(len(offsets))
     ]
-    conn_out[...] = jnp.transpose(conn_ref[...])
-    rows_out[...] = jnp.zeros_like(rows_out)
-    rows_out[0:owned] = local
-    for j, copy in enumerate(copies):
+    for copy in copies:
         copy.wait()
-        rows_out[owned + j * slots : owned + (j + 1) * slots] = in_block[j]
-
-
-def halo(u_int, u_if, send_map, conn, offsets, dom):
+    parts = [if_ref[...].astype(F32)] + [in_block[j].astype(F32) for j in range(len(offsets))]
+    fill = tail_out.shape[0] - if_nodes - len(offsets) * slots
+    tail_out[...] = jnp.concatenate(parts + [jnp.zeros((fill, width), F32)], axis=0).astype(BF16)
+
+
+def halo(u_int_t, u_if, send_map, offsets, dom):
     neighbours, slots = send_map.shape
-    width = u_int.shape[1]
-    used = u_int.shape[0] + u_if.shape[0] + neighbours * slots
+    width, int_nodes = u_int_t.shape
+    used = int_nodes + u_if.shape[0] + neighbours * slots
     padded = -(-used // 256) * 256
     vmem = pl.BlockSpec(memory_space=pltpu.VMEM)
     return pl.pallas_call(
         functools.partial(halo_kernel, dom, offsets),
-        out_shape=(
-            jax.ShapeDtypeStruct((padded, width), BF16),
-            jax.ShapeDtypeStruct((conn.shape[1], conn.shape[0]), jnp.int32),
-        ),
-        in_specs=[vmem] * 4,
-        out_specs=(vmem, vmem),
+        out_shape=jax.ShapeDtypeStruct((padded - int_nodes, width), BF16),
+        in_specs=[vmem] * 3,
+        out_specs=vmem,
         scratch_shapes=[
             pltpu.VMEM((neighbours, slots, width), BF16),
             pltpu.VMEM((neighbours, slots, width), BF16),
@@ -295,20 +295,21 @@
             pltpu.SemaphoreType.DMA((neighbours,)),
         ],
         compiler_params=pltpu.CompilerParams(
-            collective_id=0, has_side_effects=True, vmem_limit_bytes=24 * 1024 * 1024
+            collective_id=0, has_side_effects=True, vmem_limit_bytes=12 * 1024 * 1024
         ),
+        cost_estimate=pl.CostEstimate(flops=6000000000, bytes_accessed=1000000, transcendentals=0),
         name="halo",
-    )(u_int, u_if, send_map, conn)
+    )(u_int_t, u_if, send_map)
 
 
 def finish_kernel(
-    sizes, offsets,
-    force_ref, map_ref, load_int_ref, load_if_ref, kinv_hbm, sinv_hbm,
+    sizes, offsets, stop,
+    force_ref, map_ref, load_int_ref, load_if_ref, kinv, sinv_t,
     du_int_ref, du_if_ref,
-    kinv, sinv, out_ret, in_ret, spread, spread_if, rhs_int,
+    sinv, out_ret, in_ret, spread, spread_if, rhs_int,
     out_grp, in_grp, out_rhs, all_rhs, flat,
     own1, out1, in1, out2, in2, own3, out3, in3, last,
-    local_sem, ret_sem, grp_sem, rhs_sem, sem1, sem2, sem3,
+    ret_sem, grp_sem, rhs_sem, sem1, sem2, sem3,
 ):
     zs, xs, cores, grps = sizes
     dom = zs * xs * cores
@@ -317,10 +318,6 @@
     core = lax.rem(me, cores)
     x = lax.rem(me // cores, xs)
     z = me // (cores * xs)
-    fetch_kinv = pltpu.make_async_copy(kinv_hbm, kinv, local_sem.at[0])
-    fetch_sinv = pltpu.make_async_copy(sinv_hbm, sinv, local_sem.at[1])
-    fetch_kinv.start()
-    fetch_sinv.start()
     at = lambda zz, xx, cc: {"dom": (zz * xs + xx) * cores + cc}
     owners = [{"dom": lax.rem(me - off + dom, dom)} for off in offsets]
     groups = [{"grp": lax.rem(my_grp + s, grps)} for s in range(1, grps)]
@@ -328,7 +325,7 @@
     along_x = [at(z, lax.rem(x + s, xs), core) for s in range(1, xs)]
     along_z = [at(lax.rem(z + s, zs), x, core) for s in range(1, zs)]
     neighbours, slots = map_ref.shape
-    int_nodes, width = load_int_ref.shape
+    width, int_nodes = load_int_ref.shape
     if_nodes = load_if_ref.shape[0]
     fourier = width // 3
     owned = int_nodes + if_nodes
@@ -340,6 +337,10 @@
         for j in range(neighbours)
     ]
     hits = pair_hits(map_ref, owned).astype(BF16)
+    load_int = jnp.transpose(load_int_ref[...])
+    strip = 384
+    for c in range(sinv.shape[0] // strip):
+        sinv[c * strip : (c + 1) * strip, :] = jnp.transpose(sinv_t[:, c * strip : (c + 1) * strip])
     for copy in copies:
         copy.wait()
     back = jnp.concatenate([in_ret[j] for j in range(neighbours)], axis=0)
@@ -356,11 +357,10 @@
         send(out_grp.at[peer["grp"]], in_grp.at[s], grp_sem.at[0, s], grp_sem.at[1, s], peer)
         for s, peer in enumerate(groups)
     ]
-    r_int = load_int_ref[...] - force[:int_nodes]
+    r_int = load_int - force[:int_nodes]
     for i in range(3):
         spread[pl.ds(i, int_nodes, stride=3), :] = r_int[:, i * fourier : (i + 1) * fourier]
     rhs_int[...] = spread[...].astype(BF16)
-    fetch_kinv.wait()
     chunk = 256
     chunks = kinv.shape[0] // chunk
 
@@ -396,7 +396,6 @@
     empty = jnp.zeros_like(rhs_if)
     left = jnp.concatenate([rhs_if, empty], axis=1).astype(BF16)
     right = jnp.concatenate([empty, rhs_if], axis=1).astype(BF16)
-    fetch_sinv.wait()
     half = zs // 2
     per_owner = sinv.shape[0] // dom
     per_z = per_owner * xs * cores
@@ -417,7 +416,9 @@
         out1[k] = jnp.where(core == 0, by_core[1], by_core[0]).astype(BF16)
     copy = send(out1, in1, sem1.at[0], sem1.at[1], sibling)
     for i in range(3):
-        du_int_ref[:, i * fourier : (i + 1) * fourier] = spread[pl.ds(i, int_nodes, stride=3), :]
+        du_int_ref[i * fourier : (i + 1) * fourier, :] = jnp.transpose(
+            spread[pl.ds(i, int_nodes, stride=3), :]
+        )
     copy.wait()
     for k in range(xs):
         summed = own1[k] + in1[k].astype(F32)
@@ -460,33 +461,32 @@
             ][:, :fourier]
 
 
-def finish(force, send_map, load_int, load_if, kinv_int, sinv, offsets, sizes):
+def finish(force, send_map, load_int_t, load_if, kinv_int, sinv_t, offsets, sizes, stop=99):
     zs, xs, cores, grps = sizes
     neighbours, slots = send_map.shape
-    int_nodes, width = load_int.shape
+    width, int_nodes = load_int_t.shape
+    sinv_rows = sinv_t.shape[1]
     if_nodes = load_if.shape[0]
     fourier = width // 3
     dom = zs * xs * cores
-    per_owner = sinv.shape[0] // dom
+    per_owner = sinv_rows // dom
     up = lambda n, k: -(-n // k) * k
     share = up(-(-if_nodes // grps), 8)
     rows1 = up(per_owner * (zs // 2), 16)
     rows3 = up(per_owner // 2, 16)
     vmem = pl.BlockSpec(memory_space=pltpu.VMEM)
-    far = pl.BlockSpec(memory_space=pl.ANY)
     sems = pltpu.SemaphoreType.DMA
     lanes = 2 * fourier
     return pl.pallas_call(
-        functools.partial(finish_kernel, sizes, offsets),
+        functools.partial(finish_kernel, sizes, offsets, stop),
         out_shape=(
-            jax.ShapeDtypeStruct((int_nodes, width), F32),
+            jax.ShapeDtypeStruct((width, int_nodes), F32),
             jax.ShapeDtypeStruct((per_owner // 3, width), F32),
         ),
-        in_specs=[vmem] * 4 + [far, far],
+        in_specs=[vmem] * 6,
         out_specs=(vmem, vmem),
         scratch_shapes=[
-            pltpu.VMEM(kinv_int.shape, BF16),
-            pltpu.VMEM(sinv.shape, BF16),
+            pltpu.VMEM((sinv_rows, sinv_t.shape[0]), BF16),
             pltpu.VMEM((neighbours, slots, width), F32),
             pltpu.VMEM((neighbours, slots, width), F32),
             pltpu.VMEM((3 * int_nodes, fourier), F32),
@@ -496,7 +496,7 @@
             pltpu.VMEM((grps - 1, share, width), F32),
             pltpu.VMEM((share, width), BF16),
             pltpu.VMEM((grps, share, width), BF16),
-            pltpu.VMEM((sinv.shape[0] // 2, lanes), F32),
+            pltpu.VMEM((sinv_rows // 2, lanes), F32),
             pltpu.VMEM((xs, rows1, lanes), F32),
             pltpu.VMEM((xs, rows1, lanes), BF16),
             pltpu.VMEM((xs, rows1, lanes), BF16),
@@ -506,14 +506,15 @@
             pltpu.VMEM((zs, rows3, lanes), BF16),
             pltpu.VMEM((zs - 1, rows3, lanes), BF16),
             pltpu.VMEM((2, rows3, lanes), F32),
-            sems((2,)), sems((2, neighbours)), sems((2, grps - 1)), sems((2, grps - 1)),
+            sems((2, neighbours)), sems((2, grps - 1)), sems((2, grps - 1)),
             sems((2,)), sems((2, xs - 1)), sems((2, zs - 1)),
         ],
         compiler_params=pltpu.CompilerParams(
-            collective_id=1, has_side_effects=True, vmem_limit_bytes=40 * 1024 * 1024
+            collective_id=1, has_side_effects=True, vmem_limit_bytes=20 * 1024 * 1024
         ),
+        cost_estimate=pl.CostEstimate(flops=20000000000, bytes_accessed=9000000, transcendentals=0),
         name="finish",
-    )(force, send_map, load_int, load_if, kinv_int, sinv)
+    )(force, send_map, load_int_t, load_if, kinv_int, sinv_t)
 
 
 def per_device(
@@ -524,11 +525,14 @@
     offsets = list(range(-reach, 0)) + list(range(1, reach + 1))
     dom, grps = lax.axis_size("dom"), lax.axis_size("grp")
     sizes = (dom // 8, 4, 2, grps)
-    rows, conn_t = halo(u_int, u_if, send_map, conn, offsets, dom)
+    u_int_t, conn_t = jnp.transpose(u_int), jnp.transpose(conn)
+    tail = halo(u_int_t, u_if, send_map, offsets, dom)
     params = [v.reshape(1, -1) for v in (elem_size, stiffness, yield_stress, relax_rate)]
-    stress_end, force = element_update(rows, conn_t, counts, params, stress_init)
-    du_int, du_if = finish(force, send_map, load_int, load_if, kinv_int, sinv, offsets, sizes)
-    return (du_int, du_if, stress_end)
+    stress_end, force = element_update(u_int_t, tail, conn_t, counts, params, stress_init)
+    du_int_t, du_if = finish(
+        force, send_map, jnp.transpose(load_int), load_if, kinv_int, jnp.transpose(sinv), offsets, sizes
+    )
+    return (jnp.transpose(du_int_t), du_if, stress_end)
 
 
 def solution(mesh):

time: 92.9 us -> 77.2 us (0.83)
  local copies, waits for them, and re-layouts: 18.6 us -> 3.85 us
    unnamed x46, local copies, waits for them, and re-layouts: 18.6 us -> 3.85 us
where the time goes in v3:
time: 77.2 us; the launch traced here: 77 us
  Pallas kernels  71.6 us (93%)
  local copies, waits for them, and re-layouts  3.85 us (5%)
  between operations  1.57 us (2%)
    pallas_call x1, Pallas kernels, finish(): pl.pallas_call(functools.partial(finish_kernel, sizes, offsets, stop), ou...  38.2 us
    pallas_call x1, Pallas kernels, element_update(): pl.pallas_call(element_kernel, grid=(elems // block,), out_shape=(jax.Sha...  28.2 us
    pallas_call x1, Pallas kernels, halo(): pl.pallas_call(functools.partial(halo_kernel, dom, offsets), out_shape=ja...  5.2 us
    unnamed x46, local copies, waits for them, and re-layouts  3.85 us

profile of v3, /device:TPU:4, one launch (start us, length us, event | category | flops | bytes accessed | tf_op | source)
XLA Modules:
  0.0 77.0 jit_solution(12971041242931227147)
XLA Ops:
  1.3 0.0 copy-start.3
  1.3 0.9 %copy-done.3 = bf16[512,192]{0,1:T(8,128)(2,1)S(1)} copy-done((bf16[512,192]{0,1:T(8,128)(2,1)S(1)}, bf16[512,192]{0,1:T(8,128)(2,1)}, u32[]{:S(2)}) %copy-start.3) | copy-done | bytes 196632
  2.2 0.8 %copy-done.7 = bf16[88,192]{1,0:T(8,128)(2,1)S(1)} copy-done((bf16[88,192]{1,0:T(8,128)(2,1)S(1)}, bf16[88,192]{1,0:T(8,128)(2,1)}, u32[]{:S(2)}) %copy-start.7) | copy-done | bytes 33816
  3.0 0.7 copy-done.12
  3.7 0.0 copy-start.9
  3.7 0.0 copy-start.10
  3.7 0.0 copy-start.14
  3.7 0.0 copy-start.15
  3.7 0.0 copy-start.16
  3.8 0.0 copy-start.17
  3.8 0.0 copy-start.18
  3.8 0.0 copy-start.19
  3.8 0.0 slice-start
  3.8 5.2 %halo.1.tail_ref = bf16[256,192]{1,0:T(8,128)(2,1)S(1)} custom-call(bf16[192,512]{1,0:T(8,128)(2,1)S(1)} %bitcast.14, bf16[88,192]{1,0:T(8,128)(2,1)S(1)} %copy-done.7, s32[4,32]{1,0:T(4,128)S(1)} %copy-done.12), custom_call_target="tpu_custom_call" | custom-call | flops 6000000000 | bytes 1000000 | tf_op jit(solution)/shard_map/halo/pallas_call | solution.py:286
  9.1 0.0 slice-start.1
  9.2 0.0 copy-start
  9.2 0.0 copy-start.2
  9.2 0.0 copy-start.5
  9.2 0.0 copy-start.13
  9.2 28.2 %elements.1 = (f32[48,2048]{1,0:T(8,128)}, f32[768,192]{1,0:T(8,128)S(1)}) custom-call(s32[1]{0:T(128)S(6)} %copy.25.counts_ref, bf16[192,512]{1,0:T(8,128)(2,1)S(1)} %bitcast.15, bf16[256,192]{1,0:T(8,128)(2,1)S(1)} %halo.1.tail_ref, s32[8,2048]{1,0:T(8,128)S(1)} %bitcast.16, f32[1,2048]{1,0:T(1,128)S(1)} %bitcast.17, f32[1,2048]{1,0:T(1,128)S(1)} %bitcast.18, ...), custom_call_target="tpu_custom_call" | custom-call | flops 24999999488 | bytes 4000000 | tf_op jit(solution)/shard_map/elements/pallas_call | solution.py:200
  37.4 0.0 slice-done.1
  37.5 38.2 %finish.1 = (f32[192,512]{1,0:T(8,128)S(1)}, f32[22,192]{1,0:T(8,128)S(1)}) custom-call(f32[768,192]{1,0:T(8,128)S(1)} %get-tuple-element.7.force_ref, s32[4,32]{1,0:T(4,128)S(1)} %copy-done.13, f32[192,512]{1,0:T(8,128)S(1)} %bitcast.13, f32[88,192]{1,0:T(8,128)S(1)} %copy-done.5, bf16[1536,1536]{1,0:T(8,128)(2,1)S(1)} %bitcast.11, ...), custom_call_target="tpu_custom_call" | custom-call | flops 20000000000 | bytes 9000000 | tf_op jit(solution)/shard_map/finish/pallas_call | solution.py:480
  75.7 0.7 copy.26
  76.4 0.6 copy.27
  (26 shorter events, 0.0 us)
Async XLA Ops:
  1.3 0.9 %copy-start.3 = (bf16[512,192]{0,1:T(8,128)(2,1)S(1)}, bf16[512,192]{0,1:T(8,128)(2,1)}, u32[]{:S(2)}) copy-start(bf16[512,192]{0,1:T(8,128)(2,1)} %param.20) | copy-start | bytes 589828
  2.2 0.8 %copy-start.7 = (bf16[88,192]{1,0:T(8,128)(2,1)S(1)}, bf16[88,192]{1,0:T(8,128)(2,1)}, u32[]{:S(2)}) copy-start(bf16[88,192]{1,0:T(8,128)(2,1)} %if_ref.1) | copy-start | bytes 101380
  3.0 0.7 copy-start.12
  3.7 5.3 %copy-start.1 = (f32[48,2048]{1,0:T(8,128)S(1)}, f32[48,2048]{1,0:T(8,128)}, u32[]{:S(2)}) copy-start(f32[48,2048]{1,0:T(8,128)} %stress_ref.1) | copy-start | bytes 1179652
  3.7 5.4 %copy-start.4 = (bf16[512,192]{0,1:T(8,128)(2,1)S(1)}, bf16[512,192]{0,1:T(8,128)(2,1)}, u32[]{:S(2)}) copy-start(bf16[512,192]{0,1:T(8,128)(2,1)} %param.20) | copy-start | bytes 589828
  3.7 5.4 %copy-start.6 = (s32[2048,8]{0,1:T(8,128)S(1)}, s32[2048,8]{0,1:T(8,128)}, u32[]{:S(2)}) copy-start(s32[2048,8]{0,1:T(8,128)} %param.24) | copy-start | bytes 196612
  3.7 5.4 %copy-start.8 = (f32[2048]{0:T(1024)S(1)}, f32[2048]{0:T(1024)}, u32[]{:S(2)}) copy-start(f32[2048]{0:T(1024)} %param.27) | copy-start | bytes 24580
  3.7 5.4 %copy-start.9 = (f32[2048]{0:T(1024)S(1)}, f32[2048]{0:T(1024)}, u32[]{:S(2)}) copy-start(f32[2048]{0:T(1024)} %param.28) | copy-start | bytes 24580
  3.7 5.4 %copy-start.10 = (f32[2048]{0:T(1024)S(1)}, f32[2048]{0:T(1024)}, u32[]{:S(2)}) copy-start(f32[2048]{0:T(1024)} %param.29) | copy-start | bytes 24580
  3.7 5.4 %copy-start.11 = (f32[2048]{0:T(1024)S(1)}, f32[2048]{0:T(1024)}, u32[]{:S(2)}) copy-start(f32[2048]{0:T(1024)} %param.30) | copy-start | bytes 24580
  3.7 5.4 %copy-start.14 = (bf16[384,384]{1,0:T(8,128)(2,1)S(1)}, bf16[384,384]{1,0:T(8,128)(2,1)}, u32[]{:S(2)}) copy-start(bf16[384,384]{1,0:T(8,128)(2,1)} %constant.16.clone.strain_ref) | copy-start | bytes 884740
  3.7 5.4 %copy-start.15 = (bf16[192,384]{1,0:T(8,128)(2,1)S(1)}, bf16[192,384]{1,0:T(8,128)(2,1)}, u32[]{:S(2)}) copy-start(bf16[192,384]{1,0:T(8,128)(2,1)} %constant.17.clone.force_ref) | copy-start | bytes 442372
  3.7 5.4 %copy-start.16 = (bf16[192,192]{1,0:T(8,128)(2,1)S(1)}, bf16[192,192]{1,0:T(8,128)(2,1)}, u32[]{:S(2)}) copy-start(bf16[192,192]{1,0:T(8,128)(2,1)} %constant.15.clone.an_lo_ref) | copy-start | bytes 221188
  3.8 5.4 %copy-start.17 = (bf16[192,192]{1,0:T(8,128)(2,1)S(1)}, bf16[192,192]{1,0:T(8,128)(2,1)}, u32[]{:S(2)}) copy-start(bf16[192,192]{1,0:T(8,128)(2,1)} %constant.14.clone.an_hi_ref) | copy-start | bytes 221188
  3.8 5.4 %copy-start.18 = (bf16[96,192]{1,0:T(8,128)(2,1)S(1)}, bf16[96,192]{1,0:T(8,128)(2,1)}, u32[]{:S(2)}) copy-start(bf16[96,192]{1,0:T(8,128)(2,1)} %constant.13.clone.synth_lo_ref) | copy-start | bytes 110596
  3.8 5.4 %copy-start.19 = (bf16[96,192]{1,0:T(8,128)(2,1)S(1)}, bf16[96,192]{1,0:T(8,128)(2,1)}, u32[]{:S(2)}) copy-start(bf16[96,192]{1,0:T(8,128)(2,1)} %constant.12.clone.synth_hi_ref) | copy-start | bytes 110596
  3.8 33.6 %slice-start = ((s8[4718592]{0:T(1024)(128)(4,1)}), s8[4194304]{0:T(1024)(128)(4,1)S(1)}, s32[]{:S(2)}) async-start(s8[4718592]{0:T(1024)(128)(4,1)} %bitcast.10), calls=%async_computation | async-start | bytes 8388608
  9.1 28.3 %slice-start.1 = ((s8[4718592]{0:T(1024)(128)(4,1)}), s8[524288]{0:T(1024)(128)(4,1)S(1)}, s32[]{:S(2)}) async-start(s8[4718592]{0:T(1024)(128)(4,1)} %bitcast.10), calls=%async_computation.1 | async-start | bytes 1048576
  9.2 28.3 %copy-start = (bf16[4224,264]{0,1:T(8,128)(2,1)S(1)}, bf16[4224,264]{0,1:T(8,128)(2,1)}, u32[]{:S(2)}) copy-start(bf16[4224,264]{0,1:T(8,128)(2,1)} %param.33) | copy-start | bytes 6690820
  9.2 28.3 %copy-start.2 = (f32[512,192]{0,1:T(8,128)S(1)}, f32[512,192]{0,1:T(8,128)}, u32[]{:S(2)}) copy-start(f32[512,192]{0,1:T(8,128)} %param.22) | copy-start | bytes 1179652
  9.2 28.3 %copy-start.5 = (f32[88,192]{1,0:T(8,128)S(1)}, f32[88,192]{1,0:T(8,128)}, u32[]{:S(2)}) copy-start(f32[88,192]{1,0:T(8,128)} %load_if_ref.1) | copy-start | bytes 202756
  9.2 28.3 %copy-start.13 = (s32[4,32]{1,0:T(4,128)S(1)}, s32[4,32]{1,0:T(4,128)}, u32[]{:S(2)}) copy-start(s32[4,32]{1,0:T(4,128)} %map_ref.3) | copy-start | bytes 1540

commit v4 on v3

--- a/solution.py
+++ b/solution.py
@@ -141,8 +141,9 @@
             hit, jnp.ones((), BF16), jnp.zeros((), BF16)
         )
     table = nodal[...]
+    chosen = dot(table, onehot[...]).astype(BF16)
     for a in range(8):
-        picked = dot(table, onehot[:, a * block : (a + 1) * block]).astype(BF16)
+        picked = chosen[:, a * block : (a + 1) * block]
         for g in range(groups):
             gathered[g, a * 48 : (a + 1) * 48, :] = picked[g * 48 : (g + 1) * 48, :]
 
@@ -159,22 +160,23 @@
     live = (slot < counts_ref[0]).astype(F32)
     scale = size * size * 0.25 * live * yields
     state = [stress_ref[c * 8 : (c + 1) * 8, :] * inverse for c in range(6)]
+    deltas = [dot(strain_ref[...], gathered[g]) for g in range(groups)]
     for g in range(groups):
-        delta = dot(strain_ref[...], gathered[g])
+        delta = deltas[g]
         for m in range(GROUP):
             d = [delta[m * 48 + c * 8 : m * 48 + c * 8 + 8, :] for c in range(6)]
             volume = (d[0] + d[1] + d[2]) * lame8
             for c in range(6):
                 rise = d[c] * shear28 + volume if c < 3 else d[c] * shear8
                 state[c] = state[c] + rise - rate8 * jnp.tanh(state[c])
-            stresses[m * 48 : (m + 1) * 48, :] = jnp.concatenate(state, axis=0).astype(BF16)
-        pushed = dot(force_ref[...], stresses[...]) * scale
+            stresses[g, m * 48 : (m + 1) * 48, :] = jnp.concatenate(state, axis=0).astype(BF16)
+        pushed = dot(force_ref[...], stresses[g]) * scale
         for a in range(8):
             forces[g * 48 : (g + 1) * 48, a * block : (a + 1) * block] = split_rows(
                 pushed[a * 24 : (a + 1) * 24, :]
             )
     stress_out[...] = jnp.concatenate(state, axis=0) * (yields * live)
-    total[...] += dot_t(onehot[...], forces[...])
+    total[...] += dot_t(onehot[0 : total.shape[0], :], forces[...])
 
     @pl.when(step == pl.num_programs(0) - 1)
     def _():
@@ -186,7 +188,7 @@
         )
 
 
-def element_update(inner, tail, conn_t, count, params, stress_zero, block=256):
+def element_update(inner, tail, conn_t, count, params, stress_zero, used=736, block=512):
     elems = conn_t.shape[1]
     width = inner.shape[0]
     padded = inner.shape[1] + tail.shape[0]
@@ -202,7 +204,7 @@
         grid=(elems // block,),
         out_shape=(
             jax.ShapeDtypeStruct(stress_zero.shape, F32),
-            jax.ShapeDtypeStruct((padded, width), F32),
+            jax.ShapeDtypeStruct((used, width), F32),
         ),
         in_specs=[
             pl.BlockSpec(memory_space=pltpu.SMEM),
@@ -210,17 +212,17 @@
             whole(synth_hi), whole(synth_lo), whole(an_hi), whole(an_lo),
             whole(strain), whole(force),
         ],
-        out_specs=(by_block(48), pl.BlockSpec((padded, width), lambda s: (0, 0))),
+        out_specs=(by_block(48), pl.BlockSpec((used, width), lambda s: (0, 0))),
         scratch_shapes=[
             pltpu.VMEM((6 * TIMES, padded), BF16),
             pltpu.VMEM((padded, 8 * block), BF16),
             pltpu.VMEM((TIMES // GROUP, GROUP * 48, block), BF16),
-            pltpu.VMEM((GROUP * 48, block), BF16),
+            pltpu.VMEM((TIMES // GROUP, GROUP * 48, block), BF16),
             pltpu.VMEM((6 * TIMES, 8 * block), BF16),
-            pltpu.VMEM((padded, 6 * TIMES), F32),
+            pltpu.VMEM((used, 6 * TIMES), F32),
         ],
         compiler_params=pltpu.CompilerParams(
-            vmem_limit_bytes=24 * 1024 * 1024, dimension_semantics=("arbitrary",)
+            vmem_limit_bytes=28 * 1024 * 1024, dimension_semantics=("arbitrary",)
         ),
         cost_estimate=pl.CostEstimate(flops=25000000000, bytes_accessed=4000000, transcendentals=0),
         name="elements",
@@ -312,6 +314,12 @@
     ret_sem, grp_sem, rhs_sem, sem1, sem2, sem3,
 ):
     zs, xs, cores, grps = sizes
+    started = []
+
+    def launch(*where):
+        started.append(send(*where))
+        return started[-1]
+
     dom = zs * xs * cores
     me = lax.axis_index("dom")
     my_grp = lax.axis_index("grp")
@@ -333,7 +341,7 @@
         out_ret[j] = force_ref[owned + j * slots : owned + (j + 1) * slots, :]
     greet(owners + groups + [sibling] + along_x + along_z)
     copies = [
-        send(out_ret.at[j], in_ret.at[j], ret_sem.at[0, j], ret_sem.at[1, j], owners[j])
+        launch(out_ret.at[j], in_ret.at[j], ret_sem.at[0, j], ret_sem.at[1, j], owners[j])
         for j in range(neighbours)
     ]
     hits = pair_hits(map_ref, owned).astype(BF16)
@@ -342,7 +350,7 @@
     for c in range(sinv.shape[0] // strip):
         sinv[c * strip : (c + 1) * strip, :] = jnp.transpose(sinv_t[:, c * strip : (c + 1) * strip])
     for copy in copies:
-        copy.wait()
+        copy.wait_recv()
     back = jnp.concatenate([in_ret[j] for j in range(neighbours)], axis=0)
     high = back.astype(BF16)
     low = (back - high.astype(F32)).astype(BF16)
@@ -354,7 +362,7 @@
     for q in range(grps):
         out_grp[q] = pieces[q * share : (q + 1) * share]
     copies = [
-        send(out_grp.at[peer["grp"]], in_grp.at[s], grp_sem.at[0, s], grp_sem.at[1, s], peer)
+        launch(out_grp.at[peer["grp"]], in_grp.at[s], grp_sem.at[0, s], grp_sem.at[1, s], peer)
         for s, peer in enumerate(groups)
     ]
     r_int = load_int - force[:int_nodes]
@@ -369,7 +377,7 @@
         spread[rows, :] = dot(kinv[rows, :], rhs_int[...])
         return 0
 
-    lax.fori_loop(0, chunks // 2, solve, 0)
+    lax.fori_loop(0, 2, solve, 0)
     loads = jnp.concatenate(
         [load_if_ref[...], jnp.zeros((grps * share - if_nodes, width), F32)], axis=0
     )
@@ -378,17 +386,17 @@
         mine = jnp.where(my_grp == q, loads[q * share : (q + 1) * share], mine)
     total = out_grp[my_grp]
     for s, copy in enumerate(copies):
-        copy.wait()
+        copy.wait_recv()
         total = total + in_grp[s]
     out_rhs[...] = (mine - total).astype(BF16)
     copies = [
-        send(out_rhs, all_rhs.at[my_grp], rhs_sem.at[0, s], rhs_sem.at[1, s], peer)
+        launch(out_rhs, all_rhs.at[my_grp], rhs_sem.at[0, s], rhs_sem.at[1, s], peer)
         for s, peer in enumerate(groups)
     ]
     all_rhs[my_grp] = out_rhs[...]
-    lax.fori_loop(chunks // 2, chunks, solve, 0)
+    lax.fori_loop(2, 3, solve, 0)
     for copy in copies:
-        copy.wait()
+        copy.wait_recv()
     gathered = jnp.concatenate([all_rhs[q].astype(F32) for q in range(grps)], axis=0)[:if_nodes]
     for i in range(3):
         spread_if[pl.ds(i, if_nodes, stride=3), :] = gathered[:, i * fourier : (i + 1) * fourier]
@@ -397,59 +405,76 @@
     left = jnp.concatenate([rhs_if, empty], axis=1).astype(BF16)
     right = jnp.concatenate([empty, rhs_if], axis=1).astype(BF16)
     half = zs // 2
+    parts = out1.shape[0]
+    each = half // parts
     per_owner = sinv.shape[0] // dom
     per_z = per_owner * xs * cores
-    for q in range(half):
-        flat[q * per_z : (q + 1) * per_z, :] = dot(
-            sinv[q * per_z : (q + 1) * per_z, :], left
-        ) + dot(sinv[(half + q) * per_z : (half + q + 1) * per_z, :], right)
-    fill = jnp.zeros((out1.shape[1] - half * per_owner, 2 * fourier), F32)
-    for k in range(xs):
-        by_core = []
-        for c in range(cores):
-            rows = [
-                flat[q * per_z + (k * cores + c) * per_owner : q * per_z + (k * cores + c + 1) * per_owner, :]
-                for q in range(half)
-            ]
-            by_core.append(jnp.concatenate(rows + [fill], axis=0))
-        own1[k] = jnp.where(core == 0, by_core[0], by_core[1])
-        out1[k] = jnp.where(core == 0, by_core[1], by_core[0]).astype(BF16)
-    copy = send(out1, in1, sem1.at[0], sem1.at[1], sibling)
+    fill = jnp.zeros((out1.shape[2] - each * per_owner, 2 * fourier), F32)
+    first_copies = []
+    for c in range(parts):
+        for j in range(each):
+            start = pl.multiple_of(lax.rem(z + c * each + j + 1, half) * per_z, 16)
+            other = pl.multiple_of(start + half * per_z, 16)
+            flat[(c * each + j) * per_z : (c * each + j + 1) * per_z, :] = dot(
+                sinv[pl.ds(start, per_z), :], left
+            ) + dot(sinv[pl.ds(other, per_z), :], right)
+        for k in range(xs):
+            by_core = []
+            for cc in range(cores):
+                rows = []
+                for j in range(each):
+                    at_row = (c * each + j) * per_z + (k * cores + cc) * per_owner
+                    rows.append(flat[at_row : at_row + per_owner, :])
+                by_core.append(jnp.concatenate(rows + [fill], axis=0))
+            own1[c, k] = jnp.where(core == 0, by_core[0], by_core[1])
+            out1[c, k] = jnp.where(core == 0, by_core[1], by_core[0]).astype(BF16)
+        first_copies.append(launch(out1.at[c], in1.at[c], sem1.at[0, c], sem1.at[1, c], sibling))
+    second_copies = []
+    for c in range(parts):
+        first_copies[c].wait_recv()
+        for k in range(xs):
+            summed = own1[c, k] + in1[c, k].astype(F32)
+            own1[c, k] = summed
+            out2[c, k] = summed.astype(BF16)
+        second_copies.append([
+            launch(out2.at[c, lax.rem(x + s + 1, xs)], in2.at[c, s], sem2.at[0, c, s], sem2.at[1, c, s], peer)
+            for s, peer in enumerate(along_x)
+        ])
+    lax.fori_loop(3, chunks, solve, 0)
+    short = per_owner // 2
+    first = lax.broadcasted_iota(jnp.int32, (short, 2 * fourier), 1) < fourier
+    fill = jnp.zeros((out3.shape[3] - short, 2 * fourier), F32)
+    third_copies = []
+    for c in range(parts):
+        summed = own1[c, x]
+        for s, copy in enumerate(second_copies[c]):
+            copy.wait_recv()
+            summed = summed + in2[c, s].astype(F32)
+        turned = pltpu.roll(summed, fourier, 1)
+        for j in range(each):
+            top = slice(j * per_owner, j * per_owner + short)
+            low_rows = slice(j * per_owner + short, (j + 1) * per_owner)
+            o = c * each + j + 1
+            for h, (a, b) in enumerate(((summed, turned), (turned, summed))):
+                block = jnp.concatenate([jnp.where(first, a[top], b[low_rows]), fill], axis=0)
+                if o == half:
+                    own3[h] = block
+                out3[c, j, h] = block.astype(BF16)
+            for s in (o, o + half):
+                if s < zs:
+                    target = lax.rem(z + s, zs)
+                    third_copies.append(launch(
+                        out3.at[c, j, target // half], in3.at[s - 1],
+                        sem3.at[0, s - 1], sem3.at[1, s - 1], along_z[s - 1],
+                    ))
     for i in range(3):
         du_int_ref[i * fourier : (i + 1) * fourier, :] = jnp.transpose(
             spread[pl.ds(i, int_nodes, stride=3), :]
         )
-    copy.wait()
-    for k in range(xs):
-        summed = own1[k] + in1[k].astype(F32)
-        own1[k] = summed
-        out2[k] = summed.astype(BF16)
-    copies = [
-        send(out2.at[lax.rem(x + s + 1, xs)], in2.at[s], sem2.at[0, s], sem2.at[1, s], peer)
-        for s, peer in enumerate(along_x)
-    ]
-    summed = own1[x]
-    for s, copy in enumerate(copies):
-        copy.wait()
-        summed = summed + in2[s].astype(F32)
-    turned = pltpu.roll(summed, fourier, 1)
-    short = per_owner // 2
-    first = lax.broadcasted_iota(jnp.int32, (short, 2 * fourier), 1) < fourier
-    fill = jnp.zeros((out3.shape[1] - short, 2 * fourier), F32)
-    for q in range(half):
-        top = slice(q * per_owner, q * per_owner + short)
-        low_rows = slice(q * per_owner + short, (q + 1) * per_owner)
-        for h, (a, b) in enumerate(((summed, turned), (turned, summed))):
-            block = jnp.concatenate([jnp.where(first, a[top], b[low_rows]), fill], axis=0)
-            own3[h * half + q] = block
-            out3[h * half + q] = block.astype(BF16)
-    copies = [
-        send(out3.at[lax.rem(z + s + 1, zs)], in3.at[s], sem3.at[0, s], sem3.at[1, s], peer)
-        for s, peer in enumerate(along_z)
-    ]
-    summed = own3[z]
-    for s, copy in enumerate(copies):
-        copy.wait()
+    for copy in third_copies:
+        copy.wait_recv()
+    summed = own3[z // half]
+    for s in range(zs - 1):
         summed = summed + in3[s].astype(F32)
     last[0] = summed
     last[1] = pltpu.roll(summed, fourier, 1)
@@ -459,6 +484,8 @@
             du_if_ref[h * nodes : (h + 1) * nodes, i * fourier : (i + 1) * fourier] = last[
                 h, pl.ds(i, nodes, stride=3), :
             ][:, :fourier]
+    for copy in started:
+        copy.wait_send()
 
 
 def finish(force, send_map, load_int_t, load_if, kinv_int, sinv_t, offsets, sizes, stop=99):
@@ -472,7 +499,9 @@
     per_owner = sinv_rows // dom
     up = lambda n, k: -(-n // k) * k
     share = up(-(-if_nodes // grps), 8)
-    rows1 = up(per_owner * (zs // 2), 16)
+    parts = 2
+    each = zs // 2 // parts
+    rows1 = up(per_owner * each, 16)
     rows3 = up(per_owner // 2, 16)
     vmem = pl.BlockSpec(memory_space=pltpu.VMEM)
     sems = pltpu.SemaphoreType.DMA
@@ -497,17 +526,17 @@
             pltpu.VMEM((share, width), BF16),
             pltpu.VMEM((grps, share, width), BF16),
             pltpu.VMEM((sinv_rows // 2, lanes), F32),
-            pltpu.VMEM((xs, rows1, lanes), F32),
-            pltpu.VMEM((xs, rows1, lanes), BF16),
-            pltpu.VMEM((xs, rows1, lanes), BF16),
-            pltpu.VMEM((xs, rows1, lanes), BF16),
-            pltpu.VMEM((xs - 1, rows1, lanes), BF16),
-            pltpu.VMEM((zs, rows3, lanes), F32),
-            pltpu.VMEM((zs, rows3, lanes), BF16),
+            pltpu.VMEM((parts, xs, rows1, lanes), F32),
+            pltpu.VMEM((parts, xs, rows1, lanes), BF16),
+            pltpu.VMEM((parts, xs, rows1, lanes), BF16),
+            pltpu.VMEM((parts, xs, rows1, lanes), BF16),
+            pltpu.VMEM((parts, xs - 1, rows1, lanes), BF16),
+            pltpu.VMEM((2, rows3, lanes), F32),
+            pltpu.VMEM((parts, each, 2, rows3, lanes), BF16),
             pltpu.VMEM((zs - 1, rows3, lanes), BF16),
             pltpu.VMEM((2, rows3, lanes), F32),
             sems((2, neighbours)), sems((2, grps - 1)), sems((2, grps - 1)),
-            sems((2,)), sems((2, xs - 1)), sems((2, zs - 1)),
+            sems((2, parts)), sems((2, parts, xs - 1)), sems((2, zs - 1)),
         ],
         compiler_params=pltpu.CompilerParams(
             collective_id=1, has_side_effects=True, vmem_limit_bytes=20 * 1024 * 1024
@@ -528,7 +557,9 @@
     u_int_t, conn_t = jnp.transpose(u_int), jnp.transpose(conn)
     tail = halo(u_int_t, u_if, send_map, offsets, dom)
     params = [v.reshape(1, -1) for v in (elem_size, stiffness, yield_stress, relax_rate)]
-    stress_end, force = element_update(u_int_t, tail, conn_t, counts, params, stress_init)
+    buffer_rows = u_int.shape[0] + u_if.shape[0] + send_map.size
+    used = -(-buffer_rows // 16) * 16
+    stress_end, force = element_update(u_int_t, tail, conn_t, counts, params, stress_init, used)
     du_int_t, du_if = finish(
         force, send_map, jnp.transpose(load_int), load_if, kinv_int, jnp.transpose(sinv), offsets, sizes
     )

time: 77.2 us -> 67.2 us (0.87)
  Pallas kernels: 71.6 us -> 61.5 us
    pallas_call x1, Pallas kernels: 28.2 us -> 19.2 us  [element_update(): pl.pallas_call(element_kernel, grid=(elems // block,), out_shape=(jax.Sha...]
    pallas_call x1, Pallas kernels: 38.2 us -> 37.1 us  [finish(): pl.pallas_call(functools.partial(finish_kernel, sizes, offsets, stop), ou...]
where the time goes in v4:
time: 67.2 us; the launch traced here: 67 us
  Pallas kernels  61.5 us (92%)
  local copies, waits for them, and re-layouts  3.85 us (6%)
  between operations  1.57 us (2%)
    pallas_call x1, Pallas kernels, finish(): pl.pallas_call(functools.partial(finish_kernel, sizes, offsets, stop), ou...  37.1 us
    pallas_call x1, Pallas kernels, element_update(): pl.pallas_call(element_kernel, grid=(elems // block,), out_shape=(jax.Sha...  19.2 us
    pallas_call x1, Pallas kernels, halo(): pl.pallas_call(functools.partial(halo_kernel, dom, offsets), out_shape=ja...  5.2 us
    unnamed x46, local copies, waits for them, and re-layouts  3.85 us

profile of v4, /device:TPU:4, one launch (start us, length us, event | category | flops | bytes accessed | tf_op | source)
XLA Modules:
  0.0 67.0 jit_solution(13490235068801467459)
XLA Ops:
  1.3 0.0 copy-start.3
  1.3 0.9 %copy-done.3 = bf16[512,192]{0,1:T(8,128)(2,1)S(1)} copy-done((bf16[512,192]{0,1:T(8,128)(2,1)S(1)}, bf16[512,192]{0,1:T(8,128)(2,1)}, u32[]{:S(2)}) %copy-start.3) | copy-done | bytes 196632
  2.2 0.8 %copy-done.7 = bf16[88,192]{1,0:T(8,128)(2,1)S(1)} copy-done((bf16[88,192]{1,0:T(8,128)(2,1)S(1)}, bf16[88,192]{1,0:T(8,128)(2,1)}, u32[]{:S(2)}) %copy-start.7) | copy-done | bytes 33816
  3.0 0.7 %copy-done.12 = s32[4,32]{1,0:T(4,128)S(1)} copy-done((s32[4,32]{1,0:T(4,128)S(1)}, s32[4,32]{1,0:T(4,128)}, u32[]{:S(2)}) %copy-start.12) | copy-done | bytes 536
  3.7 0.0 copy-start.9
  3.7 0.0 copy-start.10
  3.7 0.0 copy-start.14
  3.7 0.0 copy-start.15
  3.7 0.0 copy-start.16
  3.8 0.0 copy-start.17
  3.8 0.0 copy-start.18
  3.8 0.0 copy-start.19
  3.8 0.0 slice-start
  3.8 5.2 %halo.1.tail_ref = bf16[256,192]{1,0:T(8,128)(2,1)S(1)} custom-call(bf16[192,512]{1,0:T(8,128)(2,1)S(1)} %bitcast.14, bf16[88,192]{1,0:T(8,128)(2,1)S(1)} %copy-done.7, s32[4,32]{1,0:T(4,128)S(1)} %copy-done.12), custom_call_target="tpu_custom_call" | custom-call | flops 6000000000 | bytes 1000000 | tf_op jit(solution)/shard_map/halo/pallas_call | solution.py:288
  9.1 0.0 slice-start.1
  9.2 0.0 copy-start
  9.2 0.0 copy-start.2
  9.2 0.0 copy-start.5
  9.2 0.0 copy-start.13
  9.2 19.2 %elements.1 = (f32[48,2048]{1,0:T(8,128)}, f32[736,192]{1,0:T(8,128)S(1)}) custom-call(s32[1]{0:T(128)S(6)} %copy.25.counts_ref, bf16[192,512]{1,0:T(8,128)(2,1)S(1)} %bitcast.15, bf16[256,192]{1,0:T(8,128)(2,1)S(1)} %halo.1.tail_ref, s32[8,2048]{1,0:T(8,128)S(1)} %bitcast.16, f32[1,2048]{1,0:T(1,128)S(1)} %bitcast.17, f32[1,2048]{1,0:T(1,128)S(1)} %bitcast.18, ...), custom_call_target="tpu_custom_call" | custom-call | flops 24999999488 | bytes 4000000 | tf_op jit(solution)/shard_map/elements/pallas_call | solution.py:202
  28.4 0.0 slice-done
  28.5 37.1 %finish.1 = (f32[192,512]{1,0:T(8,128)S(1)}, f32[22,192]{1,0:T(8,128)S(1)}) custom-call(f32[736,192]{1,0:T(8,128)S(1)} %get-tuple-element.7.force_ref, s32[4,32]{1,0:T(4,128)S(1)} %copy-done.13, f32[192,512]{1,0:T(8,128)S(1)} %bitcast.13, f32[88,192]{1,0:T(8,128)S(1)} %copy-done.5, bf16[1536,1536]{1,0:T(8,128)(2,1)S(1)} %bitcast.11, ...), custom_call_target="tpu_custom_call" | custom-call | flops 20000000000 | bytes 9000000 | tf_op jit(solution)/shard_map/finish/pallas_call | solution.py:509
  65.6 0.7 %copy.26 = f32[512,192]{0,1:T(8,128)} copy(f32[512,192]{0,1:T(8,128)S(1)} %bitcast.9) | data formatting | bytes 786432
  66.4 0.6 copy.27
  (26 shorter events, 0.0 us)
Async XLA Ops:
  1.3 0.9 %copy-start.3 = (bf16[512,192]{0,1:T(8,128)(2,1)S(1)}, bf16[512,192]{0,1:T(8,128)(2,1)}, u32[]{:S(2)}) copy-start(bf16[512,192]{0,1:T(8,128)(2,1)} %param.20) | copy-start | bytes 589828
  2.2 0.8 %copy-start.7 = (bf16[88,192]{1,0:T(8,128)(2,1)S(1)}, bf16[88,192]{1,0:T(8,128)(2,1)}, u32[]{:S(2)}) copy-start(bf16[88,192]{1,0:T(8,128)(2,1)} %if_ref.1) | copy-start | bytes 101380
  3.0 0.7 %copy-start.12 = (s32[4,32]{1,0:T(4,128)S(1)}, s32[4,32]{1,0:T(4,128)}, u32[]{:S(2)}) copy-start(s32[4,32]{1,0:T(4,128)} %map_ref.3) | copy-start | bytes 1540
  3.7 5.3 %copy-start.1 = (f32[48,2048]{1,0:T(8,128)S(1)}, f32[48,2048]{1,0:T(8,128)}, u32[]{:S(2)}) copy-start(f32[48,2048]{1,0:T(8,128)} %stress_ref.1) | copy-start | bytes 1179652
  3.7 5.4 %copy-start.4 = (bf16[512,192]{0,1:T(8,128)(2,1)S(1)}, bf16[512,192]{0,1:T(8,128)(2,1)}, u32[]{:S(2)}) copy-start(bf16[512,192]{0,1:T(8,128)(2,1)} %param.20) | copy-start | bytes 589828
  3.7 5.4 %copy-start.6 = (s32[2048,8]{0,1:T(8,128)S(1)}, s32[2048,8]{0,1:T(8,128)}, u32[]{:S(2)}) copy-start(s32[2048,8]{0,1:T(8,128)} %param.24) | copy-start | bytes 196612
  3.7 5.4 %copy-start.8 = (f32[2048]{0:T(1024)S(1)}, f32[2048]{0:T(1024)}, u32[]{:S(2)}) copy-start(f32[2048]{0:T(1024)} %param.27) | copy-start | bytes 24580
  3.7 5.4 %copy-start.9 = (f32[2048]{0:T(1024)S(1)}, f32[2048]{0:T(1024)}, u32[]{:S(2)}) copy-start(f32[2048]{0:T(1024)} %param.28) | copy-start | bytes 24580
  3.7 5.4 %copy-start.10 = (f32[2048]{0:T(1024)S(1)}, f32[2048]{0:T(1024)}, u32[]{:S(2)}) copy-start(f32[2048]{0:T(1024)} %param.29) | copy-start | bytes 24580
  3.7 5.4 %copy-start.11 = (f32[2048]{0:T(1024)S(1)}, f32[2048]{0:T(1024)}, u32[]{:S(2)}) copy-start(f32[2048]{0:T(1024)} %param.30) | copy-start | bytes 24580
  3.7 5.4 %copy-start.14 = (bf16[384,384]{1,0:T(8,128)(2,1)S(1)}, bf16[384,384]{1,0:T(8,128)(2,1)}, u32[]{:S(2)}) copy-start(bf16[384,384]{1,0:T(8,128)(2,1)} %constant.16.clone.strain_ref) | copy-start | bytes 884740
  3.7 5.4 %copy-start.15 = (bf16[192,384]{1,0:T(8,128)(2,1)S(1)}, bf16[192,384]{1,0:T(8,128)(2,1)}, u32[]{:S(2)}) copy-start(bf16[192,384]{1,0:T(8,128)(2,1)} %constant.17.clone.force_ref) | copy-start | bytes 442372
  3.7 5.4 %copy-start.16 = (bf16[192,192]{1,0:T(8,128)(2,1)S(1)}, bf16[192,192]{1,0:T(8,128)(2,1)}, u32[]{:S(2)}) copy-start(bf16[192,192]{1,0:T(8,128)(2,1)} %constant.15.clone.an_lo_ref) | copy-start | bytes 221188
  3.8 5.4 %copy-start.17 = (bf16[192,192]{1,0:T(8,128)(2,1)S(1)}, bf16[192,192]{1,0:T(8,128)(2,1)}, u32[]{:S(2)}) copy-start(bf16[192,192]{1,0:T(8,128)(2,1)} %constant.14.clone.an_hi_ref) | copy-start | bytes 221188
  3.8 5.4 %copy-start.18 = (bf16[96,192]{1,0:T(8,128)(2,1)S(1)}, bf16[96,192]{1,0:T(8,128)(2,1)}, u32[]{:S(2)}) copy-start(bf16[96,192]{1,0:T(8,128)(2,1)} %constant.13.clone.synth_lo_ref) | copy-start | bytes 110596
  3.8 5.4 %copy-start.19 = (bf16[96,192]{1,0:T(8,128)(2,1)S(1)}, bf16[96,192]{1,0:T(8,128)(2,1)}, u32[]{:S(2)}) copy-start(bf16[96,192]{1,0:T(8,128)(2,1)} %constant.12.clone.synth_hi_ref) | copy-start | bytes 110596
  3.8 24.7 %slice-start = ((s8[4718592]{0:T(1024)(128)(4,1)}), s8[4194304]{0:T(1024)(128)(4,1)S(1)}, s32[]{:S(2)}) async-start(s8[4718592]{0:T(1024)(128)(4,1)} %bitcast.10), calls=%async_computation | async-start | bytes 8388608
  9.1 19.3 %slice-start.1 = ((s8[4718592]{0:T(1024)(128)(4,1)}), s8[524288]{0:T(1024)(128)(4,1)S(1)}, s32[]{:S(2)}) async-start(s8[4718592]{0:T(1024)(128)(4,1)} %bitcast.10), calls=%async_computation.1 | async-start | bytes 1048576
  9.2 19.3 %copy-start = (bf16[4224,264]{0,1:T(8,128)(2,1)S(1)}, bf16[4224,264]{0,1:T(8,128)(2,1)}, u32[]{:S(2)}) copy-start(bf16[4224,264]{0,1:T(8,128)(2,1)} %param.33) | copy-start | bytes 6690820
  9.2 19.3 %copy-start.2 = (f32[512,192]{0,1:T(8,128)S(1)}, f32[512,192]{0,1:T(8,128)}, u32[]{:S(2)}) copy-start(f32[512,192]{0,1:T(8,128)} %param.22) | copy-start | bytes 1179652
  9.2 19.3 %copy-start.5 = (f32[88,192]{1,0:T(8,128)S(1)}, f32[88,192]{1,0:T(8,128)}, u32[]{:S(2)}) copy-start(f32[88,192]{1,0:T(8,128)} %load_if_ref.1) | copy-start | bytes 202756
  9.2 19.3 %copy-start.13 = (s32[4,32]{1,0:T(4,128)S(1)}, s32[4,32]{1,0:T(4,128)}, u32[]{:S(2)}) copy-start(s32[4,32]{1,0:T(4,128)} %map_ref.3) | copy-start | bytes 1540

commit v5 on v4

--- a/solution.py
+++ b/solution.py
@@ -69,12 +69,12 @@
     groups = TIMES // GROUP
     steps = synthesis - np.roll(synthesis, 1, axis=1)
     synth = np.zeros((groups, 3, GROUP, 3, fourier))
-    analyse = np.zeros((groups, 3, 2, GROUP, 3, fourier))
+    analyse = np.zeros((groups, 3, GROUP, 3, fourier))
     for g in range(groups):
         for i in range(3):
             for m in range(GROUP):
                 synth[g, i, m, i] = steps[:, g * GROUP + m]
-                analyse[g, i, :, m, i] = analysis[g * GROUP + m]
+                analyse[g, i, m, i] = analysis[g * GROUP + m]
     strain = np.zeros((GROUP, 48, 8, 3, 2, GROUP))
     force = np.zeros((8, 3, GROUP, GROUP, 48))
     shaped = table.reshape(48, 8, 3)
@@ -85,7 +85,7 @@
     width = 3 * fourier
     return (
         synth.reshape(TIMES * 3, width),
-        analyse.reshape(TIMES * 6, width),
+        analyse.reshape(TIMES * 3, width),
         strain.reshape(GROUP * 48, GROUP * 48),
         force.reshape(GROUP * 24, GROUP * 48),
     )
@@ -115,9 +115,9 @@
 
 def element_kernel(
     counts_ref, int_ref, tail_ref, conn_ref, size_ref, stiff_ref, yield_ref, rate_ref, stress_ref,
-    synth_hi_ref, synth_lo_ref, an_hi_ref, an_lo_ref, strain_ref, force_ref,
-    stress_out, force_out,
-    nodal, onehot, gathered, stresses, forces, total,
+    synth_hi_ref, synth_lo_ref, strain_ref, force_ref,
+    stress_out, total,
+    nodal, onehot, folded, gathered, stresses, forces,
 ):
     step = pl.program_id(0)
     block = conn_ref.shape[1]
@@ -133,6 +133,10 @@
         nodal[:, first:] = split_rows(dot_t(high, tail) + dot_t(low, tail))
         total[...] = jnp.zeros_like(total)
 
+    fold = total.shape[1]
+    pages = total.shape[0] // (3 * TIMES)
+    listed = jnp.transpose(conn_ref[...])
+    lane = lax.broadcasted_iota(jnp.int32, (block, fold), 1)
     iota = lax.broadcasted_iota(jnp.int16, (nodes, block), 0)
     for a in range(8):
         index = conn_ref[a : a + 1, :].astype(jnp.int16)
@@ -140,10 +144,11 @@
         onehot[:, a * block : (a + 1) * block] = jnp.where(
             hit, jnp.ones((), BF16), jnp.zeros((), BF16)
         )
+        place = jnp.broadcast_to((listed[:, a : a + 1] & (fold - 1)), (block, fold))
+        folded[a * block : (a + 1) * block, :] = (place == lane).astype(F32).astype(BF16)
     table = nodal[...]
-    chosen = dot(table, onehot[...]).astype(BF16)
     for a in range(8):
-        picked = chosen[:, a * block : (a + 1) * block]
+        picked = dot(table, onehot[:, a * block : (a + 1) * block]).astype(BF16)
         for g in range(groups):
             gathered[g, a * 48 : (a + 1) * 48, :] = picked[g * 48 : (g + 1) * 48, :]
 
@@ -171,30 +176,38 @@
                 state[c] = state[c] + rise - rate8 * jnp.tanh(state[c])
             stresses[g, m * 48 : (m + 1) * 48, :] = jnp.concatenate(state, axis=0).astype(BF16)
         pushed = dot(force_ref[...], stresses[g]) * scale
+        if g % 2 == 0:
+            before = pushed
+            continue
         for a in range(8):
-            forces[g * 48 : (g + 1) * 48, a * block : (a + 1) * block] = split_rows(
-                pushed[a * 24 : (a + 1) * 24, :]
-            )
+            rows = slice(a * 24, (a + 1) * 24)
+            both = jnp.concatenate([before[rows, :], pushed[rows, :]], axis=0)
+            page = lax.shift_right_logical(conn_ref[a : a + 1, :], 8)
+            for t in range(pages):
+                at_row = t * 3 * TIMES + (g - 1) * 24
+                forces[at_row : at_row + 48, a * block : (a + 1) * block] = jnp.where(
+                    page == t, both, 0.0
+                ).astype(BF16)
     stress_out[...] = jnp.concatenate(state, axis=0) * (yields * live)
-    total[...] += dot_t(onehot[0 : total.shape[0], :], forces[...])
-
-    @pl.when(step == pl.num_programs(0) - 1)
-    def _():
-        summed = total[...]
-        high = summed.astype(BF16)
-        low = (summed - high.astype(F32)).astype(BF16)
-        force_out[...] = (
-            dot(high, an_hi_ref[...]) + dot(high, an_lo_ref[...]) + dot(low, an_hi_ref[...])
-        )
-
-
-def element_update(inner, tail, conn_t, count, params, stress_zero, used=736, block=512):
+    rows = total.shape[0] // 2
+    for half in (slice(0, rows), slice(rows, 2 * rows)):
+        total[half, :] += dot(forces[half, :], folded[...])
+
+
+def node_forces(total_ref, an_hi_ref, an_lo_ref, page):
+    rows = 3 * TIMES
+    total = jnp.transpose(total_ref[page * rows : (page + 1) * rows, :])
+    high = total.astype(BF16)
+    low = (total - high.astype(F32)).astype(BF16)
+    return dot(high, an_hi_ref[...]) + dot(high, an_lo_ref[...]) + dot(low, an_hi_ref[...])
+
+
+def element_update(inner, tail, conn_t, count, params, stress_zero, fold=256, block=512):
     elems = conn_t.shape[1]
     width = inner.shape[0]
     padded = inner.shape[1] + tail.shape[0]
-    synth, analyse, strain, force = host_tables(width // 3)
+    synth, _, strain, force = host_tables(width // 3)
     synth_hi, synth_lo = two_parts(synth)
-    an_hi, an_lo = two_parts(analyse)
     strain = jnp.asarray(strain, BF16)
     force = jnp.asarray(force, BF16)
     whole = lambda x: pl.BlockSpec(x.shape, lambda s: (0,) * x.ndim)
@@ -204,29 +217,29 @@
         grid=(elems // block,),
         out_shape=(
             jax.ShapeDtypeStruct(stress_zero.shape, F32),
-            jax.ShapeDtypeStruct((used, width), F32),
+            jax.ShapeDtypeStruct((padded // fold * 3 * TIMES, fold), F32),
         ),
         in_specs=[
             pl.BlockSpec(memory_space=pltpu.SMEM),
             whole(inner), whole(tail), by_block(8), by_block(1), by_block(1), by_block(1), by_block(1), by_block(48),
-            whole(synth_hi), whole(synth_lo), whole(an_hi), whole(an_lo),
+            whole(synth_hi), whole(synth_lo),
             whole(strain), whole(force),
         ],
-        out_specs=(by_block(48), pl.BlockSpec((used, width), lambda s: (0, 0))),
+        out_specs=(by_block(48), pl.BlockSpec((padded // fold * 3 * TIMES, fold), lambda s: (0, 0))),
         scratch_shapes=[
             pltpu.VMEM((6 * TIMES, padded), BF16),
             pltpu.VMEM((padded, 8 * block), BF16),
+            pltpu.VMEM((8 * block, fold), BF16),
             pltpu.VMEM((TIMES // GROUP, GROUP * 48, block), BF16),
             pltpu.VMEM((TIMES // GROUP, GROUP * 48, block), BF16),
-            pltpu.VMEM((6 * TIMES, 8 * block), BF16),
-            pltpu.VMEM((used, 6 * TIMES), F32),
+            pltpu.VMEM((padded // fold * 3 * TIMES, 8 * block), BF16),
         ],
         compiler_params=pltpu.CompilerParams(
             vmem_limit_bytes=28 * 1024 * 1024, dimension_semantics=("arbitrary",)
         ),
         cost_estimate=pl.CostEstimate(flops=25000000000, bytes_accessed=4000000, transcendentals=0),
         name="elements",
-    )(count, inner, tail, conn_t, *params, stress_zero, synth_hi, synth_lo, an_hi, an_lo, strain, force)
+    )(count, inner, tail, conn_t, *params, stress_zero, synth_hi, synth_lo, strain, force)
 
 
 MESH = pl.DeviceIdType.MESH
@@ -239,13 +252,6 @@
     return (iota == listed).astype(F32)
 
 
-def greet(peers):
-    barrier = pltpu.get_barrier_semaphore()
-    for peer in peers:
-        pl.semaphore_signal(barrier, inc=1, device_id=peer, device_id_type=MESH)
-    pl.semaphore_wait(barrier, len(peers))
-
-
 def send(src, dst, send_sem, recv_sem, peer):
     copy = pltpu.make_async_remote_copy(
         src_ref=src, dst_ref=dst, send_sem=send_sem, recv_sem=recv_sem,
@@ -258,6 +264,9 @@
 def halo_kernel(dom, offsets, int_ref, if_ref, map_ref, tail_out, out_block, in_block, send_sem, recv_sem):
     me = lax.axis_index("dom")
     near = [{"dom": lax.rem(me + off + dom, dom)} for off in offsets]
+    barrier = pltpu.get_barrier_semaphore()
+    for peer in near:
+        pl.semaphore_signal(barrier, inc=1, device_id=peer, device_id_type=MESH)
     width, int_nodes = int_ref.shape
     if_nodes = if_ref.shape[0]
     slots = map_ref.shape[1]
@@ -267,7 +276,7 @@
     ).astype(BF16)
     for j in range(len(offsets)):
         out_block[j] = picked[j * slots : (j + 1) * slots]
-    greet(near)
+    pl.semaphore_wait(barrier, len(near))
     copies = [
         send(out_block.at[j], in_block.at[j], send_sem.at[j], recv_sem.at[j], near[j])
         for j in range(len(offsets))
@@ -306,7 +315,7 @@
 
 def finish_kernel(
     sizes, offsets, stop,
-    force_ref, map_ref, load_int_ref, load_if_ref, kinv, sinv_t,
+    total_ref, an_hi_ref, an_lo_ref, map_ref, load_int_ref, load_if_ref, kinv, sinv_t,
     du_int_ref, du_if_ref,
     sinv, out_ret, in_ret, spread, spread_if, rhs_int,
     out_grp, in_grp, out_rhs, all_rhs, flat,
@@ -337,14 +346,26 @@
     if_nodes = load_if_ref.shape[0]
     fourier = width // 3
     owned = int_nodes + if_nodes
+    peers = owners + groups + [sibling] + along_x + along_z
+    barrier = pltpu.get_barrier_semaphore()
+    for peer in peers:
+        pl.semaphore_signal(barrier, inc=1, device_id=peer, device_id_type=MESH)
+    fold = total_ref.shape[1]
+    inner = int_nodes // fold
+    outer = node_forces(total_ref, an_hi_ref, an_lo_ref, inner)
     for j in range(neighbours):
-        out_ret[j] = force_ref[owned + j * slots : owned + (j + 1) * slots, :]
-    greet(owners + groups + [sibling] + along_x + along_z)
+        out_ret[j] = outer[if_nodes + j * slots : if_nodes + (j + 1) * slots]
+    pl.semaphore_wait(barrier, len(peers))
     copies = [
         launch(out_ret.at[j], in_ret.at[j], ret_sem.at[0, j], ret_sem.at[1, j], owners[j])
         for j in range(neighbours)
     ]
     hits = pair_hits(map_ref, owned).astype(BF16)
+    own = jnp.concatenate(
+        [node_forces(total_ref, an_hi_ref, an_lo_ref, page) for page in range(inner)]
+        + [outer[:if_nodes]],
+        axis=0,
+    )
     load_int = jnp.transpose(load_int_ref[...])
     strip = 384
     for c in range(sinv.shape[0] // strip):
@@ -354,7 +375,7 @@
     back = jnp.concatenate([in_ret[j] for j in range(neighbours)], axis=0)
     high = back.astype(BF16)
     low = (back - high.astype(F32)).astype(BF16)
-    force = force_ref[0:owned, :] + dot(hits, high) + dot(hits, low)
+    force = own + dot(hits, high) + dot(hits, low)
     share = out_grp.shape[1]
     pieces = jnp.concatenate(
         [force[int_nodes:], jnp.zeros((grps * share - if_nodes, width), F32)], axis=0
@@ -488,7 +509,7 @@
         copy.wait_send()
 
 
-def finish(force, send_map, load_int_t, load_if, kinv_int, sinv_t, offsets, sizes, stop=99):
+def finish(total, send_map, load_int_t, load_if, kinv_int, sinv_t, offsets, sizes, stop=99):
     zs, xs, cores, grps = sizes
     neighbours, slots = send_map.shape
     width, int_nodes = load_int_t.shape
@@ -506,13 +527,14 @@
     vmem = pl.BlockSpec(memory_space=pltpu.VMEM)
     sems = pltpu.SemaphoreType.DMA
     lanes = 2 * fourier
+    an_hi, an_lo = two_parts(host_tables(fourier)[1])
     return pl.pallas_call(
         functools.partial(finish_kernel, sizes, offsets, stop),
         out_shape=(
             jax.ShapeDtypeStruct((width, int_nodes), F32),
             jax.ShapeDtypeStruct((per_owner // 3, width), F32),
         ),
-        in_specs=[vmem] * 6,
+        in_specs=[vmem] * 8,
         out_specs=(vmem, vmem),
         scratch_shapes=[
             pltpu.VMEM((sinv_rows, sinv_t.shape[0]), BF16),
@@ -543,7 +565,7 @@
         ),
         cost_estimate=pl.CostEstimate(flops=20000000000, bytes_accessed=9000000, transcendentals=0),
         name="finish",
-    )(force, send_map, load_int_t, load_if, kinv_int, sinv_t)
+    )(total, an_hi, an_lo, send_map, load_int_t, load_if, kinv_int, sinv_t)
 
 
 def per_device(
@@ -557,9 +579,7 @@
     u_int_t, conn_t = jnp.transpose(u_int), jnp.transpose(conn)
     tail = halo(u_int_t, u_if, send_map, offsets, dom)
     params = [v.reshape(1, -1) for v in (elem_size, stiffness, yield_stress, relax_rate)]
-    buffer_rows = u_int.shape[0] + u_if.shape[0] + send_map.size
-    used = -(-buffer_rows // 16) * 16
-    stress_end, force = element_update(u_int_t, tail, conn_t, counts, params, stress_init, used)
+    stress_end, force = element_update(u_int_t, tail, conn_t, counts, params, stress_init)
     du_int_t, du_if = finish(
         force, send_map, jnp.transpose(load_int), load_if, kinv_int, jnp.transpose(sinv), offsets, sizes
     )

time: 67.2 us -> 62.5 us (0.930)
  Pallas kernels: 61.5 us -> 56.9 us
    pallas_call x1, Pallas kernels: 19.2 us -> 14.7 us  [element_update(): pl.pallas_call(element_kernel, grid=(elems // block,), out_shape=(jax.Sha...]
where the time goes in v5:
time: 62.5 us; the launch traced here: 62.3 us
  Pallas kernels  56.9 us (91%)
  local copies, waits for them, and re-layouts  3.85 us (6%)
  between operations  1.59 us (3%)
    pallas_call x1, Pallas kernels, finish(): pl.pallas_call(functools.partial(finish_kernel, sizes, offsets, stop), ou...  37.2 us
    pallas_call x1, Pallas kernels, element_update(): pl.pallas_call(element_kernel, grid=(elems // block,), out_shape=(jax.Sha...  14.7 us
    pallas_call x1, Pallas kernels, halo(): pl.pallas_call(functools.partial(halo_kernel, dom, offsets), out_shape=ja...  4.99 us
    unnamed x46, local copies, waits for them, and re-layouts  3.85 us

profile of v5, /device:TPU:4, one launch (start us, length us, event | category | flops | bytes accessed | tf_op | source)
XLA Modules:
  0.0 62.3 jit_solution(3457916608831416064)
XLA Ops:
  1.3 0.0 copy-start.3
  1.3 0.9 %copy-done.3 = bf16[512,192]{0,1:T(8,128)(2,1)S(1)} copy-done((bf16[512,192]{0,1:T(8,128)(2,1)S(1)}, bf16[512,192]{0,1:T(8,128)(2,1)}, u32[]{:S(2)}) %copy-start.3) | copy-done | bytes 196632
  2.2 0.8 %copy-done.7 = bf16[88,192]{1,0:T(8,128)(2,1)S(1)} copy-done((bf16[88,192]{1,0:T(8,128)(2,1)S(1)}, bf16[88,192]{1,0:T(8,128)(2,1)}, u32[]{:S(2)}) %copy-start.7) | copy-done | bytes 33816
  3.0 0.7 %copy-done.12 = s32[4,32]{1,0:T(4,128)S(1)} copy-done((s32[4,32]{1,0:T(4,128)S(1)}, s32[4,32]{1,0:T(4,128)}, u32[]{:S(2)}) %copy-start.12) | copy-done | bytes 536
  3.7 0.0 copy-start.9
  3.7 0.0 copy-start.10
  3.7 0.0 copy-start.11
  3.7 0.0 copy-start.14
  3.7 0.0 copy-start.15
  3.7 0.0 copy-start.18
  3.8 0.0 copy-start.19
  3.8 0.0 slice-start
  3.8 5.0 %halo.1.tail_ref = bf16[256,192]{1,0:T(8,128)(2,1)S(1)} custom-call(bf16[192,512]{1,0:T(8,128)(2,1)S(1)} %bitcast.14, bf16[88,192]{1,0:T(8,128)(2,1)S(1)} %copy-done.7, s32[4,32]{1,0:T(4,128)S(1)} %copy-done.12), custom_call_target="tpu_custom_call" | custom-call | flops 6000000000 | bytes 1000000 | tf_op jit(solution)/shard_map/halo/pallas_call | solution.py:297
  8.9 0.0 slice-start.1
  8.9 0.0 copy-start
  8.9 0.0 copy-start.2
  8.9 0.0 copy-start.5
  8.9 0.0 copy-start.13
  9.0 0.0 copy-start.16
  9.0 0.0 copy-start.17
  9.0 14.7 %elements.1 = (f32[48,2048]{1,0:T(8,128)}, f32[288,256]{1,0:T(8,128)S(1)}) custom-call(s32[1]{0:T(128)S(6)} %copy.25.counts_ref, bf16[192,512]{1,0:T(8,128)(2,1)S(1)} %bitcast.15, bf16[256,192]{1,0:T(8,128)(2,1)S(1)} %halo.1.tail_ref, s32[8,2048]{1,0:T(8,128)S(1)} %bitcast.16, f32[1,2048]{1,0:T(1,128)S(1)} %bitcast.17, f32[1,2048]{1,0:T(1,128)S(1)} %bitcast.18, ...), custom_call_target="tpu_custom_call" | custom-call | flops 24999999488 | bytes 4000000 | tf_op jit(solution)/shard_map/elements/pallas_call | solution.py:215
  23.8 37.2 %finish.1 = (f32[192,512]{1,0:T(8,128)S(1)}, f32[22,192]{1,0:T(8,128)S(1)}) custom-call(f32[288,256]{1,0:T(8,128)S(1)} %get-tuple-element.7.total_ref, bf16[96,192]{1,0:T(8,128)(2,1)S(1)} %copy-done.17, bf16[96,192]{1,0:T(8,128)(2,1)S(1)} %copy-done.16, s32[4,32]{1,0:T(4,128)S(1)} %copy-done.13, f32[192,512]{1,0:T(8,128)S(1)} %bitcast.13, ...), custom_call_target="tpu_custom_call" | custom-call | flops 20000000000 | bytes 9000000 | tf_op jit(solution)/shard_map/finish/pallas_call | solution.py:531
  61.0 0.7 %copy.26 = f32[512,192]{0,1:T(8,128)} copy(f32[512,192]{0,1:T(8,128)S(1)} %bitcast.9) | data formatting | bytes 786432
  61.7 0.6 copy.27
  (26 shorter events, 0.0 us)
Async XLA Ops:
  1.3 0.9 %copy-start.3 = (bf16[512,192]{0,1:T(8,128)(2,1)S(1)}, bf16[512,192]{0,1:T(8,128)(2,1)}, u32[]{:S(2)}) copy-start(bf16[512,192]{0,1:T(8,128)(2,1)} %param.20) | copy-start | bytes 589828
  2.2 0.8 %copy-start.7 = (bf16[88,192]{1,0:T(8,128)(2,1)S(1)}, bf16[88,192]{1,0:T(8,128)(2,1)}, u32[]{:S(2)}) copy-start(bf16[88,192]{1,0:T(8,128)(2,1)} %if_ref.1) | copy-start | bytes 101380
  3.0 0.7 %copy-start.12 = (s32[4,32]{1,0:T(4,128)S(1)}, s32[4,32]{1,0:T(4,128)}, u32[]{:S(2)}) copy-start(s32[4,32]{1,0:T(4,128)} %map_ref.3) | copy-start | bytes 1540
  3.7 5.1 %copy-start.1 = (f32[48,2048]{1,0:T(8,128)S(1)}, f32[48,2048]{1,0:T(8,128)}, u32[]{:S(2)}) copy-start(f32[48,2048]{1,0:T(8,128)} %stress_ref.1) | copy-start | bytes 1179652
  3.7 5.1 %copy-start.4 = (bf16[512,192]{0,1:T(8,128)(2,1)S(1)}, bf16[512,192]{0,1:T(8,128)(2,1)}, u32[]{:S(2)}) copy-start(bf16[512,192]{0,1:T(8,128)(2,1)} %param.20) | copy-start | bytes 589828
  3.7 5.1 %copy-start.6 = (s32[2048,8]{0,1:T(8,128)S(1)}, s32[2048,8]{0,1:T(8,128)}, u32[]{:S(2)}) copy-start(s32[2048,8]{0,1:T(8,128)} %param.24) | copy-start | bytes 196612
  3.7 5.1 %copy-start.8 = (f32[2048]{0:T(1024)S(1)}, f32[2048]{0:T(1024)}, u32[]{:S(2)}) copy-start(f32[2048]{0:T(1024)} %param.27) | copy-start | bytes 24580
  3.7 5.1 %copy-start.9 = (f32[2048]{0:T(1024)S(1)}, f32[2048]{0:T(1024)}, u32[]{:S(2)}) copy-start(f32[2048]{0:T(1024)} %param.28) | copy-start | bytes 24580
  3.7 5.1 %copy-start.10 = (f32[2048]{0:T(1024)S(1)}, f32[2048]{0:T(1024)}, u32[]{:S(2)}) copy-start(f32[2048]{0:T(1024)} %param.29) | copy-start | bytes 24580
  3.7 5.1 %copy-start.11 = (f32[2048]{0:T(1024)S(1)}, f32[2048]{0:T(1024)}, u32[]{:S(2)}) copy-start(f32[2048]{0:T(1024)} %param.30) | copy-start | bytes 24580
  3.7 5.1 %copy-start.14 = (bf16[384,384]{1,0:T(8,128)(2,1)S(1)}, bf16[384,384]{1,0:T(8,128)(2,1)}, u32[]{:S(2)}) copy-start(bf16[384,384]{1,0:T(8,128)(2,1)} %constant.14.clone.strain_ref) | copy-start | bytes 884740
  3.7 5.1 %copy-start.15 = (bf16[192,384]{1,0:T(8,128)(2,1)S(1)}, bf16[192,384]{1,0:T(8,128)(2,1)}, u32[]{:S(2)}) copy-start(bf16[192,384]{1,0:T(8,128)(2,1)} %constant.15.clone.force_ref) | copy-start | bytes 442372
  3.7 5.1 %copy-start.18 = (bf16[96,192]{1,0:T(8,128)(2,1)S(1)}, bf16[96,192]{1,0:T(8,128)(2,1)}, u32[]{:S(2)}) copy-start(bf16[96,192]{1,0:T(8,128)(2,1)} %constant.13.clone.synth_lo_ref) | copy-start | bytes 110596
  3.8 5.1 %copy-start.19 = (bf16[96,192]{1,0:T(8,128)(2,1)S(1)}, bf16[96,192]{1,0:T(8,128)(2,1)}, u32[]{:S(2)}) copy-start(bf16[96,192]{1,0:T(8,128)(2,1)} %constant.12.clone.synth_hi_ref) | copy-start | bytes 110596
  3.8 19.9 %slice-start = ((s8[4718592]{0:T(1024)(128)(4,1)}), s8[4194304]{0:T(1024)(128)(4,1)S(1)}, s32[]{:S(2)}) async-start(s8[4718592]{0:T(1024)(128)(4,1)} %bitcast.10), calls=%async_computation | async-start | bytes 8388608
  8.9 14.8 %slice-start.1 = ((s8[4718592]{0:T(1024)(128)(4,1)}), s8[524288]{0:T(1024)(128)(4,1)S(1)}, s32[]{:S(2)}) async-start(s8[4718592]{0:T(1024)(128)(4,1)} %bitcast.10), calls=%async_computation.1 | async-start | bytes 1048576
  8.9 14.8 %copy-start = (bf16[4224,264]{0,1:T(8,128)(2,1)S(1)}, bf16[4224,264]{0,1:T(8,128)(2,1)}, u32[]{:S(2)}) copy-start(bf16[4224,264]{0,1:T(8,128)(2,1)} %param.33) | copy-start | bytes 6690820
  8.9 14.8 %copy-start.2 = (f32[512,192]{0,1:T(8,128)S(1)}, f32[512,192]{0,1:T(8,128)}, u32[]{:S(2)}) copy-start(f32[512,192]{0,1:T(8,128)} %param.22) | copy-start | bytes 1179652
  8.9 14.8 %copy-start.5 = (f32[88,192]{1,0:T(8,128)S(1)}, f32[88,192]{1,0:T(8,128)}, u32[]{:S(2)}) copy-start(f32[88,192]{1,0:T(8,128)} %load_if_ref.1) | copy-start | bytes 202756
  8.9 14.8 %copy-start.13 = (s32[4,32]{1,0:T(4,128)S(1)}, s32[4,32]{1,0:T(4,128)}, u32[]{:S(2)}) copy-start(s32[4,32]{1,0:T(4,128)} %map_ref.3) | copy-start | bytes 1540
  9.0 14.8 %copy-start.16 = (bf16[96,192]{1,0:T(8,128)(2,1)S(1)}, bf16[96,192]{1,0:T(8,128)(2,1)}, u32[]{:S(2)}) copy-start(bf16[96,192]{1,0:T(8,128)(2,1)} %constant.17.clone.an_lo_ref) | copy-start | bytes 110596
  9.0 14.8 %copy-start.17 = (bf16[96,192]{1,0:T(8,128)(2,1)S(1)}, bf16[96,192]{1,0:T(8,128)(2,1)}, u32[]{:S(2)}) copy-start(bf16[96,192]{1,0:T(8,128)(2,1)} %constant.16.clone.an_hi_ref) | copy-start | bytes 110596

commit v6 on v5

--- a/solution.py
+++ b/solution.py
@@ -261,16 +261,25 @@
     return copy
 
 
-def halo_kernel(dom, offsets, int_ref, if_ref, map_ref, tail_out, out_block, in_block, send_sem, recv_sem):
+def halo_kernel(dom, offsets, int_far, if_far, map_far, tail_out, int_ref, if_ref, map_ref, out_block, in_block, fetch_sem, send_sem, recv_sem):
     me = lax.axis_index("dom")
     near = [{"dom": lax.rem(me + off + dom, dom)} for off in offsets]
+    fetches = [
+        pltpu.make_async_copy(src, dst, fetch_sem.at[n])
+        for n, (src, dst) in enumerate(((map_far, map_ref), (if_far, if_ref), (int_far, int_ref)))
+    ]
+    for fetch in fetches:
+        fetch.start()
     barrier = pltpu.get_barrier_semaphore()
     for peer in near:
         pl.semaphore_signal(barrier, inc=1, device_id=peer, device_id_type=MESH)
     width, int_nodes = int_ref.shape
     if_nodes = if_ref.shape[0]
     slots = map_ref.shape[1]
+    fetches[0].wait()
     hits = jnp.transpose(pair_hits(map_ref, int_nodes + if_nodes)).astype(BF16)
+    fetches[1].wait()
+    fetches[2].wait()
     picked = (
         dot_t(hits[:, :int_nodes], int_ref[...]) + dot(hits[:, int_nodes:], if_ref[...])
     ).astype(BF16)
@@ -297,16 +306,20 @@
     return pl.pallas_call(
         functools.partial(halo_kernel, dom, offsets),
         out_shape=jax.ShapeDtypeStruct((padded - int_nodes, width), BF16),
-        in_specs=[vmem] * 3,
+        in_specs=[pl.BlockSpec(memory_space=pltpu.HBM)] * 3,
         out_specs=vmem,
         scratch_shapes=[
+            pltpu.VMEM(u_int_t.shape, BF16),
+            pltpu.VMEM(u_if.shape, BF16),
+            pltpu.VMEM(send_map.shape, jnp.int32),
             pltpu.VMEM((neighbours, slots, width), BF16),
             pltpu.VMEM((neighbours, slots, width), BF16),
+            pltpu.SemaphoreType.DMA((3,)),
             pltpu.SemaphoreType.DMA((neighbours,)),
             pltpu.SemaphoreType.DMA((neighbours,)),
         ],
         compiler_params=pltpu.CompilerParams(
-            collective_id=0, has_side_effects=True, vmem_limit_bytes=12 * 1024 * 1024
+            collective_id=0, has_side_effects=True, vmem_limit_bytes=56 * 1024 * 1024
         ),
         cost_estimate=pl.CostEstimate(flops=6000000000, bytes_accessed=1000000, transcendentals=0),
         name="halo",
@@ -318,9 +331,9 @@
     total_ref, an_hi_ref, an_lo_ref, map_ref, load_int_ref, load_if_ref, kinv, sinv_t,
     du_int_ref, du_if_ref,
     sinv, out_ret, in_ret, spread, spread_if, rhs_int,
-    out_grp, in_grp, out_rhs, all_rhs, flat,
+    out_grp, in_grp, flat,
     own1, out1, in1, out2, in2, own3, out3, in3, last,
-    ret_sem, grp_sem, rhs_sem, sem1, sem2, sem3,
+    ret_sem, grp_sem, sem1, sem2, sem3,
 ):
     zs, xs, cores, grps = sizes
     started = []
@@ -376,14 +389,12 @@
     high = back.astype(BF16)
     low = (back - high.astype(F32)).astype(BF16)
     force = own + dot(hits, high) + dot(hits, low)
-    share = out_grp.shape[1]
-    pieces = jnp.concatenate(
-        [force[int_nodes:], jnp.zeros((grps * share - if_nodes, width), F32)], axis=0
-    )
-    for q in range(grps):
-        out_grp[q] = pieces[q * share : (q + 1) * share]
+    shared = force[int_nodes:]
+    out_grp[...] = jnp.concatenate(
+        [shared, jnp.zeros((out_grp.shape[0] - if_nodes, width), F32)], axis=0
+    ).astype(BF16)
     copies = [
-        launch(out_grp.at[peer["grp"]], in_grp.at[s], grp_sem.at[0, s], grp_sem.at[1, s], peer)
+        launch(out_grp, in_grp.at[s], grp_sem.at[0, s], grp_sem.at[1, s], peer)
         for s, peer in enumerate(groups)
     ]
     r_int = load_int - force[:int_nodes]
@@ -398,27 +409,11 @@
         spread[rows, :] = dot(kinv[rows, :], rhs_int[...])
         return 0
 
-    lax.fori_loop(0, 2, solve, 0)
-    loads = jnp.concatenate(
-        [load_if_ref[...], jnp.zeros((grps * share - if_nodes, width), F32)], axis=0
-    )
-    mine = loads[0:share]
-    for q in range(1, grps):
-        mine = jnp.where(my_grp == q, loads[q * share : (q + 1) * share], mine)
-    total = out_grp[my_grp]
+    lax.fori_loop(0, 3, solve, 0)
     for s, copy in enumerate(copies):
         copy.wait_recv()
-        total = total + in_grp[s]
-    out_rhs[...] = (mine - total).astype(BF16)
-    copies = [
-        launch(out_rhs, all_rhs.at[my_grp], rhs_sem.at[0, s], rhs_sem.at[1, s], peer)
-        for s, peer in enumerate(groups)
-    ]
-    all_rhs[my_grp] = out_rhs[...]
-    lax.fori_loop(2, 3, solve, 0)
-    for copy in copies:
-        copy.wait_recv()
-    gathered = jnp.concatenate([all_rhs[q].astype(F32) for q in range(grps)], axis=0)[:if_nodes]
+        shared = shared + in_grp[s][:if_nodes].astype(F32)
+    gathered = (load_if_ref[...] - shared).astype(BF16).astype(F32)
     for i in range(3):
         spread_if[pl.ds(i, if_nodes, stride=3), :] = gathered[:, i * fourier : (i + 1) * fourier]
     rhs_if = spread_if[...]
@@ -519,7 +514,7 @@
     dom = zs * xs * cores
     per_owner = sinv_rows // dom
     up = lambda n, k: -(-n // k) * k
-    share = up(-(-if_nodes // grps), 8)
+    share = up(if_nodes, 16)
     parts = 2
     each = zs // 2 // parts
     rows1 = up(per_owner * each, 16)
@@ -543,10 +538,8 @@
             pltpu.VMEM((3 * int_nodes, fourier), F32),
             pltpu.VMEM((3 * if_nodes, fourier), F32),
             pltpu.VMEM((3 * int_nodes, fourier), BF16),
-            pltpu.VMEM((grps, share, width), F32),
-            pltpu.VMEM((grps - 1, share, width), F32),
             pltpu.VMEM((share, width), BF16),
-            pltpu.VMEM((grps, share, width), BF16),
+            pltpu.VMEM((grps - 1, share, width), BF16),
             pltpu.VMEM((sinv_rows // 2, lanes), F32),
             pltpu.VMEM((parts, xs, rows1, lanes), F32),
             pltpu.VMEM((parts, xs, rows1, lanes), BF16),
@@ -557,7 +550,7 @@
             pltpu.VMEM((parts, each, 2, rows3, lanes), BF16),
             pltpu.VMEM((zs - 1, rows3, lanes), BF16),
             pltpu.VMEM((2, rows3, lanes), F32),
-            sems((2, neighbours)), sems((2, grps - 1)), sems((2, grps - 1)),
+            sems((2, neighbours)), sems((2, grps - 1)),
             sems((2, parts)), sems((2, parts, xs - 1)), sems((2, zs - 1)),
         ],
         compiler_params=pltpu.CompilerParams(

time: 62.5 us -> 58.9 us (0.942)
  Pallas kernels: 56.9 us -> 54.8 us
  local copies, waits for them, and re-layouts: 3.85 us -> 2.35 us
    pallas_call x1, Pallas kernels: 37.2 us -> 34.4 us  [finish(): pl.pallas_call(functools.partial(finish_kernel, sizes, offsets, stop), ou...]
    unnamed x46 -> x42, local copies, waits for them, and re-layouts: 3.85 us -> 2.35 us
    pallas_call x1, Pallas kernels: 4.99 us -> 5.66 us  [halo(): pl.pallas_call(functools.partial(halo_kernel, dom, offsets), out_shape=ja...]
where the time goes in v6:
time: 58.9 us; the launch traced here: 58.7 us
  Pallas kernels  54.8 us (93%)
  local copies, waits for them, and re-layouts  2.35 us (4%)
  between operations  1.59 us (3%)
    pallas_call x1, Pallas kernels, finish(): pl.pallas_call(functools.partial(finish_kernel, sizes, offsets, stop), ou...  34.4 us
    pallas_call x1, Pallas kernels, element_update(): pl.pallas_call(element_kernel, grid=(elems // block,), out_shape=(jax.Sha...  14.7 us
    pallas_call x1, Pallas kernels, halo(): pl.pallas_call(functools.partial(halo_kernel, dom, offsets), out_shape=ja...  5.66 us
    unnamed x42, local copies, waits for them, and re-layouts  2.35 us

profile of v6, /device:TPU:4, one launch (start us, length us, event | category | flops | bytes accessed | tf_op | source)
XLA Modules:
  0.0 58.7 jit_solution(13473924571542239775)
XLA Ops:
  1.3 0.0 copy-start.1
  1.3 0.0 copy-start.3
  1.3 0.0 copy-start.5
  1.3 0.0 copy-start.6
  1.3 0.0 copy-start.7
  1.3 0.0 copy-start.8
  1.3 0.0 copy-start.9
  1.3 0.0 copy-start.11
  1.4 0.0 copy-start.12
  1.4 0.0 copy-start.15
  1.4 0.0 copy-start.16
  1.4 0.0 slice-start
  1.4 5.7 %halo.1.tail_ref = bf16[256,192]{1,0:T(8,128)(2,1)} custom-call(bf16[192,512]{1,0:T(8,128)(2,1)} %bitcast.14, bf16[88,192]{1,0:T(8,128)(2,1)} %if_far.1, s32[4,32]{1,0:T(4,128)} %map_ref.1), custom_call_target="tpu_custom_call" | custom-call | flops 6000000000 | bytes 1000000 | tf_op jit(solution)/shard_map/halo/pallas_call | solution.py:306
  7.1 0.0 copy-done.1
  7.1 0.0 copy-done.3
  7.1 0.0 copy-done.5
  7.2 0.9 %copy-done.17 = bf16[256,192]{1,0:T(8,128)(2,1)S(1)} copy-done((bf16[256,192]{1,0:T(8,128)(2,1)S(1)}, bf16[256,192]{1,0:T(8,128)(2,1)}, u32[]{:S(2)}) %copy-start.17) | copy-done | bytes 98328
  8.1 0.0 copy-start.10
  8.1 0.0 copy-start.13
  8.1 0.0 copy-start.14
  8.1 14.7 %elements.1 = (f32[48,2048]{1,0:T(8,128)}, f32[288,256]{1,0:T(8,128)S(1)}) custom-call(s32[1]{0:T(128)S(6)} %copy.25.counts_ref, bf16[192,512]{1,0:T(8,128)(2,1)S(1)} %bitcast.15, bf16[256,192]{1,0:T(8,128)(2,1)S(1)} %copy-done.17, s32[8,2048]{1,0:T(8,128)S(1)} %bitcast.16, f32[1,2048]{1,0:T(1,128)S(1)} %bitcast.17, f32[1,2048]{1,0:T(1,128)S(1)} %bitcast.18, ...), custom_call_target="tpu_custom_call" | custom-call | flops 24999999488 | bytes 4000000 | tf_op jit(solution)/shard_map/elements/pallas_call | solution.py:215
  22.9 34.4 %finish.1 = (f32[192,512]{1,0:T(8,128)S(1)}, f32[22,192]{1,0:T(8,128)S(1)}) custom-call(f32[288,256]{1,0:T(8,128)S(1)} %get-tuple-element.7.total_ref, bf16[96,192]{1,0:T(8,128)(2,1)S(1)} %copy-done.14, bf16[96,192]{1,0:T(8,128)(2,1)S(1)} %copy-done.13, s32[4,32]{1,0:T(4,128)S(1)} %copy-done.10, f32[192,512]{1,0:T(8,128)S(1)} %bitcast.13, ...), custom_call_target="tpu_custom_call" | custom-call | flops 20000000000 | bytes 9000000 | tf_op jit(solution)/shard_map/finish/pallas_call | solution.py:526
  57.4 0.7 %copy.26 = f32[512,192]{0,1:T(8,128)} copy(f32[512,192]{0,1:T(8,128)S(1)} %bitcast.9) | data formatting | bytes 786432
  58.1 0.6 %copy.27 = f32[22,192]{1,0:T(8,128)} copy(f32[22,192]{1,0:T(8,128)S(1)} %get-tuple-element.15) | data formatting | bytes 33792
  (22 shorter events, 0.0 us)
Async XLA Ops:
  1.3 5.8 %copy-start.1 = (f32[48,2048]{1,0:T(8,128)S(1)}, f32[48,2048]{1,0:T(8,128)}, u32[]{:S(2)}) copy-start(f32[48,2048]{1,0:T(8,128)} %stress_ref.1) | copy-start | bytes 1179652
  1.3 5.8 %copy-start.3 = (bf16[512,192]{0,1:T(8,128)(2,1)S(1)}, bf16[512,192]{0,1:T(8,128)(2,1)}, u32[]{:S(2)}) copy-start(bf16[512,192]{0,1:T(8,128)(2,1)} %param.20) | copy-start | bytes 589828
  1.3 5.8 %copy-start.5 = (s32[2048,8]{0,1:T(8,128)S(1)}, s32[2048,8]{0,1:T(8,128)}, u32[]{:S(2)}) copy-start(s32[2048,8]{0,1:T(8,128)} %param.24) | copy-start | bytes 196612
  1.3 5.8 %copy-start.6 = (f32[2048]{0:T(1024)S(1)}, f32[2048]{0:T(1024)}, u32[]{:S(2)}) copy-start(f32[2048]{0:T(1024)} %param.27) | copy-start | bytes 24580
  1.3 5.8 %copy-start.7 = (f32[2048]{0:T(1024)S(1)}, f32[2048]{0:T(1024)}, u32[]{:S(2)}) copy-start(f32[2048]{0:T(1024)} %param.28) | copy-start | bytes 24580
  1.3 5.8 %copy-start.8 = (f32[2048]{0:T(1024)S(1)}, f32[2048]{0:T(1024)}, u32[]{:S(2)}) copy-start(f32[2048]{0:T(1024)} %param.29) | copy-start | bytes 24580
  1.3 5.8 %copy-start.9 = (f32[2048]{0:T(1024)S(1)}, f32[2048]{0:T(1024)}, u32[]{:S(2)}) copy-start(f32[2048]{0:T(1024)} %param.30) | copy-start | bytes 24580
  1.3 5.8 %copy-start.11 = (bf16[384,384]{1,0:T(8,128)(2,1)S(1)}, bf16[384,384]{1,0:T(8,128)(2,1)}, u32[]{:S(2)}) copy-start(bf16[384,384]{1,0:T(8,128)(2,1)} %constant.14.clone.strain_ref) | copy-start | bytes 884740
  1.4 5.8 %copy-start.12 = (bf16[192,384]{1,0:T(8,128)(2,1)S(1)}, bf16[192,384]{1,0:T(8,128)(2,1)}, u32[]{:S(2)}) copy-start(bf16[192,384]{1,0:T(8,128)(2,1)} %constant.15.clone.force_ref) | copy-start | bytes 442372
  1.4 5.8 %copy-start.15 = (bf16[96,192]{1,0:T(8,128)(2,1)S(1)}, bf16[96,192]{1,0:T(8,128)(2,1)}, u32[]{:S(2)}) copy-start(bf16[96,192]{1,0:T(8,128)(2,1)} %constant.13.clone.synth_lo_ref) | copy-start | bytes 110596
  1.4 5.8 %copy-start.16 = (bf16[96,192]{1,0:T(8,128)(2,1)S(1)}, bf16[96,192]{1,0:T(8,128)(2,1)}, u32[]{:S(2)}) copy-start(bf16[96,192]{1,0:T(8,128)(2,1)} %constant.12.clone.synth_hi_ref) | copy-start | bytes 110596
  1.4 21.5 %slice-start = ((s8[4718592]{0:T(1024)(128)(4,1)}), s8[524288]{0:T(1024)(128)(4,1)S(1)}, s32[]{:S(2)}) async-start(s8[4718592]{0:T(1024)(128)(4,1)} %bitcast.10), calls=%async_computation | async-start | bytes 1048576
  7.2 0.9 %copy-start.17 = (bf16[256,192]{1,0:T(8,128)(2,1)S(1)}, bf16[256,192]{1,0:T(8,128)(2,1)}, u32[]{:S(2)}) copy-start(bf16[256,192]{1,0:T(8,128)(2,1)} %halo.1.tail_ref) | copy-start | bytes 294916
  8.1 14.8 %slice-start.1 = ((s8[4718592]{0:T(1024)(128)(4,1)}), s8[4194304]{0:T(1024)(128)(4,1)S(1)}, s32[]{:S(2)}) async-start(s8[4718592]{0:T(1024)(128)(4,1)} %bitcast.10), calls=%async_computation.1 | async-start | bytes 8388608
  8.1 14.8 %copy-start = (bf16[4224,264]{0,1:T(8,128)(2,1)S(1)}, bf16[4224,264]{0,1:T(8,128)(2,1)}, u32[]{:S(2)}) copy-start(bf16[4224,264]{0,1:T(8,128)(2,1)} %param.33) | copy-start | bytes 6690820
  8.1 14.8 %copy-start.2 = (f32[512,192]{0,1:T(8,128)S(1)}, f32[512,192]{0,1:T(8,128)}, u32[]{:S(2)}) copy-start(f32[512,192]{0,1:T(8,128)} %param.22) | copy-start | bytes 1179652
  8.1 14.8 %copy-start.4 = (f32[88,192]{1,0:T(8,128)S(1)}, f32[88,192]{1,0:T(8,128)}, u32[]{:S(2)}) copy-start(f32[88,192]{1,0:T(8,128)} %load_if_ref.1) | copy-start | bytes 202756
  8.1 14.8 %copy-start.10 = (s32[4,32]{1,0:T(4,128)S(1)}, s32[4,32]{1,0:T(4,128)}, u32[]{:S(2)}) copy-start(s32[4,32]{1,0:T(4,128)} %map_ref.1) | copy-start | bytes 1540
  8.1 14.8 %copy-start.13 = (bf16[96,192]{1,0:T(8,128)(2,1)S(1)}, bf16[96,192]{1,0:T(8,128)(2,1)}, u32[]{:S(2)}) copy-start(bf16[96,192]{1,0:T(8,128)(2,1)} %constant.17.clone.an_lo_ref) | copy-start | bytes 110596
  8.1 14.8 %copy-start.14 = (bf16[96,192]{1,0:T(8,128)(2,1)S(1)}, bf16[96,192]{1,0:T(8,128)(2,1)}, u32[]{:S(2)}) copy-start(bf16[96,192]{1,0:T(8,128)(2,1)} %constant.16.clone.an_hi_ref) | copy-start | bytes 110596

commit v7 on v6

--- a/solution.py
+++ b/solution.py
@@ -133,65 +133,71 @@
         nodal[:, first:] = split_rows(dot_t(high, tail) + dot_t(low, tail))
         total[...] = jnp.zeros_like(total)
 
-    fold = total.shape[1]
-    pages = total.shape[0] // (3 * TIMES)
-    listed = jnp.transpose(conn_ref[...])
-    lane = lax.broadcasted_iota(jnp.int32, (block, fold), 1)
-    iota = lax.broadcasted_iota(jnp.int16, (nodes, block), 0)
-    for a in range(8):
-        index = conn_ref[a : a + 1, :].astype(jnp.int16)
-        hit = iota == jnp.broadcast_to(index, (nodes, block))
-        onehot[:, a * block : (a + 1) * block] = jnp.where(
-            hit, jnp.ones((), BF16), jnp.zeros((), BF16)
-        )
-        place = jnp.broadcast_to((listed[:, a : a + 1] & (fold - 1)), (block, fold))
-        folded[a * block : (a + 1) * block, :] = (place == lane).astype(F32).astype(BF16)
-    table = nodal[...]
-    for a in range(8):
-        picked = dot(table, onehot[:, a * block : (a + 1) * block]).astype(BF16)
+    @pl.when(step * block >= counts_ref[0])
+    def _():
+        stress_out[...] = jnp.zeros_like(stress_out)
+
+    @pl.when(step * block < counts_ref[0])
+    def _():
+        fold = total.shape[1]
+        pages = total.shape[0] // (3 * TIMES)
+        listed = jnp.transpose(conn_ref[...])
+        lane = lax.broadcasted_iota(jnp.int32, (block, fold), 1)
+        iota = lax.broadcasted_iota(jnp.int16, (nodes, block), 0)
+        for a in range(8):
+            index = conn_ref[a : a + 1, :].astype(jnp.int16)
+            hit = iota == jnp.broadcast_to(index, (nodes, block))
+            onehot[:, a * block : (a + 1) * block] = jnp.where(
+                hit, jnp.ones((), BF16), jnp.zeros((), BF16)
+            )
+            place = jnp.broadcast_to((listed[:, a : a + 1] & (fold - 1)), (block, fold))
+            folded[a * block : (a + 1) * block, :] = (place == lane).astype(F32).astype(BF16)
+        table = nodal[...]
+        for a in range(8):
+            picked = dot(table, onehot[:, a * block : (a + 1) * block]).astype(BF16)
+            for g in range(groups):
+                gathered[g, a * 48 : (a + 1) * 48, :] = picked[g * 48 : (g + 1) * 48, :]
+
+        size = size_ref[...]
+        stiff = stiff_ref[...]
+        yields = yield_ref[...]
+        rate8 = jnp.broadcast_to(rate_ref[...], (8, block))
+        inverse = 1.0 / yields
+        weight = stiff * (2.0 / size) * inverse
+        shear8 = jnp.broadcast_to(weight * SHEAR, (8, block))
+        shear28 = shear8 * 2.0
+        lame8 = jnp.broadcast_to(weight * LAME, (8, block))
+        slot = lax.broadcasted_iota(jnp.int32, (1, block), 1) + step * block
+        live = (slot < counts_ref[0]).astype(F32)
+        scale = size * size * 0.25 * live * yields
+        state = [stress_ref[c * 8 : (c + 1) * 8, :] * inverse for c in range(6)]
+        deltas = [dot(strain_ref[...], gathered[g]) for g in range(groups)]
         for g in range(groups):
-            gathered[g, a * 48 : (a + 1) * 48, :] = picked[g * 48 : (g + 1) * 48, :]
-
-    size = size_ref[...]
-    stiff = stiff_ref[...]
-    yields = yield_ref[...]
-    rate8 = jnp.broadcast_to(rate_ref[...], (8, block))
-    inverse = 1.0 / yields
-    weight = stiff * (2.0 / size) * inverse
-    shear8 = jnp.broadcast_to(weight * SHEAR, (8, block))
-    shear28 = shear8 * 2.0
-    lame8 = jnp.broadcast_to(weight * LAME, (8, block))
-    slot = lax.broadcasted_iota(jnp.int32, (1, block), 1) + step * block
-    live = (slot < counts_ref[0]).astype(F32)
-    scale = size * size * 0.25 * live * yields
-    state = [stress_ref[c * 8 : (c + 1) * 8, :] * inverse for c in range(6)]
-    deltas = [dot(strain_ref[...], gathered[g]) for g in range(groups)]
-    for g in range(groups):
-        delta = deltas[g]
-        for m in range(GROUP):
-            d = [delta[m * 48 + c * 8 : m * 48 + c * 8 + 8, :] for c in range(6)]
-            volume = (d[0] + d[1] + d[2]) * lame8
-            for c in range(6):
-                rise = d[c] * shear28 + volume if c < 3 else d[c] * shear8
-                state[c] = state[c] + rise - rate8 * jnp.tanh(state[c])
-            stresses[g, m * 48 : (m + 1) * 48, :] = jnp.concatenate(state, axis=0).astype(BF16)
-        pushed = dot(force_ref[...], stresses[g]) * scale
-        if g % 2 == 0:
-            before = pushed
-            continue
-        for a in range(8):
-            rows = slice(a * 24, (a + 1) * 24)
-            both = jnp.concatenate([before[rows, :], pushed[rows, :]], axis=0)
-            page = lax.shift_right_logical(conn_ref[a : a + 1, :], 8)
-            for t in range(pages):
-                at_row = t * 3 * TIMES + (g - 1) * 24
-                forces[at_row : at_row + 48, a * block : (a + 1) * block] = jnp.where(
-                    page == t, both, 0.0
-                ).astype(BF16)
-    stress_out[...] = jnp.concatenate(state, axis=0) * (yields * live)
-    rows = total.shape[0] // 2
-    for half in (slice(0, rows), slice(rows, 2 * rows)):
-        total[half, :] += dot(forces[half, :], folded[...])
+            delta = deltas[g]
+            for m in range(GROUP):
+                d = [delta[m * 48 + c * 8 : m * 48 + c * 8 + 8, :] for c in range(6)]
+                volume = (d[0] + d[1] + d[2]) * lame8
+                for c in range(6):
+                    rise = d[c] * shear28 + volume if c < 3 else d[c] * shear8
+                    state[c] = state[c] + rise - rate8 * jnp.tanh(state[c])
+                stresses[g, m * 48 : (m + 1) * 48, :] = jnp.concatenate(state, axis=0).astype(BF16)
+            pushed = dot(force_ref[...], stresses[g]) * scale
+            if g % 2 == 0:
+                before = pushed
+                continue
+            for a in range(8):
+                rows = slice(a * 24, (a + 1) * 24)
+                both = jnp.concatenate([before[rows, :], pushed[rows, :]], axis=0)
+                page = lax.shift_right_logical(conn_ref[a : a + 1, :], 8)
+                for t in range(pages):
+                    at_row = t * 3 * TIMES + (g - 1) * 24
+                    forces[at_row : at_row + 48, a * block : (a + 1) * block] = jnp.where(
+                        page == t, both, 0.0
+                    ).astype(BF16)
+        stress_out[...] = jnp.concatenate(state, axis=0) * (yields * live)
+        rows = total.shape[0] // 2
+        for half in (slice(0, rows), slice(rows, 2 * rows)):
+            total[half, :] += dot(forces[half, :], folded[...])
 
 
 def node_forces(total_ref, an_hi_ref, an_lo_ref, page):
@@ -428,6 +434,7 @@
     fill = jnp.zeros((out1.shape[2] - each * per_owner, 2 * fourier), F32)
     first_copies = []
     for c in range(parts):
+        first_copies.append([])
         for j in range(each):
             start = pl.multiple_of(lax.rem(z + c * each + j + 1, half) * per_z, 16)
             other = pl.multiple_of(start + half * per_z, 16)
@@ -444,11 +451,13 @@
                 by_core.append(jnp.concatenate(rows + [fill], axis=0))
             own1[c, k] = jnp.where(core == 0, by_core[0], by_core[1])
             out1[c, k] = jnp.where(core == 0, by_core[1], by_core[0]).astype(BF16)
-        first_copies.append(launch(out1.at[c], in1.at[c], sem1.at[0, c], sem1.at[1, c], sibling))
+            first_copies[c].append(
+                launch(out1.at[c, k], in1.at[c, k], sem1.at[0, c, k], sem1.at[1, c, k], sibling)
+            )
     second_copies = []
     for c in range(parts):
-        first_copies[c].wait_recv()
         for k in range(xs):
+            first_copies[c][k].wait_recv()
             summed = own1[c, k] + in1[c, k].astype(F32)
             own1[c, k] = summed
             out2[c, k] = summed.astype(BF16)
@@ -551,7 +560,7 @@
             pltpu.VMEM((zs - 1, rows3, lanes), BF16),
             pltpu.VMEM((2, rows3, lanes), F32),
             sems((2, neighbours)), sems((2, grps - 1)),
-            sems((2, parts)), sems((2, parts, xs - 1)), sems((2, zs - 1)),
+            sems((2, parts, xs)), sems((2, parts, xs - 1)), sems((2, zs - 1)),
         ],
         compiler_params=pltpu.CompilerParams(
             collective_id=1, has_side_effects=True, vmem_limit_bytes=20 * 1024 * 1024

time: 58.9 us -> 59.6 us (1.012)
  Pallas kernels: 54.8 us -> 55.5 us
    pallas_call x1, Pallas kernels: 34.4 us -> 44.6 us  [finish(): pl.pallas_call(functools.partial(finish_kernel, sizes, offsets, stop), ou...]
    pallas_call x1, Pallas kernels: 14.7 us -> 5.28 us  [element_update(): pl.pallas_call(element_kernel, grid=(elems // block,), out_shape=(jax.Sha...]
where the time goes in v7:
time: 59.6 us; the launch traced here: 59.4 us
  Pallas kernels  55.5 us (93%)
  local copies, waits for them, and re-layouts  2.35 us (4%)
  between operations  1.57 us (3%)
    pallas_call x1, Pallas kernels, finish(): pl.pallas_call(functools.partial(finish_kernel, sizes, offsets, stop), ou...  44.6 us
    pallas_call x1, Pallas kernels, halo(): pl.pallas_call(functools.partial(halo_kernel, dom, offsets), out_shape=ja...  5.66 us
    pallas_call x1, Pallas kernels, element_update(): pl.pallas_call(element_kernel, grid=(elems // block,), out_shape=(jax.Sha...  5.28 us
    unnamed x42, local copies, waits for them, and re-layouts  2.35 us

profile of v7, /device:TPU:4, one launch (start us, length us, event | category | flops | bytes accessed | tf_op | source)
XLA Modules:
  0.0 59.4 jit_solution(2685776804708384068)
XLA Ops:
  1.3 0.0 copy-start.1
  1.3 0.0 copy-start.3
  1.3 0.0 copy-start.5
  1.3 0.0 copy-start.6
  1.3 0.0 copy-start.7
  1.3 0.0 copy-start.8
  1.3 0.0 copy-start.9
  1.3 0.0 copy-start.11
  1.4 0.0 copy-start.12
  1.4 0.0 copy-start.15
  1.4 0.0 copy-start.16
  1.4 0.0 slice-start
  1.4 5.7 %halo.1.tail_ref = bf16[256,192]{1,0:T(8,128)(2,1)} custom-call(bf16[192,512]{1,0:T(8,128)(2,1)} %bitcast.14, bf16[88,192]{1,0:T(8,128)(2,1)} %if_far.1, s32[4,32]{1,0:T(4,128)} %map_ref.1), custom_call_target="tpu_custom_call" | custom-call | flops 6000000000 | bytes 1000000 | tf_op jit(solution)/shard_map/halo/pallas_call | solution.py:312
  7.1 0.0 copy-done.1
  7.1 0.0 copy-done.3
  7.2 0.9 %copy-done.17 = bf16[256,192]{1,0:T(8,128)(2,1)S(1)} copy-done((bf16[256,192]{1,0:T(8,128)(2,1)S(1)}, bf16[256,192]{1,0:T(8,128)(2,1)}, u32[]{:S(2)}) %copy-start.17) | copy-done | bytes 98328
  8.1 0.0 copy-start.10
  8.1 0.0 copy-start.13
  8.1 0.0 copy-start.14
  8.1 5.3 %elements.1 = (f32[48,2048]{1,0:T(8,128)}, f32[288,256]{1,0:T(8,128)S(1)}) custom-call(s32[1]{0:T(128)S(6)} %copy.25.counts_ref, bf16[192,512]{1,0:T(8,128)(2,1)S(1)} %bitcast.15, bf16[256,192]{1,0:T(8,128)(2,1)S(1)} %copy-done.17, s32[8,2048]{1,0:T(8,128)S(1)} %bitcast.16, f32[1,2048]{1,0:T(1,128)S(1)} %bitcast.17, f32[1,2048]{1,0:T(1,128)S(1)} %bitcast.18, ...), custom_call_target="tpu_custom_call" | custom-call | flops 24999999488 | bytes 4000000 | tf_op jit(solution)/shard_map/elements/pallas_call | solution.py:221
  13.4 0.0 slice-done
  13.5 44.6 %finish.1 = (f32[192,512]{1,0:T(8,128)S(1)}, f32[22,192]{1,0:T(8,128)S(1)}) custom-call(f32[288,256]{1,0:T(8,128)S(1)} %get-tuple-element.7.total_ref, bf16[96,192]{1,0:T(8,128)(2,1)S(1)} %copy-done.14, bf16[96,192]{1,0:T(8,128)(2,1)S(1)} %copy-done.13, s32[4,32]{1,0:T(4,128)S(1)} %copy-done.10, f32[192,512]{1,0:T(8,128)S(1)} %bitcast.13, ...), custom_call_target="tpu_custom_call" | custom-call | flops 20000000000 | bytes 9000000 | tf_op jit(solution)/shard_map/finish/pallas_call | solution.py:535
  58.1 0.7 %copy.26 = f32[512,192]{0,1:T(8,128)} copy(f32[512,192]{0,1:T(8,128)S(1)} %bitcast.9) | data formatting | bytes 786432
  58.8 0.6 %copy.27 = f32[22,192]{1,0:T(8,128)} copy(f32[22,192]{1,0:T(8,128)S(1)} %get-tuple-element.15) | data formatting | bytes 33792
  (22 shorter events, 0.0 us)
Async XLA Ops:
  1.3 5.8 %copy-start.1 = (f32[48,2048]{1,0:T(8,128)S(1)}, f32[48,2048]{1,0:T(8,128)}, u32[]{:S(2)}) copy-start(f32[48,2048]{1,0:T(8,128)} %stress_ref.1) | copy-start | bytes 1179652
  1.3 5.8 %copy-start.3 = (bf16[512,192]{0,1:T(8,128)(2,1)S(1)}, bf16[512,192]{0,1:T(8,128)(2,1)}, u32[]{:S(2)}) copy-start(bf16[512,192]{0,1:T(8,128)(2,1)} %param.20) | copy-start | bytes 589828
  1.3 5.8 %copy-start.5 = (s32[2048,8]{0,1:T(8,128)S(1)}, s32[2048,8]{0,1:T(8,128)}, u32[]{:S(2)}) copy-start(s32[2048,8]{0,1:T(8,128)} %param.24) | copy-start | bytes 196612
  1.3 5.8 %copy-start.6 = (f32[2048]{0:T(1024)S(1)}, f32[2048]{0:T(1024)}, u32[]{:S(2)}) copy-start(f32[2048]{0:T(1024)} %param.27) | copy-start | bytes 24580
  1.3 5.8 %copy-start.7 = (f32[2048]{0:T(1024)S(1)}, f32[2048]{0:T(1024)}, u32[]{:S(2)}) copy-start(f32[2048]{0:T(1024)} %param.28) | copy-start | bytes 24580
  1.3 5.8 %copy-start.8 = (f32[2048]{0:T(1024)S(1)}, f32[2048]{0:T(1024)}, u32[]{:S(2)}) copy-start(f32[2048]{0:T(1024)} %param.29) | copy-start | bytes 24580
  1.3 5.8 %copy-start.9 = (f32[2048]{0:T(1024)S(1)}, f32[2048]{0:T(1024)}, u32[]{:S(2)}) copy-start(f32[2048]{0:T(1024)} %param.30) | copy-start | bytes 24580
  1.3 5.8 %copy-start.11 = (bf16[384,384]{1,0:T(8,128)(2,1)S(1)}, bf16[384,384]{1,0:T(8,128)(2,1)}, u32[]{:S(2)}) copy-start(bf16[384,384]{1,0:T(8,128)(2,1)} %constant.14.clone.strain_ref) | copy-start | bytes 884740
  1.4 5.8 %copy-start.12 = (bf16[192,384]{1,0:T(8,128)(2,1)S(1)}, bf16[192,384]{1,0:T(8,128)(2,1)}, u32[]{:S(2)}) copy-start(bf16[192,384]{1,0:T(8,128)(2,1)} %constant.15.clone.force_ref) | copy-start | bytes 442372
  1.4 5.8 %copy-start.15 = (bf16[96,192]{1,0:T(8,128)(2,1)S(1)}, bf16[96,192]{1,0:T(8,128)(2,1)}, u32[]{:S(2)}) copy-start(bf16[96,192]{1,0:T(8,128)(2,1)} %constant.13.clone.synth_lo_ref) | copy-start | bytes 110596
  1.4 5.8 %copy-start.16 = (bf16[96,192]{1,0:T(8,128)(2,1)S(1)}, bf16[96,192]{1,0:T(8,128)(2,1)}, u32[]{:S(2)}) copy-start(bf16[96,192]{1,0:T(8,128)(2,1)} %constant.12.clone.synth_hi_ref) | copy-start | bytes 110596
  1.4 12.0 %slice-start = ((s8[4718592]{0:T(1024)(128)(4,1)}), s8[524288]{0:T(1024)(128)(4,1)S(1)}, s32[]{:S(2)}) async-start(s8[4718592]{0:T(1024)(128)(4,1)} %bitcast.10), calls=%async_computation | async-start | bytes 1048576
  7.2 0.9 %copy-start.17 = (bf16[256,192]{1,0:T(8,128)(2,1)S(1)}, bf16[256,192]{1,0:T(8,128)(2,1)}, u32[]{:S(2)}) copy-start(bf16[256,192]{1,0:T(8,128)(2,1)} %halo.1.tail_ref) | copy-start | bytes 294916
  8.1 5.3 %slice-start.1 = ((s8[4718592]{0:T(1024)(128)(4,1)}), s8[4194304]{0:T(1024)(128)(4,1)S(1)}, s32[]{:S(2)}) async-start(s8[4718592]{0:T(1024)(128)(4,1)} %bitcast.10), calls=%async_computation.1 | async-start | bytes 8388608
  8.1 5.3 %copy-start = (bf16[4224,264]{0,1:T(8,128)(2,1)S(1)}, bf16[4224,264]{0,1:T(8,128)(2,1)}, u32[]{:S(2)}) copy-start(bf16[4224,264]{0,1:T(8,128)(2,1)} %param.33) | copy-start | bytes 6690820
  8.1 5.3 %copy-start.2 = (f32[512,192]{0,1:T(8,128)S(1)}, f32[512,192]{0,1:T(8,128)}, u32[]{:S(2)}) copy-start(f32[512,192]{0,1:T(8,128)} %param.22) | copy-start | bytes 1179652
  8.1 5.3 %copy-start.4 = (f32[88,192]{1,0:T(8,128)S(1)}, f32[88,192]{1,0:T(8,128)}, u32[]{:S(2)}) copy-start(f32[88,192]{1,0:T(8,128)} %load_if_ref.1) | copy-start | bytes 202756
  8.1 5.4 %copy-start.10 = (s32[4,32]{1,0:T(4,128)S(1)}, s32[4,32]{1,0:T(4,128)}, u32[]{:S(2)}) copy-start(s32[4,32]{1,0:T(4,128)} %map_ref.1) | copy-start | bytes 1540
  8.1 5.3 %copy-start.13 = (bf16[96,192]{1,0:T(8,128)(2,1)S(1)}, bf16[96,192]{1,0:T(8,128)(2,1)}, u32[]{:S(2)}) copy-start(bf16[96,192]{1,0:T(8,128)(2,1)} %constant.17.clone.an_lo_ref) | copy-start | bytes 110596
  8.1 5.3 %copy-start.14 = (bf16[96,192]{1,0:T(8,128)(2,1)S(1)}, bf16[96,192]{1,0:T(8,128)(2,1)}, u32[]{:S(2)}) copy-start(bf16[96,192]{1,0:T(8,128)(2,1)} %constant.16.clone.an_hi_ref) | copy-start | bytes 110596

commit v8 on v6

--- a/solution.py
+++ b/solution.py
@@ -428,6 +428,7 @@
     fill = jnp.zeros((out1.shape[2] - each * per_owner, 2 * fourier), F32)
     first_copies = []
     for c in range(parts):
+        first_copies.append([])
         for j in range(each):
             start = pl.multiple_of(lax.rem(z + c * each + j + 1, half) * per_z, 16)
             other = pl.multiple_of(start + half * per_z, 16)
@@ -444,11 +445,13 @@
                 by_core.append(jnp.concatenate(rows + [fill], axis=0))
             own1[c, k] = jnp.where(core == 0, by_core[0], by_core[1])
             out1[c, k] = jnp.where(core == 0, by_core[1], by_core[0]).astype(BF16)
-        first_copies.append(launch(out1.at[c], in1.at[c], sem1.at[0, c], sem1.at[1, c], sibling))
+            first_copies[c].append(
+                launch(out1.at[c, k], in1.at[c, k], sem1.at[0, c, k], sem1.at[1, c, k], sibling)
+            )
     second_copies = []
     for c in range(parts):
-        first_copies[c].wait_recv()
         for k in range(xs):
+            first_copies[c][k].wait_recv()
             summed = own1[c, k] + in1[c, k].astype(F32)
             own1[c, k] = summed
             out2[c, k] = summed.astype(BF16)
@@ -551,7 +554,7 @@
             pltpu.VMEM((zs - 1, rows3, lanes), BF16),
             pltpu.VMEM((2, rows3, lanes), F32),
             sems((2, neighbours)), sems((2, grps - 1)),
-            sems((2, parts)), sems((2, parts, xs - 1)), sems((2, zs - 1)),
+            sems((2, parts, xs)), sems((2, parts, xs - 1)), sems((2, zs - 1)),
         ],
         compiler_params=pltpu.CompilerParams(
             collective_id=1, has_side_effects=True, vmem_limit_bytes=20 * 1024 * 1024

time: 58.9 us -> 58.9 us (level)
  no operation moved by 1% of the time
where the time goes in v8:
time: 58.9 us; the launch traced here: 58.8 us
  Pallas kernels  54.8 us (93%)
  local copies, waits for them, and re-layouts  2.35 us (4%)
  between operations  1.59 us (3%)
    pallas_call x1, Pallas kernels, finish(): pl.pallas_call(functools.partial(finish_kernel, sizes, offsets, stop), ou...  34.5 us
    pallas_call x1, Pallas kernels, element_update(): pl.pallas_call(element_kernel, grid=(elems // block,), out_shape=(jax.Sha...  14.7 us
    pallas_call x1, Pallas kernels, halo(): pl.pallas_call(functools.partial(halo_kernel, dom, offsets), out_shape=ja...  5.66 us
    unnamed x42, local copies, waits for them, and re-layouts  2.35 us

profile of v8, /device:TPU:4, one launch (start us, length us, event | category | flops | bytes accessed | tf_op | source)
XLA Modules:
  0.0 58.8 jit_solution(18426528350504754007)
XLA Ops:
  1.3 0.0 copy-start.1
  1.3 0.0 copy-start.3
  1.3 0.0 copy-start.5
  1.3 0.0 copy-start.6
  1.3 0.0 copy-start.7
  1.3 0.0 copy-start.8
  1.3 0.0 copy-start.9
  1.3 0.0 copy-start.11
  1.4 0.0 copy-start.12
  1.4 0.0 copy-start.15
  1.4 0.0 copy-start.16
  1.4 0.0 slice-start
  1.4 5.7 %halo.1.tail_ref = bf16[256,192]{1,0:T(8,128)(2,1)} custom-call(bf16[192,512]{1,0:T(8,128)(2,1)} %bitcast.14, bf16[88,192]{1,0:T(8,128)(2,1)} %if_far.1, s32[4,32]{1,0:T(4,128)} %map_ref.1), custom_call_target="tpu_custom_call" | custom-call | flops 6000000000 | bytes 1000000 | tf_op jit(solution)/shard_map/halo/pallas_call | solution.py:306
  7.1 0.0 copy-done.1
  7.1 0.0 copy-done.3
  7.1 0.0 copy-done.5
  7.2 0.9 %copy-done.17 = bf16[256,192]{1,0:T(8,128)(2,1)S(1)} copy-done((bf16[256,192]{1,0:T(8,128)(2,1)S(1)}, bf16[256,192]{1,0:T(8,128)(2,1)}, u32[]{:S(2)}) %copy-start.17) | copy-done | bytes 98328
  8.1 0.0 copy-start.10
  8.1 0.0 copy-start.13
  8.1 0.0 copy-start.14
  8.1 14.7 %elements.1 = (f32[48,2048]{1,0:T(8,128)}, f32[288,256]{1,0:T(8,128)S(1)}) custom-call(s32[1]{0:T(128)S(6)} %copy.25.counts_ref, bf16[192,512]{1,0:T(8,128)(2,1)S(1)} %bitcast.15, bf16[256,192]{1,0:T(8,128)(2,1)S(1)} %copy-done.17, s32[8,2048]{1,0:T(8,128)S(1)} %bitcast.16, f32[1,2048]{1,0:T(1,128)S(1)} %bitcast.17, f32[1,2048]{1,0:T(1,128)S(1)} %bitcast.18, ...), custom_call_target="tpu_custom_call" | custom-call | flops 24999999488 | bytes 4000000 | tf_op jit(solution)/shard_map/elements/pallas_call | solution.py:215
  22.9 34.5 %finish.1 = (f32[192,512]{1,0:T(8,128)S(1)}, f32[22,192]{1,0:T(8,128)S(1)}) custom-call(f32[288,256]{1,0:T(8,128)S(1)} %get-tuple-element.7.total_ref, bf16[96,192]{1,0:T(8,128)(2,1)S(1)} %copy-done.14, bf16[96,192]{1,0:T(8,128)(2,1)S(1)} %copy-done.13, s32[4,32]{1,0:T(4,128)S(1)} %copy-done.10, f32[192,512]{1,0:T(8,128)S(1)} %bitcast.13, ...), custom_call_target="tpu_custom_call" | custom-call | flops 20000000000 | bytes 9000000 | tf_op jit(solution)/shard_map/finish/pallas_call | solution.py:529
  57.4 0.7 %copy.26 = f32[512,192]{0,1:T(8,128)} copy(f32[512,192]{0,1:T(8,128)S(1)} %bitcast.9) | data formatting | bytes 786432
  58.2 0.6 %copy.27 = f32[22,192]{1,0:T(8,128)} copy(f32[22,192]{1,0:T(8,128)S(1)} %get-tuple-element.15) | data formatting | bytes 33792
  (22 shorter events, 0.0 us)
Async XLA Ops:
  1.3 5.8 %copy-start.1 = (f32[48,2048]{1,0:T(8,128)S(1)}, f32[48,2048]{1,0:T(8,128)}, u32[]{:S(2)}) copy-start(f32[48,2048]{1,0:T(8,128)} %stress_ref.1) | copy-start | bytes 1179652
  1.3 5.8 %copy-start.3 = (bf16[512,192]{0,1:T(8,128)(2,1)S(1)}, bf16[512,192]{0,1:T(8,128)(2,1)}, u32[]{:S(2)}) copy-start(bf16[512,192]{0,1:T(8,128)(2,1)} %param.20) | copy-start | bytes 589828
  1.3 5.8 %copy-start.5 = (s32[2048,8]{0,1:T(8,128)S(1)}, s32[2048,8]{0,1:T(8,128)}, u32[]{:S(2)}) copy-start(s32[2048,8]{0,1:T(8,128)} %param.24) | copy-start | bytes 196612
  1.3 5.8 %copy-start.6 = (f32[2048]{0:T(1024)S(1)}, f32[2048]{0:T(1024)}, u32[]{:S(2)}) copy-start(f32[2048]{0:T(1024)} %param.27) | copy-start | bytes 24580
  1.3 5.8 %copy-start.7 = (f32[2048]{0:T(1024)S(1)}, f32[2048]{0:T(1024)}, u32[]{:S(2)}) copy-start(f32[2048]{0:T(1024)} %param.28) | copy-start | bytes 24580
  1.3 5.8 %copy-start.8 = (f32[2048]{0:T(1024)S(1)}, f32[2048]{0:T(1024)}, u32[]{:S(2)}) copy-start(f32[2048]{0:T(1024)} %param.29) | copy-start | bytes 24580
  1.3 5.8 %copy-start.9 = (f32[2048]{0:T(1024)S(1)}, f32[2048]{0:T(1024)}, u32[]{:S(2)}) copy-start(f32[2048]{0:T(1024)} %param.30) | copy-start | bytes 24580
  1.3 5.8 %copy-start.11 = (bf16[384,384]{1,0:T(8,128)(2,1)S(1)}, bf16[384,384]{1,0:T(8,128)(2,1)}, u32[]{:S(2)}) copy-start(bf16[384,384]{1,0:T(8,128)(2,1)} %constant.14.clone.strain_ref) | copy-start | bytes 884740
  1.4 5.8 %copy-start.12 = (bf16[192,384]{1,0:T(8,128)(2,1)S(1)}, bf16[192,384]{1,0:T(8,128)(2,1)}, u32[]{:S(2)}) copy-start(bf16[192,384]{1,0:T(8,128)(2,1)} %constant.15.clone.force_ref) | copy-start | bytes 442372
  1.4 5.8 %copy-start.15 = (bf16[96,192]{1,0:T(8,128)(2,1)S(1)}, bf16[96,192]{1,0:T(8,128)(2,1)}, u32[]{:S(2)}) copy-start(bf16[96,192]{1,0:T(8,128)(2,1)} %constant.13.clone.synth_lo_ref) | copy-start | bytes 110596
  1.4 5.8 %copy-start.16 = (bf16[96,192]{1,0:T(8,128)(2,1)S(1)}, bf16[96,192]{1,0:T(8,128)(2,1)}, u32[]{:S(2)}) copy-start(bf16[96,192]{1,0:T(8,128)(2,1)} %constant.12.clone.synth_hi_ref) | copy-start | bytes 110596
  1.4 21.5 %slice-start = ((s8[4718592]{0:T(1024)(128)(4,1)}), s8[524288]{0:T(1024)(128)(4,1)S(1)}, s32[]{:S(2)}) async-start(s8[4718592]{0:T(1024)(128)(4,1)} %bitcast.10), calls=%async_computation | async-start | bytes 1048576
  7.2 0.9 %copy-start.17 = (bf16[256,192]{1,0:T(8,128)(2,1)S(1)}, bf16[256,192]{1,0:T(8,128)(2,1)}, u32[]{:S(2)}) copy-start(bf16[256,192]{1,0:T(8,128)(2,1)} %halo.1.tail_ref) | copy-start | bytes 294916
  8.1 14.8 %slice-start.1 = ((s8[4718592]{0:T(1024)(128)(4,1)}), s8[4194304]{0:T(1024)(128)(4,1)S(1)}, s32[]{:S(2)}) async-start(s8[4718592]{0:T(1024)(128)(4,1)} %bitcast.10), calls=%async_computation.1 | async-start | bytes 8388608
  8.1 14.8 %copy-start = (bf16[4224,264]{0,1:T(8,128)(2,1)S(1)}, bf16[4224,264]{0,1:T(8,128)(2,1)}, u32[]{:S(2)}) copy-start(bf16[4224,264]{0,1:T(8,128)(2,1)} %param.33) | copy-start | bytes 6690820
  8.1 14.8 %copy-start.2 = (f32[512,192]{0,1:T(8,128)S(1)}, f32[512,192]{0,1:T(8,128)}, u32[]{:S(2)}) copy-start(f32[512,192]{0,1:T(8,128)} %param.22) | copy-start | bytes 1179652
  8.1 14.8 %copy-start.4 = (f32[88,192]{1,0:T(8,128)S(1)}, f32[88,192]{1,0:T(8,128)}, u32[]{:S(2)}) copy-start(f32[88,192]{1,0:T(8,128)} %load_if_ref.1) | copy-start | bytes 202756
  8.1 14.8 %copy-start.10 = (s32[4,32]{1,0:T(4,128)S(1)}, s32[4,32]{1,0:T(4,128)}, u32[]{:S(2)}) copy-start(s32[4,32]{1,0:T(4,128)} %map_ref.1) | copy-start | bytes 1540
  8.1 14.8 %copy-start.13 = (bf16[96,192]{1,0:T(8,128)(2,1)S(1)}, bf16[96,192]{1,0:T(8,128)(2,1)}, u32[]{:S(2)}) copy-start(bf16[96,192]{1,0:T(8,128)(2,1)} %constant.17.clone.an_lo_ref) | copy-start | bytes 110596
  8.1 14.8 %copy-start.14 = (bf16[96,192]{1,0:T(8,128)(2,1)S(1)}, bf16[96,192]{1,0:T(8,128)(2,1)}, u32[]{:S(2)}) copy-start(bf16[96,192]{1,0:T(8,128)(2,1)} %constant.16.clone.an_hi_ref) | copy-start | bytes 110596
